TPU v7x, 32 devices: a whole 2x2x4 slice. The times are simulated.
32 devices in a mesh: blk: 16 (over z, x, core), tgt: 2 (over y).
Axes of the slice: x: 2, y: 2, z: 4, core: 2. Of those that a mesh axis runs over, the one named last changes fastest.
Arguments:
- gradients: bfloat16 [8192, 8192], P('blk', 'tgt'), may hold values from -6 to 6
- targets: bfloat16 [8192, 64], P('blk'), may hold values from -0.15625 to 0.15625
Outputs:
- kernel_tiles: bfloat16 [3, 8192, 512], P(None, ('blk', 'tgt'))
- influence: float32 [8192, 64], P(('blk', 'tgt'))
All inputs are finite; a program needn't handle non-finite values.
Results may differ from a plain program's by a relative error of at most 0.0029.
Values may be sent and summed in bfloat16 or wider, within the bound.
No kernel may reach another device: no remote copies, remote signals or barrier semaphores. Data moves between devices by JAX's collectives and lax.ppermute only.
A program may use at most 64 MiB of HBM per device.

v0:
```python
import jax
import jax.numpy as jnp
from jax import lax
from jax.sharding import PartitionSpec as P

P_SIZE = 8192
ROUNDS = 2


def from_partner(block, axis, stride):
    count = lax.axis_size(axis)
    route = []
    for low in range(count):
        high = low | 1 << stride
        if high != low and high < count:
            route += [(low, high), (high, low)]
    return lax.ppermute(block, axis, route)


def contract(left, right):
    return lax.dot_general(
        left, right, (((1,), (1,)), ((), ())), preferred_element_type=jnp.float32
    )


def per_device(gradients, targets):
    scale = 1.0 / P_SIZE**0.5
    levels = list(range(ROUNDS))
    levels = levels[::-1]
    tile_map = {}
    self_summed = lax.psum_scatter(
        contract(gradients, gradients), "tgt", scatter_dimension=0, tiled=True
    )
    self_tile = (self_summed * scale).astype(jnp.bfloat16)
    influence = jnp.dot(self_tile, targets, preferred_element_type=jnp.float32)
    for level in levels:
        opponent_grads, opponent_targets = from_partner((gradients, targets), "blk", level)
        partial_value = contract(gradients, opponent_grads)
        summed = lax.psum_scatter(partial_value, "tgt", scatter_dimension=0, tiled=True)
        tile = (summed * scale).astype(jnp.bfloat16)
        tile_map[level] = tile
        influence = influence + jnp.dot(tile, opponent_targets, preferred_element_type=jnp.float32)
    kernel_tiles = jnp.stack([self_tile] + [tile_map[level] for level in range(ROUNDS)], 0)
    return (kernel_tiles, influence)


def solution(mesh):
    placed = (P("blk", "tgt"), P("blk", None))
    return jax.shard_map(
        per_device,
        mesh=mesh,
        in_specs=placed,
        out_specs=(P(None, ("blk", "tgt"), None), P(("blk", "tgt"), None)),
        check_vma=False,
    )
```

profile of v0, /device:TPU:1, one launch (start us, length us, event | category | flops | bytes accessed | tf_op | source)
XLA Modules:
  0.0 140.6 jit_solution(8935334531736470765)
XLA Ops:
  7.2 0.0 reduce-scatter.4.cloned.1.call-start
  7.2 0.1 collective-permute-start
  7.3 2.7 %collective-permute-start.1 = (bf16[512,4096]{1,0:T(8,128)(2,1)}, bf16[512,4096]{1,0:T(8,128)(2,1)}, u32[]{:S(2)}, u32[]{:S(2)}) collective-permute-start(bf16[512,4096]{1,0:T(8,128)(2,1)} %param.2), channel_id=1, source_target_pairs={{0,4},{4,0},{2,6},{6,2},{8,12},{12,8},{10,14},{14,10},{16,20},{20,... | collective-permute-start | bytes 12582920 | tf_op jit(solution)/shard_map/ppermute | solution.py:17
  10.0 6.8 %fusion.7 = f32[512,512]{1,0:T(8,128)} fusion(bf16[512,4096]{1,0:T(8,128)(2,1)} %param.2), kind=kOutput, calls=%fused_computation.13 | convolution fusion | flops 2147483648 | bytes 5242880 | tf_op jit(solution)/shard_map/dot_general | solution.py:21
  16.8 0.0 reduce-scatter.4.cloned.1.call-update
  16.8 0.0 reduce-scatter.6.cloned.1.call-start
  16.9 6.9 %fusion.8 = f32[512,512]{1,0:T(8,128)} fusion(bf16[512,4096]{1,0:T(8,128)(2,1)} %param.2, bf16[512,4096]{1,0:T(8,128)(2,1)} %collective-permute-done), kind=kOutput, calls=%fused_computation.14 | convolution fusion | flops 2147483648 | bytes 9437184 | tf_op jit(solution)/shard_map/dot_general | solution.py:21
  23.8 0.0 reduce-scatter.6.cloned.1.call-update
  23.8 0.0 copy-start.1
  23.8 0.0 reduce-scatter.8.cloned.1.call-start
  23.8 77.3 %collective-permute-done.1 = bf16[512,4096]{1,0:T(8,128)(2,1)} collective-permute-done((bf16[512,4096]{1,0:T(8,128)(2,1)}, bf16[512,4096]{1,0:T(8,128)(2,1)}, u32[]{:S(2)}, u32[]{:S(2)}) %collective-permute-start.1) | collective-permute-done | bytes 4194336 | tf_op jit(solution)/shard_map/ppermute | solution.py:17
  101.2 6.8 %fusion.9 = f32[512,512]{1,0:T(8,128)} fusion(bf16[512,4096]{1,0:T(8,128)(2,1)} %param.2, bf16[512,4096]{1,0:T(8,128)(2,1)} %collective-permute-done.1), kind=kOutput, calls=%fused_computation.15 | convolution fusion | flops 2147483648 | bytes 9437184 | tf_op jit(solution)/shard_map/dot_general | solution.py:21
  108.0 0.0 reduce-scatter.8.cloned.1.call-update
  108.0 1.3 collective-permute-start.2
  109.3 1.1 collective-permute-start.3
  110.5 1.2 fusion
  111.7 1.1 fusion.1
  112.8 0.0 reduce-scatter.6.cloned.1.call-done
  112.9 1.1 fusion.2
  114.0 15.9 %reduce-scatter.8.cloned.1.call-done = f32[256,512]{1,0:T(8,128)} async-done(((f32[512,512]{1,0:T(8,128)}), f32[256,512]{1,0:T(8,128)}) %reduce-scatter.8.cloned.1.call-update) | async-done | bytes 524304 | tf_op jit(solution)/shard_map/reduce_scatter | solution.py:39
  129.9 1.1 fusion.3
  131.0 1.3 convolution_add_fusion.1
  132.3 1.0 pad_maximum_fusion
  133.3 0.8 convolution_add_fusion
  (7 shorter events, 0.0 us)
Async XLA Ops:
  7.2 103.3 %reduce-scatter.4.cloned.1.call-start = ((), (), s32[]{:S(2)}) async-start(), calls=%async_computation.3 | async-start | bytes 1572864 | tf_op jit(solution)/shard_map/reduce_scatter | solution.py:31
  7.2 9.7 %collective-permute-start = (bf16[512,4096]{1,0:T(8,128)(2,1)}, bf16[512,4096]{1,0:T(8,128)(2,1)}, u32[]{:S(2)}, u32[]{:S(2)}) collective-permute-start(bf16[512,4096]{1,0:T(8,128)(2,1)} %param.2), channel_id=1, source_target_pairs={{0,2},{2,0},{4,6},{6,4},{8,10},{10,8},{12,14},{14,12},{16,18},{18,... | collective-permute-start | bytes 12582920 | tf_op jit(solution)/shard_map/ppermute | solution.py:17
  7.3 93.8 %collective-permute-start.1 = (bf16[512,4096]{1,0:T(8,128)(2,1)}, bf16[512,4096]{1,0:T(8,128)(2,1)}, u32[]{:S(2)}, u32[]{:S(2)}) collective-permute-start(bf16[512,4096]{1,0:T(8,128)(2,1)} %param.2), channel_id=1, source_target_pairs={{0,4},{4,0},{2,6},{6,2},{8,12},{12,8},{10,14},{14,10},{16,20},{20,... | collective-permute-start | bytes 12582920 | tf_op jit(solution)/shard_map/ppermute | solution.py:17
  16.8 96.0 %reduce-scatter.6.cloned.1.call-start = ((), (), s32[]{:S(2)}) async-start(), calls=%async_computation.4 | async-start | bytes 1572864 | tf_op jit(solution)/shard_map/reduce_scatter | solution.py:39
  23.8 84.2 %copy-start.1 = (bf16[512,64]{0,1:T(8,128)(2,1)S(1)}, bf16[512,64]{0,1:T(8,128)(2,1)}, u32[]{:S(2)}) copy-start(bf16[512,64]{0,1:T(8,128)(2,1)} %param.3) | copy-start | bytes 196612
  23.8 106.2 %reduce-scatter.8.cloned.1.call-start = ((), (), s32[]{:S(2)}) async-start(), calls=%async_computation.5 | async-start | bytes 1572864 | tf_op jit(solution)/shard_map/reduce_scatter | solution.py:39
  108.0 23.0 %collective-permute-start.2 = (bf16[512,64]{0,1:T(8,128)(2,1)S(1)}, bf16[512,64]{0,1:T(8,128)(2,1)S(1)}, u32[]{:S(2)}, u32[]{:S(2)}) collective-permute-start(bf16[512,64]{0,1:T(8,128)(2,1)S(1)} %copy-done.1), channel_id=1, source_target_pairs={{0,4},{4,0},{2,6},{6,2},{8,12},{12,8},{10,14},{14,10},{16,20},{20,... | collective-permute-start | bytes 196616 | tf_op jit(solution)/shard_map/ppermute | solution.py:17
  109.3 23.9 %collective-permute-start.3 = (bf16[512,64]{0,1:T(8,128)(2,1)S(1)}, bf16[512,64]{0,1:T(8,128)(2,1)S(1)}, u32[]{:S(2)}, u32[]{:S(2)}) collective-permute-start(bf16[512,64]{0,1:T(8,128)(2,1)S(1)} %copy-done.1), channel_id=1, source_target_pairs={{0,2},{2,0},{4,6},{6,4},{8,10},{10,8},{12,14},{14,12},{16,18},{18,... | collective-permute-start | bytes 196616 | tf_op jit(solution)/shard_map/ppermute | solution.py:17
  112.9 20.4 %copy-start = (f32[256,512]{1,0:T(8,128)S(1)}, f32[256,512]{1,0:T(8,128)}, u32[]{:S(2)}) copy-start(f32[256,512]{1,0:T(8,128)} %reduce-scatter.6.cloned.1.call-done) | copy-start | bytes 1572868
Sparse Core Ops, SparseCore 0:
  16.9 20.3 reduce-scatter.3
  39.6 20.3 reduce-scatter.5
  108.1 21.7 reduce-scatter.7
where the time goes:
time: 142 us; the launch traced here: 141 us
  waiting for transfers between devices  93.3 us (66%)
  matrix products  23.8 us (17%)
  between operations  13.8 us (10%)
  starting transfers between devices  5.4 us (4%)
  other arithmetic  4.29 us (3%)
    ppermute x4, waiting for transfers between devices, from_partner(): return lax.ppermute(block, axis, route)  77.3 us
    dot_general x3, matrix products, contract(): lax.dot_general(left, right, (((1,), (1,)), ((), ())), preferred_element_...  20.5 us
    reduce_scatter x2, waiting for transfers between devices, per_device(): lax.psum_scatter(partial_value, 'tgt', scatter_dimension=0, tiled=True)  16 us
    ppermute x4, starting transfers between devices, from_partner(): return lax.ppermute(block, axis, route)  5.28 us
    another operation x4, other arithmetic, per_device(): jnp.stack([self_tile] + [tile_map[level] for level in range(ROUNDS)], 0)  4.29 us
  transfers between devices with their start and end apart: 7, of which 2 were waited for; matrix products, arithmetic and copies ran while one was open for 19% of the time, Pallas kernels for 0%

commit v1 on v0

v1 whole, which is shorter than its diff:
```python
import jax
import jax.numpy as jnp
from jax import lax
from jax.sharding import PartitionSpec as P

AFTER = {0: 1, 1: 3, 3: 2, 2: 0}
BEFORE = {after: before for before, after in AFTER.items()}
PARTS = (64, 64, 64, 32, 32)


def contract(left, right):
    return lax.dot_general(
        left, right, (((1,), (1,)), ((), ())), preferred_element_type=jnp.float32
    )


def per_device(gradients, targets):
    blocks, groups = lax.axis_size("blk"), lax.axis_size("tgt")
    rows, features = gradients.shape
    half = rows // groups
    scale = 1.0 / (features * groups) ** 0.5
    forward = [(b, b - b % 4 + AFTER[b % 4]) for b in range(blocks)]
    back = [(b, b - b % 4 + BEFORE[b % 4]) for b in range(blocks)]
    across = [(t, 1 - t) for t in range(groups)]
    back_across = [(b * groups + t, c * groups + 1 - t) for b, c in back for t in range(groups)]
    me, t = lax.axis_index("blk"), lax.axis_index("tgt")
    other = 1 - t

    halves = gradients.reshape(groups, half, features)
    got, at, source = [], 0, halves
    for width in PARTS:
        piece = source[:, at : at + width].reshape(groups * width, features)
        source, piece = lax.optimization_barrier((source, piece))
        got.append(lax.ppermute(piece, "blk", forward))
        at += width
    targets_before = lax.ppermute(targets, "blk", forward)
    targets_after = lax.ppermute(targets, "blk", back)

    mine = lax.dynamic_slice_in_dim(gradients, t * half, half, 0)
    others = lax.dynamic_slice_in_dim(gradients, other * half, half, 0)

    sent = lax.ppermute(contract(others, gradients), "tgt", across)
    self_tile = ((contract(mine, gradients) + sent) * scale).astype(jnp.bfloat16)
    influence = jnp.dot(self_tile, targets, preferred_element_type=jnp.float32)

    columns, far = [], []
    for width, block in zip(PARTS, got):
        sent = lax.ppermute(contract(block, others), "tgt", across)
        part = ((contract(block, mine) + sent) * scale).astype(jnp.bfloat16)
        part = part.reshape(groups, width, half)
        columns.append(part)
        near = lax.dynamic_index_in_dim(part, t, 0, keepdims=False)
        cross = lax.dynamic_index_in_dim(part, other, 0, keepdims=False)
        near = lax.ppermute(near, "blk", back)
        cross = lax.ppermute(cross, ("blk", "tgt"), back_across)
        far.append(jnp.where(t == 0, jnp.concatenate([near, cross], 1), jnp.concatenate([cross, near], 1)))
    met = jnp.concatenate(columns, 1).reshape(rows, half).T
    back_tile = jnp.concatenate(far, 0)
    influence = influence + jnp.dot(met, targets_before, preferred_element_type=jnp.float32)
    influence = influence + jnp.dot(back_tile, targets_after, preferred_element_type=jnp.float32)

    first = (me % 4 == 1) | (me % 4 == 2)
    tiles = jnp.stack([self_tile, jnp.where(first, met, back_tile), jnp.where(first, back_tile, met)], 0)
    return tiles, influence


def solution(mesh):
    return jax.shard_map(
        per_device,
        mesh=mesh,
        in_specs=(P("blk", "tgt"), P("blk", None)),
        out_specs=(P(None, ("blk", "tgt"), None), P(("blk", "tgt"), None)),
        check_vma=False,
    )
```

time: 142 us -> 110 us (0.77)
  waiting for transfers between devices: 93.3 us -> 39.9 us
  starting transfers between devices: 5.4 us -> 32.3 us
  between operations: 13.8 us -> 0.92 us
  local copies, waits for them, and re-layouts: 0.01 us -> 12.1 us
  other arithmetic: 4.29 us -> 1.87 us
  matrix products: 23.8 us -> 22.1 us
    ppermute x4 -> x23, waiting for transfers between devices: 77.3 us -> 39.9 us  [the longest x5 23.3 us: per_device(): got.append(lax.ppermute(piece, 'blk', forward))]
    ppermute x4 -> x23, starting transfers between devices: 5.28 us -> 32.3 us  [the longest x5 9.7 us: per_device(): near = lax.ppermute(near, 'blk', back)]
    reduce_scatter x3 -> x0, waiting for transfers between devices: 16 us -> none  [the longest x2 16 us: per_device(): lax.psum_scatter(partial_value, 'tgt', scatter_dimension=0, tiled=True)]
    slice x0 -> x5, local copies, waits for them, and re-layouts: none -> 10.6 us  [per_device(): piece = source[:, at:at + width].reshape(groups * width, features)]
    another operation x4 -> x2, other arithmetic: 4.29 us -> 1.01 us  [per_device(): jnp.stack([self_tile, jnp.where(first, met, back_tile), jnp.where(first,...]
    dot_general x3 -> x12, matrix products: 20.5 us -> 20 us  [contract(): lax.dot_general(left, right, (((1,), (1,)), ((), ())), preferred_element_...]
  transfers between devices with their start and end apart: 7 -> 23, of which waited for: 2 -> 9; matrix products, arithmetic and copies ran while one was open for 19% -> 23% of each run, Pallas kernels for 0% -> 0%
where the time goes in v1:
time: 110 us; the launch traced here: 109 us
  waiting for transfers between devices  39.9 us (36%)
  starting transfers between devices  32.3 us (29%)
  matrix products  22.1 us (20%)
  local copies, waits for them, and re-layouts  12.1 us (11%)
  other arithmetic  1.87 us (2%)
    ppermute x5, waiting for transfers between devices, per_device(): got.append(lax.ppermute(piece, 'blk', forward))  23.3 us
    dot_general x12, matrix products, contract(): lax.dot_general(left, right, (((1,), (1,)), ((), ())), preferred_element_...  20 us
    slice x5, local copies, waits for them, and re-layouts, per_device(): piece = source[:, at:at + width].reshape(groups * width, features)  10.6 us
    ppermute x5, waiting for transfers between devices, per_device(): sent = lax.ppermute(contract(block, others), 'tgt', across)  10.4 us
    ppermute x5, starting transfers between devices, per_device(): near = lax.ppermute(near, 'blk', back)  9.7 us
    ppermute x5, starting transfers between devices, per_device(): cross = lax.ppermute(cross, ('blk', 'tgt'), back_across)  8.23 us
    ppermute x1, waiting for transfers between devices, per_device(): sent = lax.ppermute(contract(others, gradients), 'tgt', across)  5.68 us
    ppermute x1, starting transfers between devices, per_device(): targets_after = lax.ppermute(targets, 'blk', back)  4.37 us
  transfers between devices with their start and end apart: 23, of which 9 were waited for; matrix products, arithmetic and copies ran while one was open for 23% of the time, Pallas kernels for 0%

profile of v1, /device:TPU:1, one launch (start us, length us, event | category | flops | bytes accessed | tf_op | source)
XLA Modules:
  0.0 109.2 jit_solution(8993438771685829629)
XLA Ops:
  0.6 2.3 %slice.20 = bf16[2,64,4096]{2,1,0:T(8,128)(2,1)} slice(bf16[2,256,4096]{2,1,0:T(8,128)(2,1)} %bitcast.62), slice={[0:2], [0:64], [0:4096]} | slice | bytes 2097152 | tf_op jit(solution)/shard_map/slice | solution.py:32
  2.9 2.3 %slice.16 = bf16[2,64,4096]{2,1,0:T(8,128)(2,1)} slice(bf16[2,256,4096]{2,1,0:T(8,128)(2,1)} %bitcast.63), slice={[0:2], [64:128], [0:4096]} | slice | bytes 2097152 | tf_op jit(solution)/shard_map/slice | solution.py:32
  5.2 2.3 %slice.17 = bf16[2,64,4096]{2,1,0:T(8,128)(2,1)} slice(bf16[2,256,4096]{2,1,0:T(8,128)(2,1)} %bitcast.64), slice={[0:2], [128:192], [0:4096]} | slice | bytes 2097152 | tf_op jit(solution)/shard_map/slice | solution.py:32
  7.5 1.9 %slice.18 = bf16[2,32,4096]{2,1,0:T(8,128)(2,1)} slice(bf16[2,256,4096]{2,1,0:T(8,128)(2,1)} %bitcast.65), slice={[0:2], [192:224], [0:4096]} | slice | bytes 1048576 | tf_op jit(solution)/shard_map/slice | solution.py:32
  9.4 2.0 %collective-permute-start.7 = (bf16[64,4096]{1,0:T(8,128)(2,1)}, bf16[64,4096]{1,0:T(8,128)(2,1)}, u32[]{:S(2)}, u32[]{:S(2)}) collective-permute-start(bf16[64,4096]{1,0:T(8,128)(2,1)} %bitcast.8), channel_id=1, source_target_pairs={{0,2},{2,6},{4,0},{6,4},{8,10},{10,14},{12,8},{14,12},{16,18},{18,... | collective-permute-start | bytes 1572872 | tf_op jit(solution)/shard_map/ppermute | solution.py:34
  11.4 4.9 %fusion.22 = f32[256,512]{1,0:T(8,128)} fusion(bf16[512,4096]{1,0:T(8,128)(2,1)} %param.2, s32[]{:T(128)S(6)} %select_n.72), kind=kOutput, calls=%fused_computation.28 | convolution fusion | flops 1073741824 | bytes 6815748 | tf_op jit(solution)/shard_map/dot_general | solution.py:12
  19.2 1.9 %slice.19 = bf16[2,32,4096]{2,1,0:T(8,128)(2,1)} slice(bf16[2,256,4096]{2,1,0:T(8,128)(2,1)} %bitcast.66), slice={[0:2], [224:256], [0:4096]} | slice | bytes 1048576 | tf_op jit(solution)/shard_map/slice | solution.py:32
  21.8 2.5 %fusion.14 = f32[64,256]{1,0:T(8,128)S(1)} fusion(bf16[64,4096]{1,0:T(8,128)(2,1)} %collective-permute-done.7, bf16[512,4096]{1,0:T(8,128)(2,1)} %param.2, s32[]{:T(128)S(6)} %select_n.72), kind=kOutput, calls=%fused_computation.20 | convolution fusion | flops 134217728 | bytes 2686980 | tf_op jit(solution)/shard_map/dot_general | solution.py:12
  24.3 5.7 %collective-permute-done = f32[256,512]{1,0:T(8,128)} collective-permute-done((f32[256,512]{1,0:T(8,128)}, f32[256,512]{1,0:T(8,128)}, u32[]{:S(2)}, u32[]{:S(2)}) %collective-permute-start) | collective-permute-done | bytes 524320 | tf_op jit(solution)/shard_map/ppermute | solution.py:42
  30.9 4.2 %fusion.1 = bf16[256,512]{1,0:T(8,128)(2,1)S(1)} fusion(f32[256,512]{1,0:T(8,128)} %collective-permute-done, bf16[512,4096]{1,0:T(8,128)(2,1)} %param.2, s32[]{:T(128)S(6)} %select_n.71), kind=kOutput, calls=%fused_computation.2 | convolution fusion | flops 1074135040 | bytes 7077892 | tf_op jit(solution)/shard_map/dot_general | solution.py:12
  35.1 23.3 %collective-permute-done.9 = bf16[64,4096]{1,0:T(8,128)(2,1)S(1)} collective-permute-done((bf16[64,4096]{1,0:T(8,128)(2,1)}, bf16[64,4096]{1,0:T(8,128)(2,1)S(1)}, u32[]{:S(2)}, u32[]{:S(2)}) %collective-permute-start.9) | collective-permute-done | bytes 524320 | tf_op jit(solution)/shard_map/ppermute | solution.py:34
  59.7 1.9 %collective-permute-done.8 = f32[64,256]{1,0:T(8,128)S(1)} collective-permute-done((f32[64,256]{1,0:T(8,128)S(1)}, f32[64,256]{1,0:T(8,128)S(1)}, u32[]{:S(2)}, u32[]{:S(2)}) %collective-permute-start.8) | collective-permute-done | bytes 65568 | tf_op jit(solution)/shard_map/ppermute | solution.py:48
  61.8 1.8 %fusion.10 = bf16[64,256]{1,0:T(8,128)(2,1)S(1)} fusion(f32[64,256]{1,0:T(8,128)S(1)} %collective-permute-done.8, bf16[64,4096]{1,0:T(8,128)(2,1)} %collective-permute-done.7, bf16[512,4096]{1,0:T(8,128)(2,1)S(1)} %copy-done, s32[]{:T(128)S(6)} %select_n.71), kind=kOutput, calls=%fused_computation.16 | convolution fusion | flops 134266880 | bytes 2719748 | tf_op jit(solution)/shard_map/dot_general | solution.py:12
  64.8 4.4 %collective-permute-start.22 = (bf16[512,64]{0,1:T(8,128)(2,1)S(1)}, bf16[512,64]{0,1:T(8,128)(2,1)}, u32[]{:S(2)}, u32[]{:S(2)}) collective-permute-start(bf16[512,64]{0,1:T(8,128)(2,1)S(1)} %copy-done.1), channel_id=1, source_target_pairs={{0,4},{2,0},{4,6},{6,2},{8,12},{10,8},{12,14},{14,10},{16,20},{18,... | collective-permute-start | bytes 196616 | tf_op jit(solution)/shard_map/ppermute | solution.py:37
  74.7 3.4 %collective-permute-done.2 = f32[128,256]{1,0:T(8,128)S(1)} collective-permute-done((f32[128,256]{1,0:T(8,128)S(1)}, f32[128,256]{1,0:T(8,128)S(1)}, u32[]{:S(2)}, u32[]{:S(2)}) %collective-permute-start.2) | collective-permute-done | bytes 131104 | tf_op jit(solution)/shard_map/ppermute | solution.py:48
  80.0 2.5 %collective-permute-done.4 = f32[128,256]{1,0:T(8,128)S(1)} collective-permute-done((f32[128,256]{1,0:T(8,128)S(1)}, f32[128,256]{1,0:T(8,128)S(1)}, u32[]{:S(2)}, u32[]{:S(2)}) %collective-permute-start.4) | collective-permute-done | bytes 131104 | tf_op jit(solution)/shard_map/ppermute | solution.py:48
  84.3 2.0 %collective-permute-done.6 = f32[128,256]{1,0:T(8,128)S(1)} collective-permute-done((f32[128,256]{1,0:T(8,128)S(1)}, f32[128,256]{1,0:T(8,128)S(1)}, u32[]{:S(2)}, u32[]{:S(2)}) %collective-permute-start.6) | collective-permute-done | bytes 131104 | tf_op jit(solution)/shard_map/ppermute | solution.py:48
  86.3 3.5 %collective-permute-start.12 = (bf16[64,256]{1,0:T(8,128)(2,1)S(1)}, bf16[64,256]{1,0:T(8,128)(2,1)S(1)}, u32[]{:S(2)}, u32[]{:S(2)}) collective-permute-start(bf16[64,256]{1,0:T(8,128)(2,1)S(1)} %get-tuple-element.27), channel_id=1, source_target_pairs={{0,5},{1,4},{2,1},{3,0},{4,7},{5,6},{6,3},{7,2},{8,13},{9,12},{10,... | collective-permute-start | bytes 98312 | tf_op jit(solution)/shard_map/ppermute | solution.py:55
  93.5 2.4 %collective-permute-start.13 = (bf16[64,256]{1,0:T(8,128)(2,1)S(1)}, bf16[64,256]{1,0:T(8,128)(2,1)S(1)}, u32[]{:S(2)}, u32[]{:S(2)}) collective-permute-start(bf16[64,256]{1,0:T(8,128)(2,1)S(1)} %get-tuple-element.24), channel_id=1, source_target_pairs={{0,4},{2,0},{4,6},{6,2},{8,12},{10,8},{12,14},{14,10},{16,20},{18,... | collective-permute-start | bytes 98312 | tf_op jit(solution)/shard_map/ppermute | solution.py:54
  96.1 1.7 %collective-permute-start.16 = (bf16[64,256]{1,0:T(8,128)(2,1)S(1)}, bf16[64,256]{1,0:T(8,128)(2,1)S(1)}, u32[]{:S(2)}, u32[]{:S(2)}) collective-permute-start(bf16[64,256]{1,0:T(8,128)(2,1)S(1)} %get-tuple-element.23), channel_id=1, source_target_pairs={{0,5},{1,4},{2,1},{3,0},{4,7},{5,6},{6,3},{7,2},{8,13},{9,12},{10,... | collective-permute-start | bytes 98312 | tf_op jit(solution)/shard_map/ppermute | solution.py:55
  97.8 3.0 %collective-permute-start.15 = (bf16[64,256]{1,0:T(8,128)(2,1)S(1)}, bf16[64,256]{1,0:T(8,128)(2,1)S(1)}, u32[]{:S(2)}, u32[]{:S(2)}) collective-permute-start(bf16[64,256]{1,0:T(8,128)(2,1)S(1)} %get-tuple-element.22), channel_id=1, source_target_pairs={{0,4},{2,0},{4,6},{6,2},{8,12},{10,8},{12,14},{14,10},{16,20},{18,... | collective-permute-start | bytes 98312 | tf_op jit(solution)/shard_map/ppermute | solution.py:54
  100.8 1.8 %collective-permute-start.20 = (bf16[32,256]{1,0:T(8,128)(2,1)S(1)}, bf16[32,256]{1,0:T(8,128)(2,1)S(1)}, u32[]{:S(2)}, u32[]{:S(2)}) collective-permute-start(bf16[32,256]{1,0:T(8,128)(2,1)S(1)} %copy-done.3), channel_id=1, source_target_pairs={{0,5},{1,4},{2,1},{3,0},{4,7},{5,6},{6,3},{7,2},{8,13},{9,12},{10,... | collective-permute-start | bytes 49160 | tf_op jit(solution)/shard_map/ppermute | solution.py:55
  102.6 3.0 %collective-permute-start.19 = (bf16[32,256]{1,0:T(8,128)(2,1)S(1)}, bf16[32,256]{1,0:T(8,128)(2,1)S(1)}, u32[]{:S(2)}, u32[]{:S(2)}) collective-permute-start(bf16[32,256]{1,0:T(8,128)(2,1)S(1)} %copy-done.2), channel_id=1, source_target_pairs={{0,4},{2,0},{4,6},{6,2},{8,12},{10,8},{12,14},{14,10},{16,20},{18,... | collective-permute-start | bytes 49160 | tf_op jit(solution)/shard_map/ppermute | solution.py:54
  107.5 1.7 %add_add_fusion = f32[256,64]{0,1:T(8,128)} fusion(f32[256,64]{0,1:T(8,128)S(1)} %fusion.49, f32[256,64]{0,1:T(8,128)S(1)} %fusion.50, bf16[256,512]{1,0:T(8,128)(2,1)S(1)} %fusion.36, bf16[512,64]{0,1:T(8,128)(2,1)} %collective-permute-done.22), kind=kOutput, calls=%fused_computation.47 | convolution fusion | flops 16809984 | bytes 524288 | tf_op jit(solution)/shard_map/dot_general | solution.py:60
  (68 shorter events, 21.9 us)
Async XLA Ops:
  9.4 11.6 %collective-permute-start.7 = (bf16[64,4096]{1,0:T(8,128)(2,1)}, bf16[64,4096]{1,0:T(8,128)(2,1)}, u32[]{:S(2)}, u32[]{:S(2)}) collective-permute-start(bf16[64,4096]{1,0:T(8,128)(2,1)} %bitcast.8), channel_id=1, source_target_pairs={{0,2},{2,6},{4,0},{6,4},{8,10},{10,14},{12,8},{14,12},{16,18},{18,... | collective-permute-start | bytes 1572872 | tf_op jit(solution)/shard_map/ppermute | solution.py:34
  16.4 13.6 %collective-permute-start = (f32[256,512]{1,0:T(8,128)}, f32[256,512]{1,0:T(8,128)}, u32[]{:S(2)}, u32[]{:S(2)}) collective-permute-start(f32[256,512]{1,0:T(8,128)} %fusion.22), channel_id=1, source_target_pairs={{0,1},{1,0},{2,3},{3,2},{4,5},{5,4},{6,7},{7,6},{8,9},{9,8},{10,11... | collective-permute-start | bytes 1572872 | tf_op jit(solution)/shard_map/ppermute | solution.py:42
  17.6 52.9 %collective-permute-start.1 = (bf16[128,4096]{1,0:T(8,128)(2,1)}, bf16[128,4096]{1,0:T(8,128)(2,1)S(1)}, u32[]{:S(2)}, u32[]{:S(2)}) collective-permute-start(bf16[128,4096]{1,0:T(8,128)(2,1)} %bitcast.2), channel_id=1, source_target_pairs={{0,2},{2,6},{4,0},{6,4},{8,10},{10,14},{12,8},{14,12},{16,18},{18,... | collective-permute-start | bytes 3145736 | tf_op jit(solution)/shard_map/ppermute | solution.py:34
  18.3 53.5 %collective-permute-start.3 = (bf16[128,4096]{1,0:T(8,128)(2,1)}, bf16[128,4096]{1,0:T(8,128)(2,1)S(1)}, u32[]{:S(2)}, u32[]{:S(2)}) collective-permute-start(bf16[128,4096]{1,0:T(8,128)(2,1)} %bitcast.4), channel_id=1, source_target_pairs={{0,2},{2,6},{4,0},{6,4},{8,10},{10,14},{12,8},{14,12},{16,18},{18,... | collective-permute-start | bytes 3145736 | tf_op jit(solution)/shard_map/ppermute | solution.py:34
  19.1 53.6 %collective-permute-start.5 = (bf16[128,4096]{1,0:T(8,128)(2,1)}, bf16[128,4096]{1,0:T(8,128)(2,1)S(1)}, u32[]{:S(2)}, u32[]{:S(2)}) collective-permute-start(bf16[128,4096]{1,0:T(8,128)(2,1)} %bitcast.69), channel_id=1, source_target_pairs={{0,2},{2,6},{4,0},{6,4},{8,10},{10,14},{12,8},{14,12},{16,18},{18,... | collective-permute-start | bytes 3145736 | tf_op jit(solution)/shard_map/ppermute | solution.py:34
  21.0 37.4 %collective-permute-start.9 = (bf16[64,4096]{1,0:T(8,128)(2,1)}, bf16[64,4096]{1,0:T(8,128)(2,1)S(1)}, u32[]{:S(2)}, u32[]{:S(2)}) collective-permute-start(bf16[64,4096]{1,0:T(8,128)(2,1)} %bitcast.77), channel_id=1, source_target_pairs={{0,2},{2,6},{4,0},{6,4},{8,10},{10,14},{12,8},{14,12},{16,18},{18,... | collective-permute-start | bytes 1572872 | tf_op jit(solution)/shard_map/ppermute | solution.py:34
  24.3 34.4 %copy-start = (bf16[512,4096]{1,0:T(8,128)(2,1)S(1)}, bf16[512,4096]{1,0:T(8,128)(2,1)}, u32[]{:S(2)}) copy-start(bf16[512,4096]{1,0:T(8,128)(2,1)} %param.2) | copy-start | bytes 12582916
  30.0 60.8 %collective-permute-start.21 = (bf16[512,64]{0,1:T(8,128)(2,1)S(1)}, bf16[512,64]{0,1:T(8,128)(2,1)S(1)}, u32[]{:S(2)}, u32[]{:S(2)}) collective-permute-start(bf16[512,64]{0,1:T(8,128)(2,1)S(1)} %copy-done.1), channel_id=1, source_target_pairs={{0,2},{2,6},{4,0},{6,4},{8,10},{10,14},{12,8},{14,12},{16,18},{18,... | collective-permute-start | bytes 196616 | tf_op jit(solution)/shard_map/ppermute | solution.py:36
  58.5 3.1 %collective-permute-start.8 = (f32[64,256]{1,0:T(8,128)S(1)}, f32[64,256]{1,0:T(8,128)S(1)}, u32[]{:S(2)}, u32[]{:S(2)}) collective-permute-start(f32[64,256]{1,0:T(8,128)S(1)} %fusion.14), channel_id=1, source_target_pairs={{0,1},{1,0},{2,3},{3,2},{4,5},{5,4},{6,7},{7,6},{8,9},{9,8},{10,11... | collective-permute-start | bytes 196616 | tf_op jit(solution)/shard_map/ppermute | solution.py:48
  61.6 3.2 %collective-permute-start.10 = (f32[64,256]{1,0:T(8,128)S(1)}, f32[64,256]{1,0:T(8,128)S(1)}, u32[]{:S(2)}, u32[]{:S(2)}) collective-permute-start(f32[64,256]{1,0:T(8,128)S(1)} %fusion.12), channel_id=1, source_target_pairs={{0,1},{1,0},{2,3},{3,2},{4,5},{5,4},{6,7},{7,6},{8,9},{9,8},{10,11... | collective-permute-start | bytes 196616 | tf_op jit(solution)/shard_map/ppermute | solution.py:48
  64.8 42.8 %collective-permute-start.22 = (bf16[512,64]{0,1:T(8,128)(2,1)S(1)}, bf16[512,64]{0,1:T(8,128)(2,1)}, u32[]{:S(2)}, u32[]{:S(2)}) collective-permute-start(bf16[512,64]{0,1:T(8,128)(2,1)S(1)} %copy-done.1), channel_id=1, source_target_pairs={{0,4},{2,0},{4,6},{6,2},{8,12},{10,8},{12,14},{14,10},{16,20},{18,... | collective-permute-start | bytes 196616 | tf_op jit(solution)/shard_map/ppermute | solution.py:37
  70.5 35.1 %collective-permute-start.18 = (bf16[32,256]{1,0:T(8,128)(2,1)}, bf16[32,256]{1,0:T(8,128)(2,1)}, u32[]{:S(2)}, u32[]{:S(2)}) collective-permute-start(bf16[32,256]{1,0:T(8,128)(2,1)} %get-tuple-element.31), channel_id=1, source_target_pairs={{0,5},{1,4},{2,1},{3,0},{4,7},{5,6},{6,3},{7,2},{8,13},{9,12},{10,... | collective-permute-start | bytes 49160 | tf_op jit(solution)/shard_map/ppermute | solution.py:55
  71.8 33.8 %collective-permute-start.17 = (bf16[32,256]{1,0:T(8,128)(2,1)S(1)}, bf16[32,256]{1,0:T(8,128)(2,1)}, u32[]{:S(2)}, u32[]{:S(2)}) collective-permute-start(bf16[32,256]{1,0:T(8,128)(2,1)S(1)} %get-tuple-element.30), channel_id=1, source_target_pairs={{0,4},{2,0},{4,6},{6,2},{8,12},{10,8},{12,14},{14,10},{16,20},{18,... | collective-permute-start | bytes 49160 | tf_op jit(solution)/shard_map/ppermute | solution.py:54
  72.7 5.4 %collective-permute-start.2 = (f32[128,256]{1,0:T(8,128)S(1)}, f32[128,256]{1,0:T(8,128)S(1)}, u32[]{:S(2)}, u32[]{:S(2)}) collective-permute-start(f32[128,256]{1,0:T(8,128)S(1)} %fusion.20), channel_id=1, source_target_pairs={{0,1},{1,0},{2,3},{3,2},{4,5},{5,4},{6,7},{7,6},{8,9},{9,8},{10,11... | collective-permute-start | bytes 393224 | tf_op jit(solution)/shard_map/ppermute | solution.py:48
  78.1 4.4 %collective-permute-start.4 = (f32[128,256]{1,0:T(8,128)S(1)}, f32[128,256]{1,0:T(8,128)S(1)}, u32[]{:S(2)}, u32[]{:S(2)}) collective-permute-start(f32[128,256]{1,0:T(8,128)S(1)} %fusion.18), channel_id=1, source_target_pairs={{0,1},{1,0},{2,3},{3,2},{4,5},{5,4},{6,7},{7,6},{8,9},{9,8},{10,11... | collective-permute-start | bytes 393224 | tf_op jit(solution)/shard_map/ppermute | solution.py:48
  82.5 3.8 %collective-permute-start.6 = (f32[128,256]{1,0:T(8,128)S(1)}, f32[128,256]{1,0:T(8,128)S(1)}, u32[]{:S(2)}, u32[]{:S(2)}) collective-permute-start(f32[128,256]{1,0:T(8,128)S(1)} %fusion.16), channel_id=1, source_target_pairs={{0,1},{1,0},{2,3},{3,2},{4,5},{5,4},{6,7},{7,6},{8,9},{9,8},{10,11... | collective-permute-start | bytes 393224 | tf_op jit(solution)/shard_map/ppermute | solution.py:48
  86.3 6.1 %collective-permute-start.12 = (bf16[64,256]{1,0:T(8,128)(2,1)S(1)}, bf16[64,256]{1,0:T(8,128)(2,1)S(1)}, u32[]{:S(2)}, u32[]{:S(2)}) collective-permute-start(bf16[64,256]{1,0:T(8,128)(2,1)S(1)} %get-tuple-element.27), channel_id=1, source_target_pairs={{0,5},{1,4},{2,1},{3,0},{4,7},{5,6},{6,3},{7,2},{8,13},{9,12},{10,... | collective-permute-start | bytes 98312 | tf_op jit(solution)/shard_map/ppermute | solution.py:55
  90.7 2.8 %collective-permute-start.11 = (bf16[64,256]{1,0:T(8,128)(2,1)S(1)}, bf16[64,256]{1,0:T(8,128)(2,1)S(1)}, u32[]{:S(2)}, u32[]{:S(2)}) collective-permute-start(bf16[64,256]{1,0:T(8,128)(2,1)S(1)} %get-tuple-element.26), channel_id=1, source_target_pairs={{0,4},{2,0},{4,6},{6,2},{8,12},{10,8},{12,14},{14,10},{16,20},{18,... | collective-permute-start | bytes 98312 | tf_op jit(solution)/shard_map/ppermute | solution.py:54
  92.4 3.7 %collective-permute-start.14 = (bf16[64,256]{1,0:T(8,128)(2,1)S(1)}, bf16[64,256]{1,0:T(8,128)(2,1)S(1)}, u32[]{:S(2)}, u32[]{:S(2)}) collective-permute-start(bf16[64,256]{1,0:T(8,128)(2,1)S(1)} %get-tuple-element.25), channel_id=1, source_target_pairs={{0,5},{1,4},{2,1},{3,0},{4,7},{5,6},{6,3},{7,2},{8,13},{9,12},{10,... | collective-permute-start | bytes 98312 | tf_op jit(solution)/shard_map/ppermute | solution.py:55
  93.5 4.3 %collective-permute-start.13 = (bf16[64,256]{1,0:T(8,128)(2,1)S(1)}, bf16[64,256]{1,0:T(8,128)(2,1)S(1)}, u32[]{:S(2)}, u32[]{:S(2)}) collective-permute-start(bf16[64,256]{1,0:T(8,128)(2,1)S(1)} %get-tuple-element.24), channel_id=1, source_target_pairs={{0,4},{2,0},{4,6},{6,2},{8,12},{10,8},{12,14},{14,10},{16,20},{18,... | collective-permute-start | bytes 98312 | tf_op jit(solution)/shard_map/ppermute | solution.py:54
  96.1 4.7 %collective-permute-start.16 = (bf16[64,256]{1,0:T(8,128)(2,1)S(1)}, bf16[64,256]{1,0:T(8,128)(2,1)S(1)}, u32[]{:S(2)}, u32[]{:S(2)}) collective-permute-start(bf16[64,256]{1,0:T(8,128)(2,1)S(1)} %get-tuple-element.23), channel_id=1, source_target_pairs={{0,5},{1,4},{2,1},{3,0},{4,7},{5,6},{6,3},{7,2},{8,13},{9,12},{10,... | collective-permute-start | bytes 98312 | tf_op jit(solution)/shard_map/ppermute | solution.py:55
  97.8 4.8 %collective-permute-start.15 = (bf16[64,256]{1,0:T(8,128)(2,1)S(1)}, bf16[64,256]{1,0:T(8,128)(2,1)S(1)}, u32[]{:S(2)}, u32[]{:S(2)}) collective-permute-start(bf16[64,256]{1,0:T(8,128)(2,1)S(1)} %get-tuple-element.22), channel_id=1, source_target_pairs={{0,4},{2,0},{4,6},{6,2},{8,12},{10,8},{12,14},{14,10},{16,20},{18,... | collective-permute-start | bytes 98312 | tf_op jit(solution)/shard_map/ppermute | solution.py:54
  100.8 5.6 %collective-permute-start.20 = (bf16[32,256]{1,0:T(8,128)(2,1)S(1)}, bf16[32,256]{1,0:T(8,128)(2,1)S(1)}, u32[]{:S(2)}, u32[]{:S(2)}) collective-permute-start(bf16[32,256]{1,0:T(8,128)(2,1)S(1)} %copy-done.3), channel_id=1, source_target_pairs={{0,5},{1,4},{2,1},{3,0},{4,7},{5,6},{6,3},{7,2},{8,13},{9,12},{10,... | collective-permute-start | bytes 49160 | tf_op jit(solution)/shard_map/ppermute | solution.py:55
  102.6 3.8 %collective-permute-start.19 = (bf16[32,256]{1,0:T(8,128)(2,1)S(1)}, bf16[32,256]{1,0:T(8,128)(2,1)S(1)}, u32[]{:S(2)}, u32[]{:S(2)}) collective-permute-start(bf16[32,256]{1,0:T(8,128)(2,1)S(1)} %copy-done.2), channel_id=1, source_target_pairs={{0,4},{2,0},{4,6},{6,2},{8,12},{10,8},{12,14},{14,10},{16,20},{18,... | collective-permute-start | bytes 49160 | tf_op jit(solution)/shard_map/ppermute | solution.py:54
  (3 other events, 62.1 us)

commit v2 on v1

v2 whole, which is shorter than its diff:
```python
import functools

import jax
import jax.numpy as jnp
from jax import lax
from jax.experimental import pallas as pl
from jax.experimental.pallas import tpu as pltpu
from jax.sharding import PartitionSpec as P

AFTER = {0: 1, 1: 3, 3: 2, 2: 0}
BEFORE = {after: before for before, after in AFTER.items()}
SIXTEENTHS = (6, 5, 3, 2)

VMEM = pl.BlockSpec(memory_space=pltpu.VMEM)
ANY = pl.BlockSpec(memory_space=pl.ANY)
COST = pl.CostEstimate(flops=0, bytes_accessed=0, transcendentals=0)


def call(kernel, out, in_specs, out_specs, scratch=(), aliases=None, vmem=16):
    return pl.pallas_call(
        kernel,
        out_shape=out,
        in_specs=in_specs,
        out_specs=out_specs,
        scratch_shapes=scratch,
        input_output_aliases=aliases or {},
        cost_estimate=COST,
        compiler_params=pltpu.CompilerParams(vmem_limit_bytes=vmem * 2**20),
    )


def contract(left, right):
    return lax.dot_general(
        left, right, (((1,), (1,)), ((), ())), preferred_element_type=jnp.float32
    )


def multiply(left, right):
    return jnp.dot(left, right, preferred_element_type=jnp.float32)


def part_of(index, size):
    return pl.ds(pl.multiple_of(index * size, size), size)


def run_copies(copies, sems):
    copies = [pltpu.make_async_copy(*ends, sems.at[i]) for i, ends in enumerate(copies)]
    for copy in copies:
        copy.start()
    for copy in copies:
        copy.wait()


def first_kernel(width, half, grads, flat, out, sems):
    wide = out.shape[1]
    copies = [
        (
            grads.at[pl.ds(h * half, width), pl.ds(k * wide, wide)],
            out.at[pl.ds((2 * k + h) * width, width)],
        )
        for k in range(2)
        for h in range(2)
    ]
    long = flat.shape[1]
    for j in range(flat.shape[0] // 16):
        down, along = divmod(j, wide // long)
        copies.append(
            (
                flat.at[pl.ds(16 * j, 16)],
                out.at[pl.ds(4 * width + 16 * down, 16), pl.ds(along * long, long)],
            )
        )
    run_copies(copies, sems)


def rest_kernel(spans, half, grads, before, *refs):
    del before
    *outs, sems = refs
    run_copies(
        [
            (grads.at[pl.ds(h * half + at, width)], out.at[pl.ds(h * width, width)])
            for (at, width), out in zip(spans, outs)
            for h in range(2)
        ],
        sems,
    )


def self_kernel(half, grads, before, sent, kept):
    del before
    t = lax.axis_index("tgt")
    sent[...] = contract(grads[part_of(1 - t, half), :], grads[...])
    kept[...] = contract(grads[part_of(t, half), :], grads[...])


def self_finish_kernel(scale, kept, got, tile):
    tile[...] = ((kept[...] + got[...]) * scale).astype(jnp.bfloat16)


def share(sent, kept, width):
    t = lax.axis_index("tgt")
    sent[2 * width :, :] = kept[part_of(1 - t, width), :]
    kept[2 * width :, :] = sent[part_of(t, width), :]


def first_pair_kernel(width, half, columns, piece, grads, sent, kept, flat):
    wide = piece.shape[1]
    t = lax.axis_index("tgt")
    for to, index in ((sent, 1 - t), (kept, t)):
        rows = part_of(index, half)
        to[: 2 * width, :] = contract(piece[: 2 * width, :], grads[rows, :wide]) + contract(
            piece[2 * width : 4 * width, :], grads[rows, wide:]
        )
    share(sent, kept, width)
    long = flat.shape[1]
    for j in range(columns // 16):
        down, along = divmod(j, wide // long)
        flat[16 * j : 16 * j + 16, :] = piece[
            4 * width + 16 * down : 4 * width + 16 * down + 16, along * long : (along + 1) * long
        ]


def pair_kernel(width, half, piece, grads, before, sent, kept):
    del before
    t = lax.axis_index("tgt")
    sent[: 2 * width, :] = contract(piece[...], grads[part_of(1 - t, half), :])
    kept[: 2 * width, :] = contract(piece[...], grads[part_of(t, half), :])
    share(sent, kept, width)


def last_pair_kernel(width, half, piece, grads, sent, kept, near, cross):
    t = lax.axis_index("tgt")
    sent[...] = contract(piece[...], grads[part_of(1 - t, half), :])
    kept[...] = contract(piece[...], grads[part_of(t, half), :])
    for to, index in ((near, t), (cross, 1 - t)):
        to[:, part_of(t, half)] = kept[part_of(index, width), :]
        to[:, part_of(1 - t, half)] = sent[part_of(index, width), :]


def finish_kernel(widths, half, scale, *refs):
    ins, (flat, before, met, back) = refs[: 2 * len(widths)], refs[2 * len(widths) :]
    del before
    t = lax.axis_index("tgt")
    at = 0
    for i, width in enumerate(widths):
        kept, got = ins[2 * i : 2 * i + 2]
        value = ((kept[...] + got[...]) * scale).astype(jnp.bfloat16)
        for h in range(2):
            met[h * half + at : h * half + at + width, :] = value[h * width : (h + 1) * width]
        back[at : at + width, part_of(1 - t, half)] = value[2 * width :]
        at += width
    back[:at, part_of(t, half)] = met[pl.ds(pl.multiple_of(t * half, half), at), :]
    back[at:, :] = flat[...]
    for h in range(2):
        met[h * half + at : (h + 1) * half, :] = jnp.zeros((half - at, half), jnp.bfloat16)


def own_slot():
    place = lax.rem(lax.axis_index("blk"), 4)
    return jnp.where((place == 1) | (place == 2), 1, 2)


def most_kernel(half, edge, self_tile, met, flat, flat_before, tiles, partial, turned, sems):
    slot = own_slot()
    whole = pltpu.make_async_copy(self_tile, tiles.at[0], sems.at[0])
    whole.start()
    value = contract(flat[...], self_tile[...])
    copies = []
    for h in range(2):
        rows = slice(h * half, h * half + edge)
        turned[h] = met[rows, :].T
        copies.append(
            pltpu.make_async_copy(
                turned.at[h], tiles.at[slot, :, pl.ds(h * half, edge)], sems.at[1 + h]
            )
        )
        copies[h].start()
        value += multiply(flat_before[:, rows], met[rows, :])
    partial[...] = value
    whole.wait()
    for copy in copies:
        copy.wait()


def last_kernel(
    half, edge, scale, before, partial, met, back, flat_before, kept, got, near, cross,
    tiles, influence, turned, far, late, total, sems,
):
    del before
    slot = own_slot()
    rows, width = far.shape[0], near.shape[0]
    done = rows - width
    copies = [
        pltpu.make_async_copy(
            back.at[pl.ds(0, done)], tiles.at[3 - slot, pl.ds(0, done)], sems.at[0]
        )
    ]
    copies[0].start()
    far[done:, :] = ((near[...] + cross[...]) * scale).astype(jnp.bfloat16)
    copies.append(
        pltpu.make_async_copy(
            far.at[pl.ds(done, width)], tiles.at[3 - slot, pl.ds(done, width)], sems.at[1]
        )
    )
    copies[1].start()
    new = ((kept[...] + got[...]) * scale).astype(jnp.bfloat16)
    value = partial[...]
    for h in range(2):
        stop = (h + 1) * half
        late[h, : done - edge, :] = met[h * half + edge : h * half + done, :]
        late[h, done - edge :, :] = new[h * width : (h + 1) * width]
        turned[h] = late[h].T
        copies.append(
            pltpu.make_async_copy(
                turned.at[h], tiles.at[slot, :, pl.ds(h * half + edge, half - edge)], sems.at[2 + h]
            )
        )
        copies[-1].start()
        value += multiply(flat_before[:, h * half + edge : stop], late[h])
    far[:done, :] = back[:done, :]
    total[...] = value + contract(back[done:, :], far[...])
    copies.append(pltpu.make_async_copy(total, influence, sems.at[4]))
    copies[-1].start()
    for copy in copies:
        copy.wait()


def per_device(gradients, targets):
    blocks, groups = lax.axis_size("blk"), lax.axis_size("tgt")
    rows, features = gradients.shape
    columns = targets.shape[1]
    half = rows // groups
    scale = 1.0 / (features * groups) ** 0.5
    forward = [(b, b - b % 4 + AFTER[b % 4]) for b in range(blocks)]
    back = [(b, b - b % 4 + BEFORE[b % 4]) for b in range(blocks)]
    across = [(t, 1 - t) for t in range(groups)]
    back_across = [(b * groups + t, c * groups + 1 - t) for b, c in back for t in range(groups)]

    def f32(*shape):
        return jax.ShapeDtypeStruct(shape, jnp.float32)

    def b16(*shape):
        return jax.ShapeDtypeStruct(shape, jnp.bfloat16)

    widths = [half * n // 16 for n in SIXTEENTHS]
    spans = [(sum(widths[:i]), w) for i, w in enumerate(widths)]
    done = spans[-1][0]
    edge = half // 2
    flat = targets.T

    wide = features // 2
    below = 16 * -(-(columns // 16) // (wide // rows))
    piece = call(
        functools.partial(first_kernel, widths[0], half),
        b16(4 * widths[0] + below, wide),
        [ANY] * 2,
        ANY,
        [pltpu.SemaphoreType.DMA((4 + columns // 16,))],
    )(gradients, flat)
    sent, kept = call(
        functools.partial(self_kernel, half), [f32(half, rows)] * 2, [VMEM, ANY], [VMEM] * 2
    )(gradients, piece)
    pieces = call(
        functools.partial(rest_kernel, spans[1:], half),
        [b16(2 * w, features) for w in widths[1:]],
        [ANY] * 2,
        [ANY] * 3,
        [pltpu.SemaphoreType.DMA((6,))],
    )(gradients, kept)
    got = [lax.ppermute(piece, "blk", forward) for piece in (piece, *pieces)]
    self_tile = call(
        functools.partial(self_finish_kernel, scale), b16(half, rows), [VMEM] * 2, VMEM
    )(kept, lax.ppermute(sent, "tgt", across))

    sums = []
    sent, kept, flat_before = call(
        functools.partial(first_pair_kernel, widths[0], half, columns),
        [f32(3 * widths[0], half)] * 2 + [b16(columns, rows)],
        [VMEM] * 2,
        [VMEM] * 3,
    )(got[0], gradients)
    sums += [kept, lax.ppermute(sent, "tgt", across)]
    after = self_tile
    for width, piece in zip(widths[1:3], got[1:3]):
        sent, kept = call(
            functools.partial(pair_kernel, width, half),
            [f32(3 * width, half)] * 2,
            [VMEM] * 2 + [ANY],
            [VMEM] * 2,
        )(piece, gradients, after)
        sums += [kept, lax.ppermute(sent, "tgt", across)]
        after = kept
    width = widths[3]
    sent, kept, near, cross = call(
        functools.partial(last_pair_kernel, width, half),
        [f32(2 * width, half)] * 2 + [f32(width, rows)] * 2,
        [VMEM] * 2,
        [VMEM] * 4,
    )(got[3], gradients)
    last = [
        kept,
        lax.ppermute(sent, "tgt", across),
        lax.ppermute(near, "blk", back),
        lax.ppermute(cross, ("blk", "tgt"), back_across),
    ]
    met, returned = call(
        functools.partial(finish_kernel, widths[:3], half, scale),
        [b16(rows, half), b16(done + columns, rows)],
        [VMEM] * 7 + [ANY],
        [VMEM] * 2,
    )(*sums, flat, kept)
    returned = lax.ppermute(returned, "blk", back)

    tiles, partial = call(
        functools.partial(most_kernel, half, edge),
        [b16(3, half, rows), f32(columns, half)],
        [VMEM] * 4,
        [ANY, VMEM],
        [pltpu.VMEM((2, half, edge), jnp.bfloat16), pltpu.SemaphoreType.DMA((3,))],
    )(self_tile, met, flat, flat_before)
    tiles, influence = call(
        functools.partial(last_kernel, half, edge, scale),
        [b16(3, half, rows), f32(columns, half)],
        [ANY] + [VMEM] * 8,
        [ANY] * 2,
        [
            pltpu.VMEM((2, half, half - edge), jnp.bfloat16),
            pltpu.VMEM((half, rows), jnp.bfloat16),
            pltpu.VMEM((2, half - edge, half), jnp.bfloat16),
            pltpu.VMEM((columns, half), jnp.float32),
            pltpu.SemaphoreType.DMA((5,)),
        ],
        {0: 0},
    )(tiles, partial, met, returned, flat_before, *last)
    return tiles, influence.T


def solution(mesh):
    return jax.shard_map(
        per_device,
        mesh=mesh,
        in_specs=(P("blk", "tgt"), P("blk", None)),
        out_specs=(P(None, ("blk", "tgt"), None), P(("blk", "tgt"), None)),
        check_vma=False,
    )
```

time: 110 us -> 64.1 us (0.58)
  matrix products: 22.1 us -> 0 us
  starting transfers between devices: 32.3 us -> 13.2 us
  Pallas kernels: 0 us -> 11.3 us
  local copies, waits for them, and re-layouts: 12.1 us -> 3.03 us
  waiting for transfers between devices: 39.9 us -> 35.3 us
  other arithmetic: 1.87 us -> 0 us
    dot_general x15 -> x0, matrix products: 22.1 us -> none  [the longest x12 20 us: contract(): lax.dot_general(left, right, (((1,), (1,)), ((), ())), preferred_element_...]
    ppermute x23 -> x12, starting transfers between devices: 32.3 us -> 13.2 us  [the longest x3 3.91 us: per_device(): sums += [kept, lax.ppermute(sent, 'tgt', across)]]
    pallas_call x0 -> x11, Pallas kernels: none -> 11.3 us  [the longest x2 3 us: per_device(): call(functools.partial(pair_kernel, width, half), [f32(3 * width, half)]...]
    slice x5 -> x0, local copies, waits for them, and re-layouts: 10.6 us -> none  [per_device(): piece = source[:, at:at + width].reshape(groups * width, features)]
    ppermute x23 -> x12, waiting for transfers between devices: 39.9 us -> 35.3 us  [the longest x4 31.8 us: per_device(): got = [lax.ppermute(piece, 'blk', forward) for piece in (piece, *pieces)]]
    unnamed x12 -> x8, local copies, waits for them, and re-layouts: 0.04 us -> 3.03 us
    squeeze x5 -> x0, local copies, waits for them, and re-layouts: 1.27 us -> none  [per_device(): near = lax.dynamic_index_in_dim(part, t, 0, keepdims=False)]
  transfers between devices with their start and end apart: 23 -> 12, of which waited for: 9 -> 6; matrix products, arithmetic and copies ran while one was open for 23% -> 0% of each run, Pallas kernels for 0% -> 16%
where the time goes in v2:
time: 64.1 us; the launch traced here: 63.6 us
  waiting for transfers between devices  35.3 us (55%)
  starting transfers between devices  13.2 us (21%)
  Pallas kernels  11.3 us (18%)
  local copies, waits for them, and re-layouts  3.03 us (5%)
  between operations  0.77 us (1%)
    ppermute x4, waiting for transfers between devices, per_device(): got = [lax.ppermute(piece, 'blk', forward) for piece in (piece, *pieces)]  31.8 us
    ppermute x3, starting transfers between devices, per_device(): sums += [kept, lax.ppermute(sent, 'tgt', across)]  3.91 us
    ppermute x2, starting transfers between devices, per_device(): lax.ppermute(sent, 'tgt', across)  3.5 us
    unnamed x8, local copies, waits for them, and re-layouts  3.03 us
    pallas_call x2, Pallas kernels, per_device(): call(functools.partial(pair_kernel, width, half), [f32(3 * width, half)]...  3 us
    ppermute x4, starting transfers between devices, per_device(): got = [lax.ppermute(piece, 'blk', forward) for piece in (piece, *pieces)]  2.82 us
    pallas_call x1, Pallas kernels, per_device(): call(functools.partial(self_kernel, half), [f32(half, rows)] * 2, [VMEM,...  2.35 us
    ppermute x1, starting transfers between devices, per_device(): returned = lax.ppermute(returned, 'blk', back)  2 us
  transfers between devices with their start and end apart: 12, of which 6 were waited for; matrix products, arithmetic and copies ran while one was open for 0% of the time, Pallas kernels for 16%

profile of v2, /device:TPU:1, one launch (start us, length us, event | category | flops | bytes accessed | tf_op | source)
XLA Modules:
  0.0 63.6 jit_solution(15173129458748741727)
XLA Ops:
  0.6 2.2 %copy-done = bf16[512,4096]{1,0:T(8,128)(2,1)S(1)} copy-done((bf16[512,4096]{1,0:T(8,128)(2,1)S(1)}, bf16[512,4096]{1,0:T(8,128)(2,1)}, u32[]{:S(2)}) %copy-start) | copy-done | bytes 4194328
  2.8 0.8 %copy-done.2 = bf16[512,64]{0,1:T(8,128)(2,1)S(1)} copy-done((bf16[512,64]{0,1:T(8,128)(2,1)S(1)}, bf16[512,64]{0,1:T(8,128)(2,1)}, u32[]{:S(2)}) %copy-start.2) | copy-done | bytes 65560
  3.9 2.1 %collective-permute-start.1 = (bf16[400,2048]{1,0:T(8,128)(2,1)S(1)}, bf16[400,2048]{1,0:T(8,128)(2,1)S(1)}, u32[]{:S(2)}, u32[]{:S(2)}) collective-permute-start(bf16[400,2048]{1,0:T(8,128)(2,1)S(1)} %shard_map.41.before), channel_id=1, source_target_pairs={{0,2},{2,6},{4,0},{6,4},{8,10},{10,14},{12,8},{14,12},{16,18},{18,... | collective-permute-start | bytes 4915208 | tf_op jit(solution)/shard_map/ppermute | solution.py:270
  6.0 2.4 %shard_map.42 = (f32[256,512]{1,0:T(8,128)S(1)}, f32[256,512]{1,0:T(8,128)S(1)}) custom-call(bf16[512,4096]{1,0:T(8,128)(2,1)S(1)} %copy-done, bf16[400,2048]{1,0:T(8,128)(2,1)S(1)} %shard_map.41.before), custom_call_target="tpu_custom_call" | custom-call | tf_op jit(solution)/shard_map/pallas_call | solution.py:260
  8.3 0.9 %shard_map.45 = (bf16[160,4096]{1,0:T(8,128)(2,1)S(1)}, bf16[96,4096]{1,0:T(8,128)(2,1)S(1)}, bf16[64,4096]{1,0:T(8,128)(2,1)S(1)}) custom-call(bf16[512,4096]{1,0:T(8,128)(2,1)S(1)} %copy-done, f32[256,512]{1,0:T(8,128)S(1)} %get-tuple-element.24.kept.before), custom_call_target="tpu_custom_call" | custom-call | tf_op jit(solution)/shard_map/pallas_call | solution.py:263
  9.9 1.7 %collective-permute-start = (f32[256,512]{1,0:T(8,128)S(1)}, f32[256,512]{1,0:T(8,128)S(1)}, u32[]{:S(2)}, u32[]{:S(2)}) collective-permute-start(f32[256,512]{1,0:T(8,128)S(1)} %get-tuple-element.25), channel_id=1, source_target_pairs={{0,1},{1,0},{2,3},{3,2},{4,5},{5,4},{6,7},{7,6},{8,9},{9,8},{10,11... | collective-permute-start | bytes 1572872 | tf_op jit(solution)/shard_map/ppermute | solution.py:273
  11.7 12.3 %collective-permute-done.1.piece = bf16[400,2048]{1,0:T(8,128)(2,1)S(1)} collective-permute-done((bf16[400,2048]{1,0:T(8,128)(2,1)S(1)}, bf16[400,2048]{1,0:T(8,128)(2,1)S(1)}, u32[]{:S(2)}, u32[]{:S(2)}) %collective-permute-start.1) | collective-permute-done | bytes 1638432 | tf_op jit(solution)/shard_map/ppermute | solution.py:270
  24.0 1.6 %shard_map.44 = (f32[288,256]{1,0:T(8,128)S(1)}, f32[288,256]{1,0:T(8,128)S(1)}, bf16[64,512]{1,0:T(8,128)(2,1)S(1)}) custom-call(bf16[400,2048]{1,0:T(8,128)(2,1)S(1)} %collective-permute-done.1.piece, bf16[512,4096]{1,0:T(8,128)(2,1)S(1)} %copy-done), custom_call_target="tpu_custom_call" | custom-call | tf_op jit(solution)/shard_map/pallas_call | solution.py:276
  25.6 1.3 %collective-permute-start.2 = (f32[288,256]{1,0:T(8,128)S(1)}, f32[288,256]{1,0:T(8,128)S(1)}, u32[]{:S(2)}, u32[]{:S(2)}) collective-permute-start(f32[288,256]{1,0:T(8,128)S(1)} %get-tuple-element.27), channel_id=1, source_target_pairs={{0,1},{1,0},{2,3},{3,2},{4,5},{5,4},{6,7},{7,6},{8,9},{9,8},{10,11... | collective-permute-start | bytes 884744 | tf_op jit(solution)/shard_map/ppermute | solution.py:282
  27.0 11.1 %collective-permute-done.3.piece = bf16[160,4096]{1,0:T(8,128)(2,1)S(1)} collective-permute-done((bf16[160,4096]{1,0:T(8,128)(2,1)S(1)}, bf16[160,4096]{1,0:T(8,128)(2,1)S(1)}, u32[]{:S(2)}, u32[]{:S(2)}) %collective-permute-start.3) | collective-permute-done | bytes 1310752 | tf_op jit(solution)/shard_map/ppermute | solution.py:270
  38.1 1.6 %shard_map.46 = (f32[240,256]{1,0:T(8,128)S(1)}, f32[240,256]{1,0:T(8,128)S(1)}) custom-call(bf16[160,4096]{1,0:T(8,128)(2,1)S(1)} %collective-permute-done.3.piece, bf16[512,4096]{1,0:T(8,128)(2,1)S(1)} %copy-done.1, bf16[256,512]{1,0:T(8,128)(2,1)S(1)} %shard_map.43.before.self_tile), custom_call_target="tpu_custom_call" | custom-call | tf_op jit(solution)/shard_map/pallas_call | solution.py:285
  39.6 1.3 %collective-permute-start.4 = (f32[240,256]{1,0:T(8,128)S(1)}, f32[240,256]{1,0:T(8,128)S(1)}, u32[]{:S(2)}, u32[]{:S(2)}) collective-permute-start(f32[240,256]{1,0:T(8,128)S(1)} %get-tuple-element.30), channel_id=1, source_target_pairs={{0,1},{1,0},{2,3},{3,2},{4,5},{5,4},{6,7},{7,6},{8,9},{9,8},{10,11... | collective-permute-start | bytes 737288 | tf_op jit(solution)/shard_map/ppermute | solution.py:291
  41.0 5.5 %collective-permute-done.5.piece = bf16[96,4096]{1,0:T(8,128)(2,1)S(1)} collective-permute-done((bf16[96,4096]{1,0:T(8,128)(2,1)S(1)}, bf16[96,4096]{1,0:T(8,128)(2,1)S(1)}, u32[]{:S(2)}, u32[]{:S(2)}) %collective-permute-start.5) | collective-permute-done | bytes 786464 | tf_op jit(solution)/shard_map/ppermute | solution.py:270
  46.5 1.4 %shard_map.47 = (f32[144,256]{1,0:T(8,128)S(1)}, f32[144,256]{1,0:T(8,128)S(1)}) custom-call(bf16[96,4096]{1,0:T(8,128)(2,1)S(1)} %collective-permute-done.5.piece, bf16[512,4096]{1,0:T(8,128)(2,1)S(1)} %copy-done.1, f32[240,256]{1,0:T(8,128)S(1)} %get-tuple-element.29.before.refs_2_), custom_call_target="tpu_custom_call" | custom-call | tf_op jit(solution)/shard_map/pallas_call | solution.py:285
  47.9 1.3 %collective-permute-start.6 = (f32[144,256]{1,0:T(8,128)S(1)}, f32[144,256]{1,0:T(8,128)S(1)}, u32[]{:S(2)}, u32[]{:S(2)}) collective-permute-start(f32[144,256]{1,0:T(8,128)S(1)} %get-tuple-element.33), channel_id=1, source_target_pairs={{0,1},{1,0},{2,3},{3,2},{4,5},{5,4},{6,7},{7,6},{8,9},{9,8},{10,11... | collective-permute-start | bytes 442376 | tf_op jit(solution)/shard_map/ppermute | solution.py:291
  49.2 2.9 %collective-permute-done.7.piece = bf16[64,4096]{1,0:T(8,128)(2,1)S(1)} collective-permute-done((bf16[64,4096]{1,0:T(8,128)(2,1)S(1)}, bf16[64,4096]{1,0:T(8,128)(2,1)S(1)}, u32[]{:S(2)}, u32[]{:S(2)}) %collective-permute-start.7) | collective-permute-done | bytes 524320 | tf_op jit(solution)/shard_map/ppermute | solution.py:270
  52.1 1.4 %shard_map.48 = (f32[64,256]{1,0:T(8,128)S(1)}, f32[64,256]{1,0:T(8,128)S(1)}, f32[32,512]{1,0:T(8,128)S(1)}, f32[32,512]{1,0:T(8,128)S(1)}) custom-call(bf16[64,4096]{1,0:T(8,128)(2,1)S(1)} %collective-permute-done.7.piece, bf16[512,4096]{1,0:T(8,128)(2,1)S(1)} %copy-done.1), custom_call_target="tpu_custom_call" | custom-call | tf_op jit(solution)/shard_map/pallas_call | solution.py:294
  53.7 2.0 %collective-permute-start.8 = (bf16[288,512]{1,0:T(8,128)(2,1)S(1)}, bf16[288,512]{1,0:T(8,128)(2,1)S(1)}, u32[]{:S(2)}, u32[]{:S(2)}) collective-permute-start(bf16[288,512]{1,0:T(8,128)(2,1)S(1)} %get-tuple-element.40), channel_id=1, source_target_pairs={{0,4},{2,0},{4,6},{6,2},{8,12},{10,8},{12,14},{14,10},{16,20},{18,... | collective-permute-start | bytes 884744 | tf_op jit(solution)/shard_map/ppermute | solution.py:312
  55.7 1.8 %collective-permute-start.9 = (f32[64,256]{1,0:T(8,128)S(1)}, f32[64,256]{1,0:T(8,128)S(1)}, u32[]{:S(2)}, u32[]{:S(2)}) collective-permute-start(f32[64,256]{1,0:T(8,128)S(1)} %get-tuple-element.41), channel_id=1, source_target_pairs={{0,1},{1,0},{2,3},{3,2},{4,5},{5,4},{6,7},{7,6},{8,9},{9,8},{10,11... | collective-permute-start | bytes 196616 | tf_op jit(solution)/shard_map/ppermute | solution.py:302
  57.5 1.0 %collective-permute-start.10 = (f32[32,512]{1,0:T(8,128)S(1)}, f32[32,512]{1,0:T(8,128)S(1)}, u32[]{:S(2)}, u32[]{:S(2)}) collective-permute-start(f32[32,512]{1,0:T(8,128)S(1)} %get-tuple-element.42), channel_id=1, source_target_pairs={{0,4},{2,0},{4,6},{6,2},{8,12},{10,8},{12,14},{14,10},{16,20},{18,... | collective-permute-start | bytes 196616 | tf_op jit(solution)/shard_map/ppermute | solution.py:303
  58.4 0.8 %shard_map.50 = (bf16[3,256,512]{2,1,0:T(8,128)(2,1)}, f32[64,256]{1,0:T(8,128)S(1)}) custom-call(bf16[256,512]{1,0:T(8,128)(2,1)S(1)} %shard_map.43.before.self_tile, bf16[512,256]{1,0:T(8,128)(2,1)S(1)} %get-tuple-element.36.met, bf16[64,512]{1,0:T(8,128)(2,1)S(1)} %bitcast.4, bf16[64,512]{1,0:T(8,128)(2,1)S(1)} %get-tuple-element.37.flat_before), custom_call_target="tpu_custom_call" | custom-call | tf_op jit(solution)/shard_map/pallas_call | solution.py:314
  59.2 1.5 %collective-permute-done.10.near = f32[32,512]{1,0:T(8,128)S(1)} collective-permute-done((f32[32,512]{1,0:T(8,128)S(1)}, f32[32,512]{1,0:T(8,128)S(1)}, u32[]{:S(2)}, u32[]{:S(2)}) %collective-permute-start.10) | collective-permute-done | bytes 65568 | tf_op jit(solution)/shard_map/ppermute | solution.py:303
  60.7 1.9 %collective-permute-done.11.cross = f32[32,512]{1,0:T(8,128)S(1)} collective-permute-done((f32[32,512]{1,0:T(8,128)S(1)}, f32[32,512]{1,0:T(8,128)S(1)}, u32[]{:S(2)}, u32[]{:S(2)}) %collective-permute-start.11) | collective-permute-done | bytes 65568 | tf_op jit(solution)/shard_map/ppermute | solution.py:304
  62.7 0.9 %shard_map.51 = (bf16[3,256,512]{2,1,0:T(8,128)(2,1)}, f32[64,256]{1,0:T(8,128)}) custom-call(bf16[3,256,512]{2,1,0:T(8,128)(2,1)} %get-tuple-element.38.before, f32[64,256]{1,0:T(8,128)S(1)} %get-tuple-element.39.partial, bf16[512,256]{1,0:T(8,128)(2,1)S(1)} %get-tuple-element.36.met, ...), custom_call_target="tpu_custom_call", output_to_operand_aliasing={{0}: (0, {})} | custom-call | tf_op jit(solution)/shard_map/pallas_call | solution.py:321
  (19 shorter events, 1.2 us)
Async XLA Ops:
  0.6 2.2 %copy-start = (bf16[512,4096]{1,0:T(8,128)(2,1)S(1)}, bf16[512,4096]{1,0:T(8,128)(2,1)}, u32[]{:S(2)}) copy-start(bf16[512,4096]{1,0:T(8,128)(2,1)} %grads.13) | copy-start | bytes 12582916
  2.8 0.8 %copy-start.2 = (bf16[512,64]{0,1:T(8,128)(2,1)S(1)}, bf16[512,64]{0,1:T(8,128)(2,1)}, u32[]{:S(2)}) copy-start(bf16[512,64]{0,1:T(8,128)(2,1)} %param.3) | copy-start | bytes 196612
  3.9 20.1 %collective-permute-start.1 = (bf16[400,2048]{1,0:T(8,128)(2,1)S(1)}, bf16[400,2048]{1,0:T(8,128)(2,1)S(1)}, u32[]{:S(2)}, u32[]{:S(2)}) collective-permute-start(bf16[400,2048]{1,0:T(8,128)(2,1)S(1)} %shard_map.41.before), channel_id=1, source_target_pairs={{0,2},{2,6},{4,0},{6,4},{8,10},{10,14},{12,8},{14,12},{16,18},{18,... | collective-permute-start | bytes 4915208 | tf_op jit(solution)/shard_map/ppermute | solution.py:270
  9.2 28.9 %collective-permute-start.3 = (bf16[160,4096]{1,0:T(8,128)(2,1)S(1)}, bf16[160,4096]{1,0:T(8,128)(2,1)S(1)}, u32[]{:S(2)}, u32[]{:S(2)}) collective-permute-start(bf16[160,4096]{1,0:T(8,128)(2,1)S(1)} %get-tuple-element.28), channel_id=1, source_target_pairs={{0,2},{2,6},{4,0},{6,4},{8,10},{10,14},{12,8},{14,12},{16,18},{18,... | collective-permute-start | bytes 3932168 | tf_op jit(solution)/shard_map/ppermute | solution.py:270
  9.9 36.6 %collective-permute-start.5 = (bf16[96,4096]{1,0:T(8,128)(2,1)S(1)}, bf16[96,4096]{1,0:T(8,128)(2,1)S(1)}, u32[]{:S(2)}, u32[]{:S(2)}) collective-permute-start(bf16[96,4096]{1,0:T(8,128)(2,1)S(1)} %get-tuple-element.31), channel_id=1, source_target_pairs={{0,2},{2,6},{4,0},{6,4},{8,10},{10,14},{12,8},{14,12},{16,18},{18,... | collective-permute-start | bytes 2359304 | tf_op jit(solution)/shard_map/ppermute | solution.py:270
  9.9 17.0 %collective-permute-start = (f32[256,512]{1,0:T(8,128)S(1)}, f32[256,512]{1,0:T(8,128)S(1)}, u32[]{:S(2)}, u32[]{:S(2)}) collective-permute-start(f32[256,512]{1,0:T(8,128)S(1)} %get-tuple-element.25), channel_id=1, source_target_pairs={{0,1},{1,0},{2,3},{3,2},{4,5},{5,4},{6,7},{7,6},{8,9},{9,8},{10,11... | collective-permute-start | bytes 1572872 | tf_op jit(solution)/shard_map/ppermute | solution.py:273
  11.7 40.4 %collective-permute-start.7 = (bf16[64,4096]{1,0:T(8,128)(2,1)S(1)}, bf16[64,4096]{1,0:T(8,128)(2,1)S(1)}, u32[]{:S(2)}, u32[]{:S(2)}) collective-permute-start(bf16[64,4096]{1,0:T(8,128)(2,1)S(1)} %get-tuple-element.34), channel_id=1, source_target_pairs={{0,2},{2,6},{4,0},{6,4},{8,10},{10,14},{12,8},{14,12},{16,18},{18,... | collective-permute-start | bytes 1572872 | tf_op jit(solution)/shard_map/ppermute | solution.py:270
  24.0 14.0 %copy-start.1 = (bf16[512,4096]{1,0:T(8,128)(2,1)S(1)}, bf16[512,4096]{1,0:T(8,128)(2,1)}, u32[]{:S(2)}) copy-start(bf16[512,4096]{1,0:T(8,128)(2,1)} %grads.13) | copy-start | bytes 12582916
  25.6 27.9 %collective-permute-start.2 = (f32[288,256]{1,0:T(8,128)S(1)}, f32[288,256]{1,0:T(8,128)S(1)}, u32[]{:S(2)}, u32[]{:S(2)}) collective-permute-start(f32[288,256]{1,0:T(8,128)S(1)} %get-tuple-element.27), channel_id=1, source_target_pairs={{0,1},{1,0},{2,3},{3,2},{4,5},{5,4},{6,7},{7,6},{8,9},{9,8},{10,11... | collective-permute-start | bytes 884744 | tf_op jit(solution)/shard_map/ppermute | solution.py:282
  39.6 13.9 %collective-permute-start.4 = (f32[240,256]{1,0:T(8,128)S(1)}, f32[240,256]{1,0:T(8,128)S(1)}, u32[]{:S(2)}, u32[]{:S(2)}) collective-permute-start(f32[240,256]{1,0:T(8,128)S(1)} %get-tuple-element.30), channel_id=1, source_target_pairs={{0,1},{1,0},{2,3},{3,2},{4,5},{5,4},{6,7},{7,6},{8,9},{9,8},{10,11... | collective-permute-start | bytes 737288 | tf_op jit(solution)/shard_map/ppermute | solution.py:291
  47.9 5.6 %copy-start.3 = (bf16[512,64]{0,1:T(8,128)(2,1)S(1)}, bf16[512,64]{0,1:T(8,128)(2,1)}, u32[]{:S(2)}) copy-start(bf16[512,64]{0,1:T(8,128)(2,1)} %param.3) | copy-start | bytes 196612
  47.9 5.6 %collective-permute-start.6 = (f32[144,256]{1,0:T(8,128)S(1)}, f32[144,256]{1,0:T(8,128)S(1)}, u32[]{:S(2)}, u32[]{:S(2)}) collective-permute-start(f32[144,256]{1,0:T(8,128)S(1)} %get-tuple-element.33), channel_id=1, source_target_pairs={{0,1},{1,0},{2,3},{3,2},{4,5},{5,4},{6,7},{7,6},{8,9},{9,8},{10,11... | collective-permute-start | bytes 442376 | tf_op jit(solution)/shard_map/ppermute | solution.py:291
  53.7 9.0 %collective-permute-start.8 = (bf16[288,512]{1,0:T(8,128)(2,1)S(1)}, bf16[288,512]{1,0:T(8,128)(2,1)S(1)}, u32[]{:S(2)}, u32[]{:S(2)}) collective-permute-start(bf16[288,512]{1,0:T(8,128)(2,1)S(1)} %get-tuple-element.40), channel_id=1, source_target_pairs={{0,4},{2,0},{4,6},{6,2},{8,12},{10,8},{12,14},{14,10},{16,20},{18,... | collective-permute-start | bytes 884744 | tf_op jit(solution)/shard_map/ppermute | solution.py:312
  55.7 3.5 %collective-permute-start.9 = (f32[64,256]{1,0:T(8,128)S(1)}, f32[64,256]{1,0:T(8,128)S(1)}, u32[]{:S(2)}, u32[]{:S(2)}) collective-permute-start(f32[64,256]{1,0:T(8,128)S(1)} %get-tuple-element.41), channel_id=1, source_target_pairs={{0,1},{1,0},{2,3},{3,2},{4,5},{5,4},{6,7},{7,6},{8,9},{9,8},{10,11... | collective-permute-start | bytes 196616 | tf_op jit(solution)/shard_map/ppermute | solution.py:302
  57.5 3.3 %collective-permute-start.10 = (f32[32,512]{1,0:T(8,128)S(1)}, f32[32,512]{1,0:T(8,128)S(1)}, u32[]{:S(2)}, u32[]{:S(2)}) collective-permute-start(f32[32,512]{1,0:T(8,128)S(1)} %get-tuple-element.42), channel_id=1, source_target_pairs={{0,4},{2,0},{4,6},{6,2},{8,12},{10,8},{12,14},{14,10},{16,20},{18,... | collective-permute-start | bytes 196616 | tf_op jit(solution)/shard_map/ppermute | solution.py:303
  58.4 4.2 %collective-permute-start.11 = (f32[32,512]{1,0:T(8,128)S(1)}, f32[32,512]{1,0:T(8,128)S(1)}, u32[]{:S(2)}, u32[]{:S(2)}) collective-permute-start(f32[32,512]{1,0:T(8,128)S(1)} %get-tuple-element.43), channel_id=1, source_target_pairs={{0,5},{1,4},{2,1},{3,0},{4,7},{5,6},{6,3},{7,2},{8,13},{9,12},{10,... | collective-permute-start | bytes 196616 | tf_op jit(solution)/shard_map/ppermute | solution.py:304

commit v3 on v2

v3 whole, which is shorter than its diff:
```python
import functools

import jax
import jax.numpy as jnp
from jax import lax
from jax.experimental import pallas as pl
from jax.experimental.pallas import tpu as pltpu
from jax.sharding import PartitionSpec as P

AFTER = {0: 1, 1: 3, 3: 2, 2: 0}
BEFORE = {after: before for before, after in AFTER.items()}
SIXTEENTHS = (7, 5, 2, 2)

FIRST_VMEM = 50
VMEM = pl.BlockSpec(memory_space=pltpu.VMEM)
ANY = pl.BlockSpec(memory_space=pl.ANY)
COST = pl.CostEstimate(flops=0, bytes_accessed=0, transcendentals=0)


def call(kernel, out, in_specs, out_specs, scratch=(), aliases=None, vmem=16):
    return pl.pallas_call(
        kernel,
        out_shape=out,
        in_specs=in_specs,
        out_specs=out_specs,
        scratch_shapes=scratch,
        input_output_aliases=aliases or {},
        cost_estimate=COST,
        compiler_params=pltpu.CompilerParams(vmem_limit_bytes=vmem * 2**20),
    )


def contract(left, right):
    return lax.dot_general(
        left, right, (((1,), (1,)), ((), ())), preferred_element_type=jnp.float32
    )


def multiply(left, right):
    return jnp.dot(left, right, preferred_element_type=jnp.float32)


def part_of(index, size):
    return pl.ds(pl.multiple_of(index * size, size), size)


def run_copies(copies, sems):
    copies = [pltpu.make_async_copy(*ends, sems.at[i]) for i, ends in enumerate(copies)]
    for copy in copies:
        copy.start()
    for copy in copies:
        copy.wait()


def first_kernel(width, half, grads, out, mark, sems):
    run_copies(
        [
            (grads.at[pl.ds(h * half, width)], out.at[pl.ds(h * width, width)])
            for h in range(2)
        ],
        sems,
    )
    mark[...] = jnp.zeros_like(mark)


def load_kernel(grads, before, out, sems):
    del before
    size = grads.shape[0] // 4
    run_copies([(grads.at[pl.ds(i * size, size)], out.at[pl.ds(i * size, size)]) for i in range(4)], sems)


def rest_kernel(spans, half, grads, before, *refs):
    del before
    *outs, sems = refs
    run_copies(
        [
            (grads.at[pl.ds(h * half + at, width)], out.at[pl.ds(h * width, width)])
            for (at, width), out in zip(spans, outs)
            for h in range(2)
        ],
        sems,
    )


def self_kernel(half, grads, before, sent, kept):
    del before
    t = lax.axis_index("tgt")
    sent[...] = contract(grads[part_of(1 - t, half), :], grads[...])
    kept[...] = contract(grads[part_of(t, half), :], grads[...])


def self_finish_kernel(scale, kept, got, tile):
    tile[...] = ((kept[...] + got[...]) * scale).astype(jnp.bfloat16)


def share(sent, kept, width):
    t = lax.axis_index("tgt")
    sent[2 * width :, :] = kept[part_of(1 - t, width), :]
    kept[2 * width :, :] = sent[part_of(t, width), :]


def pair_kernel(width, half, piece, grads, before, sent, kept):
    del before
    t = lax.axis_index("tgt")
    sent[: 2 * width, :] = contract(piece[...], grads[part_of(1 - t, half), :])
    kept[: 2 * width, :] = contract(piece[...], grads[part_of(t, half), :])
    share(sent, kept, width)


def last_pair_kernel(width, half, scale, piece, grads, third, got, before, sent, kept, near, cross, tile):
    del before
    t = lax.axis_index("tgt")
    sent[...] = contract(piece[...], grads[part_of(1 - t, half), :])
    kept[...] = contract(piece[...], grads[part_of(t, half), :])
    for to, index in ((near, t), (cross, 1 - t)):
        to[:width, part_of(t, half)] = kept[part_of(index, width), :]
        to[:width, part_of(1 - t, half)] = sent[part_of(index, width), :]
    above = tile.shape[0] // 2
    value = (third[...] + got[...]) * scale
    tile[...] = value[: 2 * above].astype(jnp.bfloat16)
    near[width:, part_of(1 - t, half)] = value[2 * above :]
    rows = part_of(t, above)
    near[width:, part_of(t, half)] = (third[rows, :] + got[rows, :]) * scale


def finish_kernel(widths, half, scale, flat, before, *refs):
    del before
    *ins, tile, back, copy = refs
    t = lax.axis_index("tgt")
    at, total = 0, sum(widths)
    for i, width in enumerate(widths):
        kept, got = ins[2 * i : 2 * i + 2]
        value = ((kept[...] + got[...]) * scale).astype(jnp.bfloat16)
        for h in range(2):
            tile[h * total + at : h * total + at + width, :] = value[h * width : (h + 1) * width]
        back[at : at + width, part_of(1 - t, half)] = value[2 * width :]
        at += width
    back[:, part_of(t, half)] = tile[part_of(t, total), :]
    copy[...] = flat[...]


def own_slot():
    place = lax.rem(lax.axis_index("blk"), 4)
    return jnp.where((place == 1) | (place == 2), 1, 2)


def most_kernel(half, edge, self_tile, tile, flat, tiles, partial, turned, sems):
    slot = own_slot()
    whole = pltpu.make_async_copy(self_tile, tiles.at[0], sems.at[0])
    whole.start()
    partial[...] = contract(flat[...], self_tile[...])
    copies, size = [], tile.shape[0] // 2
    for h in range(2):
        part = tile[h * size : h * size + edge, :]
        turned[h] = part.T
        copies.append(
            pltpu.make_async_copy(
                turned.at[h], tiles.at[slot, :, pl.ds(h * half, edge)], sems.at[1 + h]
            )
        )
        copies[h].start()
    whole.wait()
    for copy in copies:
        copy.wait()


def last_kernel(
    half, edge, scale, before, partial, early, third, back_early, flat_before, flat_after,
    kept, got, near, cross, tiles, influence, turned, far, late, total, sems,
):
    del before
    slot = own_slot()
    width = cross.shape[0]
    first, second = early.shape[0] // 2, third.shape[0] // 2
    done = first + second
    copies = []

    def copy(source, target):
        copies.append(pltpu.make_async_copy(source, target, sems.at[len(copies)]))
        copies[-1].start()

    copy(back_early, tiles.at[3 - slot, pl.ds(0, first)])
    far[first:done, :] = near[width:, :].astype(jnp.bfloat16)
    far[done:, :] = ((near[:width, :] + cross[...]) * scale).astype(jnp.bfloat16)
    copy(
        far.at[pl.ds(first, second + width)], tiles.at[3 - slot, pl.ds(first, second + width)]
    )
    new = ((kept[...] + got[...]) * scale).astype(jnp.bfloat16)
    value = partial[...]
    for h in range(2):
        late[h, : first - edge, :] = early[h * first + edge : (h + 1) * first, :]
        late[h, first - edge : done - edge, :] = third[h * second : (h + 1) * second, :]
        late[h, done - edge :, :] = new[h * width : (h + 1) * width]
        turned[h] = late[h].T
        copy(turned.at[h], tiles.at[slot, :, pl.ds(h * half + edge, half - edge)])
        value += multiply(
            flat_before[:, h * half : h * half + edge], early[h * first : h * first + edge, :]
        ) + multiply(flat_before[:, h * half + edge : (h + 1) * half], late[h])
    far[:first, :] = back_early[...]
    total[...] = value + contract(flat_after[...], far[...])
    copy(total, influence)
    for each in copies:
        each.wait()


def per_device(gradients, targets):
    blocks, groups = lax.axis_size("blk"), lax.axis_size("tgt")
    rows, features = gradients.shape
    columns = targets.shape[1]
    half = rows // groups
    scale = 1.0 / (features * groups) ** 0.5
    forward = [(b, b - b % 4 + AFTER[b % 4]) for b in range(blocks)]
    back = [(b, b - b % 4 + BEFORE[b % 4]) for b in range(blocks)]
    across = [(t, 1 - t) for t in range(groups)]
    back_across = [(b * groups + t, c * groups + 1 - t) for b, c in back for t in range(groups)]

    def f32(*shape):
        return jax.ShapeDtypeStruct(shape, jnp.float32)

    def b16(*shape):
        return jax.ShapeDtypeStruct(shape, jnp.bfloat16)

    widths = [half * n // 16 for n in SIXTEENTHS]
    spans = [(sum(widths[:i]), w) for i, w in enumerate(widths)]
    first = spans[2][0]
    edge = half // 2
    flat = targets.T

    piece, mark = call(
        functools.partial(first_kernel, widths[0], half),
        [b16(2 * widths[0], features), f32(8, 128)],
        [ANY],
        [ANY, VMEM],
        [pltpu.SemaphoreType.DMA((2,))],
        vmem=FIRST_VMEM,
    )(gradients)
    gradients = call(
        load_kernel,
        b16(rows, features),
        [ANY] * 2,
        ANY,
        [pltpu.SemaphoreType.DMA((4,))],
        vmem=48,
    )(gradients, mark)
    sent, kept = call(
        functools.partial(self_kernel, half), [f32(half, rows)] * 2, [VMEM, ANY], [VMEM] * 2
    )(gradients, mark)
    pieces = call(
        functools.partial(rest_kernel, spans[1:], half),
        [b16(2 * w, features) for w in widths[1:]],
        [ANY] * 2,
        [ANY] * len(widths[1:]),
        [pltpu.SemaphoreType.DMA((2 * len(widths[1:]),))],
    )(gradients, kept)
    got = [lax.ppermute(piece, "blk", forward) for piece in (piece, *pieces)]
    self_tile = call(
        functools.partial(self_finish_kernel, scale), b16(half, rows), [VMEM] * 2, VMEM
    )(kept, lax.ppermute(sent, "tgt", across))

    def pair(width, piece, after):
        sent, kept = call(
            functools.partial(pair_kernel, width, half),
            [f32(3 * width, half)] * 2,
            [VMEM] * 2 + [ANY],
            [VMEM] * 2,
        )(piece, gradients, after)
        return [kept, lax.ppermute(sent, "tgt", across)]

    flat_before = lax.ppermute(flat, "blk", forward)
    sums = pair(widths[0], got[0], mark) + pair(widths[1], got[1], mark)
    third_sums = pair(widths[2], got[2], self_tile)
    early, back_early, flat_after = call(
        functools.partial(finish_kernel, widths[:2], half, scale),
        [b16(2 * first, half), b16(first, rows), b16(columns, rows)],
        [VMEM, ANY] + [VMEM] * 4,
        [VMEM] * 3,
    )(flat, third_sums[0], *sums)
    back_early = lax.ppermute(back_early, "blk", back)
    flat_after = lax.ppermute(flat_after, "blk", back)
    *_, second, width = widths
    sent, kept, near, cross, third = call(
        functools.partial(last_pair_kernel, width, half, scale),
        [f32(2 * width, half)] * 2
        + [f32(width + second, rows), f32(width, rows), b16(2 * second, half)],
        [VMEM] * 4 + [ANY],
        [VMEM] * 5,
    )(got[3], gradients, *third_sums, early)
    cross = lax.ppermute(cross, ("blk", "tgt"), back_across)
    near = lax.ppermute(near, "blk", back)
    sent = lax.ppermute(sent, "tgt", across)

    tiles, partial = call(
        functools.partial(most_kernel, half, edge),
        [b16(3, half, rows), f32(columns, half)],
        [VMEM] * 3,
        [ANY, VMEM],
        [pltpu.VMEM((2, half, edge), jnp.bfloat16), pltpu.SemaphoreType.DMA((3,))],
    )(self_tile, early, flat)
    tiles, influence = call(
        functools.partial(last_kernel, half, edge, scale),
        [b16(3, half, rows), f32(columns, half)],
        [ANY] + [VMEM] * 10,
        [ANY] * 2,
        [
            pltpu.VMEM((2, half, half - edge), jnp.bfloat16),
            pltpu.VMEM((half, rows), jnp.bfloat16),
            pltpu.VMEM((2, half - edge, half), jnp.bfloat16),
            pltpu.VMEM((columns, half), jnp.float32),
            pltpu.SemaphoreType.DMA((5,)),
        ],
        {0: 0},
    )(tiles, partial, early, third, back_early, flat_before, flat_after,
      kept, sent, near, cross)
    return tiles, influence.T


def solution(mesh):
    return jax.shard_map(
        per_device,
        mesh=mesh,
        in_specs=(P("blk", "tgt"), P("blk", None)),
        out_specs=(P(None, ("blk", "tgt"), None), P(("blk", "tgt"), None)),
        check_vma=False,
    )
```

time: 64.1 us -> 61 us (0.952)
  waiting for transfers between devices: 35.3 us -> 29.2 us
  starting transfers between devices: 13.2 us -> 16.6 us
  local copies, waits for them, and re-layouts: 3.03 us -> 0.01 us
  Pallas kernels: 11.3 us -> 14.3 us
    ppermute x4, waiting for transfers between devices: 31.8 us -> 26.2 us  [per_device(): got = [lax.ppermute(piece, 'blk', forward) for piece in (piece, *pieces)]]
    ppermute x6 -> x9, starting transfers between devices: 6.87 us -> 11.7 us  [the longest x3 3.89 us: pair(): return [kept, lax.ppermute(sent, 'tgt', across)]]
    pallas_call x6 -> x7, Pallas kernels: 6.33 us -> 9.63 us  [the longest x3 4.42 us: pair(): call(functools.partial(pair_kernel, width, half), [f32(3 * width, half)]...]
    unnamed x8 -> x2, local copies, waits for them, and re-layouts: 3.03 us -> 0.01 us
    ppermute x2 -> x1, starting transfers between devices: 3.5 us -> 1.24 us  [per_device(): lax.ppermute(sent, 'tgt', across)]
    ppermute x4, starting transfers between devices: 2.82 us -> 3.64 us  [per_device(): got = [lax.ppermute(piece, 'blk', forward) for piece in (piece, *pieces)]]
    ppermute x6 -> x9, waiting for transfers between devices: 3.44 us -> 3.02 us  [the longest x1 1.65 us: per_device(): cross = lax.ppermute(cross, ('blk', 'tgt'), back_across)]
  transfers between devices with their start and end apart: 12 -> 14, of which waited for: 6 -> 5; matrix products, arithmetic and copies ran while one was open for 0% -> 0% of each run, Pallas kernels for 16% -> 20%
where the time goes in v3:
time: 61 us; the launch traced here: 60.9 us
  waiting for transfers between devices  29.2 us (48%)
  starting transfers between devices  16.6 us (27%)
  Pallas kernels  14.3 us (23%)
  between operations  0.74 us (1%)
    ppermute x4, waiting for transfers between devices, per_device(): got = [lax.ppermute(piece, 'blk', forward) for piece in (piece, *pieces)]  26.2 us
    pallas_call x3, Pallas kernels, pair(): call(functools.partial(pair_kernel, width, half), [f32(3 * width, half)]...  4.42 us
    ppermute x3, starting transfers between devices, pair(): return [kept, lax.ppermute(sent, 'tgt', across)]  3.89 us
    ppermute x4, starting transfers between devices, per_device(): got = [lax.ppermute(piece, 'blk', forward) for piece in (piece, *pieces)]  3.64 us
    ppermute x1, starting transfers between devices, per_device(): back_early = lax.ppermute(back_early, 'blk', back)  2.81 us
    ppermute x1, starting transfers between devices, per_device(): near = lax.ppermute(near, 'blk', back)  2.38 us
    pallas_call x1, Pallas kernels, per_device(): call(functools.partial(self_kernel, half), [f32(half, rows)] * 2, [VMEM,...  2.35 us
    pallas_call x1, Pallas kernels, per_device(): call(load_kernel, b16(rows, features), [ANY] * 2, ANY, [pltpu.SemaphoreTy...  2.2 us
  transfers between devices with their start and end apart: 14, of which 5 were waited for; matrix products, arithmetic and copies ran while one was open for 0% of the time, Pallas kernels for 20%

profile of v3, /device:TPU:1, one launch (start us, length us, event | category | flops | bytes accessed | tf_op | source)
XLA Modules:
  0.0 60.9 jit_solution(12320027099829917434)
XLA Ops:
  0.6 1.5 %shard_map.41 = (bf16[224,4096]{1,0:T(8,128)(2,1)S(1)}, f32[8,128]{1,0:T(8,128)S(1)}) custom-call(bf16[512,4096]{1,0:T(8,128)(2,1)} %grads.3), custom_call_target="tpu_custom_call" | custom-call | tf_op jit(solution)/shard_map/pallas_call | solution.py:229
  2.1 2.1 %collective-permute-start.2 = (bf16[224,4096]{1,0:T(8,128)(2,1)S(1)}, bf16[224,4096]{1,0:T(8,128)(2,1)S(1)}, u32[]{:S(2)}, u32[]{:S(2)}) collective-permute-start(bf16[224,4096]{1,0:T(8,128)(2,1)S(1)} %get-tuple-element.32), channel_id=1, source_target_pairs={{0,2},{2,6},{4,0},{6,4},{8,10},{10,14},{12,8},{14,12},{16,18},{18,... | collective-permute-start | bytes 5505032 | tf_op jit(solution)/shard_map/ppermute | solution.py:255
  4.2 2.2 %shard_map.42.grads = bf16[512,4096]{1,0:T(8,128)(2,1)S(1)} custom-call(bf16[512,4096]{1,0:T(8,128)(2,1)} %grads.3, f32[8,128]{1,0:T(8,128)S(1)} %get-tuple-element.27.before), custom_call_target="tpu_custom_call" | custom-call | tf_op jit(solution)/shard_map/pallas_call | solution.py:237
  6.4 2.4 %shard_map.43 = (f32[256,512]{1,0:T(8,128)S(1)}, f32[256,512]{1,0:T(8,128)S(1)}) custom-call(bf16[512,4096]{1,0:T(8,128)(2,1)S(1)} %shard_map.42.grads, f32[8,128]{1,0:T(8,128)S(1)} %get-tuple-element.27.before), custom_call_target="tpu_custom_call" | custom-call | tf_op jit(solution)/shard_map/pallas_call | solution.py:245
  9.3 0.7 %collective-permute-start.4 = (bf16[160,4096]{1,0:T(8,128)(2,1)S(1)}, bf16[160,4096]{1,0:T(8,128)(2,1)S(1)}, u32[]{:S(2)}, u32[]{:S(2)}) collective-permute-start(bf16[160,4096]{1,0:T(8,128)(2,1)S(1)} %get-tuple-element.35), channel_id=1, source_target_pairs={{0,2},{2,6},{4,0},{6,4},{8,10},{10,14},{12,8},{14,12},{16,18},{18,... | collective-permute-start | bytes 3932168 | tf_op jit(solution)/shard_map/ppermute | solution.py:255
  10.0 1.2 %collective-permute-start = (f32[256,512]{1,0:T(8,128)S(1)}, f32[256,512]{1,0:T(8,128)S(1)}, u32[]{:S(2)}, u32[]{:S(2)}) collective-permute-start(f32[256,512]{1,0:T(8,128)S(1)} %get-tuple-element.29), channel_id=1, source_target_pairs={{0,1},{1,0},{2,3},{3,2},{4,5},{5,4},{6,7},{7,6},{8,9},{9,8},{10,11... | collective-permute-start | bytes 1572872 | tf_op jit(solution)/shard_map/ppermute | solution.py:258
  11.2 0.6 collective-permute-start.1
  12.1 12.2 %collective-permute-done.2.piece = bf16[224,4096]{1,0:T(8,128)(2,1)S(1)} collective-permute-done((bf16[224,4096]{1,0:T(8,128)(2,1)S(1)}, bf16[224,4096]{1,0:T(8,128)(2,1)S(1)}, u32[]{:S(2)}, u32[]{:S(2)}) %collective-permute-start.2) | collective-permute-done | bytes 1835040 | tf_op jit(solution)/shard_map/ppermute | solution.py:255
  24.3 1.4 %shard_map.47 = (f32[336,256]{1,0:T(8,128)S(1)}, f32[336,256]{1,0:T(8,128)S(1)}) custom-call(bf16[224,4096]{1,0:T(8,128)(2,1)S(1)} %collective-permute-done.2.piece, bf16[512,4096]{1,0:T(8,128)(2,1)S(1)} %shard_map.42.grads, f32[8,128]{1,0:T(8,128)S(1)} %get-tuple-element.27.before), custom_call_target="tpu_custom_call" | custom-call | tf_op jit(solution)/shard_map/pallas_call | solution.py:261
  25.8 1.3 %collective-permute-start.3 = (f32[336,256]{1,0:T(8,128)S(1)}, f32[336,256]{1,0:T(8,128)S(1)}, u32[]{:S(2)}, u32[]{:S(2)}) collective-permute-start(f32[336,256]{1,0:T(8,128)S(1)} %get-tuple-element.34), channel_id=1, source_target_pairs={{0,1},{1,0},{2,3},{3,2},{4,5},{5,4},{6,7},{7,6},{8,9},{9,8},{10,11... | collective-permute-start | bytes 1032200 | tf_op jit(solution)/shard_map/ppermute | solution.py:267
  27.1 11.3 %collective-permute-done.4.piece = bf16[160,4096]{1,0:T(8,128)(2,1)S(1)} collective-permute-done((bf16[160,4096]{1,0:T(8,128)(2,1)S(1)}, bf16[160,4096]{1,0:T(8,128)(2,1)S(1)}, u32[]{:S(2)}, u32[]{:S(2)}) %collective-permute-start.4) | collective-permute-done | bytes 1310752 | tf_op jit(solution)/shard_map/ppermute | solution.py:255
  38.4 1.6 %shard_map.48 = (f32[240,256]{1,0:T(8,128)S(1)}, f32[240,256]{1,0:T(8,128)S(1)}) custom-call(bf16[160,4096]{1,0:T(8,128)(2,1)S(1)} %collective-permute-done.4.piece, bf16[512,4096]{1,0:T(8,128)(2,1)S(1)} %shard_map.42.grads, f32[8,128]{1,0:T(8,128)S(1)} %get-tuple-element.27.before), custom_call_target="tpu_custom_call" | custom-call | tf_op jit(solution)/shard_map/pallas_call | solution.py:261
  40.0 1.3 %collective-permute-start.5 = (f32[240,256]{1,0:T(8,128)S(1)}, f32[240,256]{1,0:T(8,128)S(1)}, u32[]{:S(2)}, u32[]{:S(2)}) collective-permute-start(f32[240,256]{1,0:T(8,128)S(1)} %get-tuple-element.37), channel_id=1, source_target_pairs={{0,1},{1,0},{2,3},{3,2},{4,5},{5,4},{6,7},{7,6},{8,9},{9,8},{10,11... | collective-permute-start | bytes 737288 | tf_op jit(solution)/shard_map/ppermute | solution.py:267
  41.4 2.7 %collective-permute-done.1.piece = bf16[64,4096]{1,0:T(8,128)(2,1)S(1)} collective-permute-done((bf16[64,4096]{1,0:T(8,128)(2,1)S(1)}, bf16[64,4096]{1,0:T(8,128)(2,1)S(1)}, u32[]{:S(2)}, u32[]{:S(2)}) %collective-permute-start.1) | collective-permute-done | bytes 524320 | tf_op jit(solution)/shard_map/ppermute | solution.py:255
  44.0 1.4 %shard_map.46 = (f32[96,256]{1,0:T(8,128)S(1)}, f32[96,256]{1,0:T(8,128)S(1)}) custom-call(bf16[64,4096]{1,0:T(8,128)(2,1)S(1)} %collective-permute-done.1.piece, bf16[512,4096]{1,0:T(8,128)(2,1)S(1)} %shard_map.42.grads, bf16[256,512]{1,0:T(8,128)(2,1)S(1)} %shard_map.44.before.self_tile), custom_call_target="tpu_custom_call" | custom-call | tf_op jit(solution)/shard_map/pallas_call | solution.py:261
  45.4 1.3 %collective-permute-start.7 = (f32[96,256]{1,0:T(8,128)S(1)}, f32[96,256]{1,0:T(8,128)S(1)}, u32[]{:S(2)}, u32[]{:S(2)}) collective-permute-start(f32[96,256]{1,0:T(8,128)S(1)} %get-tuple-element.42), channel_id=1, source_target_pairs={{0,1},{1,0},{2,3},{3,2},{4,5},{5,4},{6,7},{7,6},{8,9},{9,8},{10,11... | collective-permute-start | bytes 294920 | tf_op jit(solution)/shard_map/ppermute | solution.py:267
  46.9 2.8 %collective-permute-start.8 = (bf16[192,512]{1,0:T(8,128)(2,1)S(1)}, bf16[192,512]{1,0:T(8,128)(2,1)S(1)}, u32[]{:S(2)}, u32[]{:S(2)}) collective-permute-start(bf16[192,512]{1,0:T(8,128)(2,1)S(1)} %get-tuple-element.44), channel_id=1, source_target_pairs={{0,4},{2,0},{4,6},{6,2},{8,12},{10,8},{12,14},{14,10},{16,20},{18,... | collective-permute-start | bytes 589832 | tf_op jit(solution)/shard_map/ppermute | solution.py:278
  49.8 1.4 %shard_map.51 = (f32[64,256]{1,0:T(8,128)S(1)}, f32[64,256]{1,0:T(8,128)S(1)}, f32[64,512]{1,0:T(8,128)S(1)}, f32[32,512]{1,0:T(8,128)S(1)}, bf16[64,256]{1,0:T(8,128)(2,1)S(1)}) custom-call(bf16[64,4096]{1,0:T(8,128)(2,1)S(1)} %collective-permute-done.6.piece, bf16[512,4096]{1,0:T(8,128)(2,1)S(1)} %shard_map.42.grads, ...), custom_call_target="tpu_custom_call" | custom-call | tf_op jit(solution)/shard_map/pallas_call | solution.py:281
  51.2 2.4 %collective-permute-start.12 = (f32[64,512]{1,0:T(8,128)S(1)}, f32[64,512]{1,0:T(8,128)S(1)}, u32[]{:S(2)}, u32[]{:S(2)}) collective-permute-start(f32[64,512]{1,0:T(8,128)S(1)} %get-tuple-element.48), channel_id=1, source_target_pairs={{0,4},{2,0},{4,6},{6,2},{8,12},{10,8},{12,14},{14,10},{16,20},{18,... | collective-permute-start | bytes 393224 | tf_op jit(solution)/shard_map/ppermute | solution.py:289
  53.9 2.0 %collective-permute-start.11 = (f32[64,256]{1,0:T(8,128)S(1)}, f32[64,256]{1,0:T(8,128)S(1)}, u32[]{:S(2)}, u32[]{:S(2)}) collective-permute-start(f32[64,256]{1,0:T(8,128)S(1)} %get-tuple-element.47), channel_id=1, source_target_pairs={{0,1},{1,0},{2,3},{3,2},{4,5},{5,4},{6,7},{7,6},{8,9},{9,8},{10,11... | collective-permute-start | bytes 196616 | tf_op jit(solution)/shard_map/ppermute | solution.py:290
  56.1 0.8 %shard_map.50 = (bf16[3,256,512]{2,1,0:T(8,128)(2,1)}, f32[64,256]{1,0:T(8,128)S(1)}) custom-call(bf16[256,512]{1,0:T(8,128)(2,1)S(1)} %shard_map.44.before.self_tile, bf16[384,256]{1,0:T(8,128)(2,1)S(1)} %get-tuple-element.38.tile.before.early, bf16[64,512]{1,0:T(8,128)(2,1)S(1)} %bitcast.4), custom_call_target="tpu_custom_call" | custom-call | tf_op jit(solution)/shard_map/pallas_call | solution.py:292
  56.9 1.4 %collective-permute-done.11.got = f32[64,256]{1,0:T(8,128)S(1)} collective-permute-done((f32[64,256]{1,0:T(8,128)S(1)}, f32[64,256]{1,0:T(8,128)S(1)}, u32[]{:S(2)}, u32[]{:S(2)}) %collective-permute-start.11) | collective-permute-done | bytes 65568 | tf_op jit(solution)/shard_map/ppermute | solution.py:290
  58.3 1.7 %collective-permute-done.13.cross = f32[32,512]{1,0:T(8,128)S(1)} collective-permute-done((f32[32,512]{1,0:T(8,128)S(1)}, f32[32,512]{1,0:T(8,128)S(1)}, u32[]{:S(2)}, u32[]{:S(2)}) %collective-permute-start.13) | collective-permute-done | bytes 65568 | tf_op jit(solution)/shard_map/ppermute | solution.py:288
  59.9 0.9 %shard_map.52 = (bf16[3,256,512]{2,1,0:T(8,128)(2,1)}, f32[64,256]{1,0:T(8,128)}) custom-call(bf16[3,256,512]{2,1,0:T(8,128)(2,1)} %get-tuple-element.39.before, f32[64,256]{1,0:T(8,128)S(1)} %get-tuple-element.40.partial, bf16[384,256]{1,0:T(8,128)(2,1)S(1)} %get-tuple-element.38.tile.before.early, ...), custom_call_target="tpu_custom_call", output_to_operand_aliasing={{0}: (0, {})} | custom-call | tf_op jit(solution)/shard_map/pallas_call | solution.py:299
  (18 shorter events, 1.7 us)
Async XLA Ops:
  2.1 22.2 %collective-permute-start.2 = (bf16[224,4096]{1,0:T(8,128)(2,1)S(1)}, bf16[224,4096]{1,0:T(8,128)(2,1)S(1)}, u32[]{:S(2)}, u32[]{:S(2)}) collective-permute-start(bf16[224,4096]{1,0:T(8,128)(2,1)S(1)} %get-tuple-element.32), channel_id=1, source_target_pairs={{0,2},{2,6},{4,0},{6,4},{8,10},{10,14},{12,8},{14,12},{16,18},{18,... | collective-permute-start | bytes 5505032 | tf_op jit(solution)/shard_map/ppermute | solution.py:255
  9.3 29.1 %collective-permute-start.4 = (bf16[160,4096]{1,0:T(8,128)(2,1)S(1)}, bf16[160,4096]{1,0:T(8,128)(2,1)S(1)}, u32[]{:S(2)}, u32[]{:S(2)}) collective-permute-start(bf16[160,4096]{1,0:T(8,128)(2,1)S(1)} %get-tuple-element.35), channel_id=1, source_target_pairs={{0,2},{2,6},{4,0},{6,4},{8,10},{10,14},{12,8},{14,12},{16,18},{18,... | collective-permute-start | bytes 3932168 | tf_op jit(solution)/shard_map/ppermute | solution.py:255
  10.0 31.3 %collective-permute-start = (f32[256,512]{1,0:T(8,128)S(1)}, f32[256,512]{1,0:T(8,128)S(1)}, u32[]{:S(2)}, u32[]{:S(2)}) collective-permute-start(f32[256,512]{1,0:T(8,128)S(1)} %get-tuple-element.29), channel_id=1, source_target_pairs={{0,1},{1,0},{2,3},{3,2},{4,5},{5,4},{6,7},{7,6},{8,9},{9,8},{10,11... | collective-permute-start | bytes 1572872 | tf_op jit(solution)/shard_map/ppermute | solution.py:258
  11.2 32.8 %collective-permute-start.1 = (bf16[64,4096]{1,0:T(8,128)(2,1)S(1)}, bf16[64,4096]{1,0:T(8,128)(2,1)S(1)}, u32[]{:S(2)}, u32[]{:S(2)}) collective-permute-start(bf16[64,4096]{1,0:T(8,128)(2,1)S(1)} %get-tuple-element.30), channel_id=1, source_target_pairs={{0,2},{2,6},{4,0},{6,4},{8,10},{10,14},{12,8},{14,12},{16,18},{18,... | collective-permute-start | bytes 1572872 | tf_op jit(solution)/shard_map/ppermute | solution.py:255
  11.8 38.0 %collective-permute-start.6 = (bf16[64,4096]{1,0:T(8,128)(2,1)S(1)}, bf16[64,4096]{1,0:T(8,128)(2,1)S(1)}, u32[]{:S(2)}, u32[]{:S(2)}) collective-permute-start(bf16[64,4096]{1,0:T(8,128)(2,1)S(1)} %get-tuple-element.41), channel_id=1, source_target_pairs={{0,2},{2,6},{4,0},{6,4},{8,10},{10,14},{12,8},{14,12},{16,18},{18,... | collective-permute-start | bytes 1572872 | tf_op jit(solution)/shard_map/ppermute | solution.py:255
  25.8 20.9 %collective-permute-start.3 = (f32[336,256]{1,0:T(8,128)S(1)}, f32[336,256]{1,0:T(8,128)S(1)}, u32[]{:S(2)}, u32[]{:S(2)}) collective-permute-start(f32[336,256]{1,0:T(8,128)S(1)} %get-tuple-element.34), channel_id=1, source_target_pairs={{0,1},{1,0},{2,3},{3,2},{4,5},{5,4},{6,7},{7,6},{8,9},{9,8},{10,11... | collective-permute-start | bytes 1032200 | tf_op jit(solution)/shard_map/ppermute | solution.py:267
  40.0 6.8 %collective-permute-start.5 = (f32[240,256]{1,0:T(8,128)S(1)}, f32[240,256]{1,0:T(8,128)S(1)}, u32[]{:S(2)}, u32[]{:S(2)}) collective-permute-start(f32[240,256]{1,0:T(8,128)S(1)} %get-tuple-element.37), channel_id=1, source_target_pairs={{0,1},{1,0},{2,3},{3,2},{4,5},{5,4},{6,7},{7,6},{8,9},{9,8},{10,11... | collective-permute-start | bytes 737288 | tf_op jit(solution)/shard_map/ppermute | solution.py:267
  41.3 5.4 %copy-start = (bf16[512,64]{0,1:T(8,128)(2,1)S(1)}, bf16[512,64]{0,1:T(8,128)(2,1)}, u32[]{:S(2)}) copy-start(bf16[512,64]{0,1:T(8,128)(2,1)} %param.3) | copy-start | bytes 196612
  45.4 4.3 %collective-permute-start.7 = (f32[96,256]{1,0:T(8,128)S(1)}, f32[96,256]{1,0:T(8,128)S(1)}, u32[]{:S(2)}, u32[]{:S(2)}) collective-permute-start(f32[96,256]{1,0:T(8,128)S(1)} %get-tuple-element.42), channel_id=1, source_target_pairs={{0,1},{1,0},{2,3},{3,2},{4,5},{5,4},{6,7},{7,6},{8,9},{9,8},{10,11... | collective-permute-start | bytes 294920 | tf_op jit(solution)/shard_map/ppermute | solution.py:267
  46.9 13.1 %collective-permute-start.8 = (bf16[192,512]{1,0:T(8,128)(2,1)S(1)}, bf16[192,512]{1,0:T(8,128)(2,1)S(1)}, u32[]{:S(2)}, u32[]{:S(2)}) collective-permute-start(bf16[192,512]{1,0:T(8,128)(2,1)S(1)} %get-tuple-element.44), channel_id=1, source_target_pairs={{0,4},{2,0},{4,6},{6,2},{8,12},{10,8},{12,14},{14,10},{16,20},{18,... | collective-permute-start | bytes 589832 | tf_op jit(solution)/shard_map/ppermute | solution.py:278
  49.7 6.2 %collective-permute-start.9 = (bf16[64,512]{1,0:T(8,128)(2,1)S(1)}, bf16[64,512]{1,0:T(8,128)(2,1)S(1)}, u32[]{:S(2)}, u32[]{:S(2)}) collective-permute-start(bf16[64,512]{1,0:T(8,128)(2,1)S(1)} %bitcast.3), channel_id=1, source_target_pairs={{0,2},{2,6},{4,0},{6,4},{8,10},{10,14},{12,8},{14,12},{16,18},{18,... | collective-permute-start | bytes 196616 | tf_op jit(solution)/shard_map/ppermute | solution.py:269
  51.2 8.7 %collective-permute-start.12 = (f32[64,512]{1,0:T(8,128)S(1)}, f32[64,512]{1,0:T(8,128)S(1)}, u32[]{:S(2)}, u32[]{:S(2)}) collective-permute-start(f32[64,512]{1,0:T(8,128)S(1)} %get-tuple-element.48), channel_id=1, source_target_pairs={{0,4},{2,0},{4,6},{6,2},{8,12},{10,8},{12,14},{14,10},{16,20},{18,... | collective-permute-start | bytes 393224 | tf_op jit(solution)/shard_map/ppermute | solution.py:289
  53.6 3.3 %collective-permute-start.10 = (bf16[64,512]{1,0:T(8,128)(2,1)S(1)}, bf16[64,512]{1,0:T(8,128)(2,1)S(1)}, u32[]{:S(2)}, u32[]{:S(2)}) collective-permute-start(bf16[64,512]{1,0:T(8,128)(2,1)S(1)} %get-tuple-element.45), channel_id=1, source_target_pairs={{0,4},{2,0},{4,6},{6,2},{8,12},{10,8},{12,14},{14,10},{16,20},{18,... | collective-permute-start | bytes 196616 | tf_op jit(solution)/shard_map/ppermute | solution.py:279
  53.9 4.4 %collective-permute-start.11 = (f32[64,256]{1,0:T(8,128)S(1)}, f32[64,256]{1,0:T(8,128)S(1)}, u32[]{:S(2)}, u32[]{:S(2)}) collective-permute-start(f32[64,256]{1,0:T(8,128)S(1)} %get-tuple-element.47), channel_id=1, source_target_pairs={{0,1},{1,0},{2,3},{3,2},{4,5},{5,4},{6,7},{7,6},{8,9},{9,8},{10,11... | collective-permute-start | bytes 196616 | tf_op jit(solution)/shard_map/ppermute | solution.py:290
  55.9 4.1 %collective-permute-start.13 = (f32[32,512]{1,0:T(8,128)S(1)}, f32[32,512]{1,0:T(8,128)S(1)}, u32[]{:S(2)}, u32[]{:S(2)}) collective-permute-start(f32[32,512]{1,0:T(8,128)S(1)} %get-tuple-element.49), channel_id=1, source_target_pairs={{0,5},{1,4},{2,1},{3,0},{4,7},{5,6},{6,3},{7,2},{8,13},{9,12},{10,... | collective-permute-start | bytes 196616 | tf_op jit(solution)/shard_map/ppermute | solution.py:288

commit v4 on v3

--- a/solution.py
+++ b/solution.py
@@ -9,15 +9,16 @@
 
 AFTER = {0: 1, 1: 3, 3: 2, 2: 0}
 BEFORE = {after: before for before, after in AFTER.items()}
-SIXTEENTHS = (7, 5, 2, 2)
+SIXTEENTHS = (5, 4, 3, 2, 2)
 
 FIRST_VMEM = 50
+EARLY = 3
+FLOPS = 3000000000
 VMEM = pl.BlockSpec(memory_space=pltpu.VMEM)
 ANY = pl.BlockSpec(memory_space=pl.ANY)
-COST = pl.CostEstimate(flops=0, bytes_accessed=0, transcendentals=0)
-
-
-def call(kernel, out, in_specs, out_specs, scratch=(), aliases=None, vmem=16):
+
+
+def call(kernel, out, in_specs, out_specs, scratch=(), aliases=None, vmem=16, flops=0):
     return pl.pallas_call(
         kernel,
         out_shape=out,
@@ -25,7 +26,7 @@
         out_specs=out_specs,
         scratch_shapes=scratch,
         input_output_aliases=aliases or {},
-        cost_estimate=COST,
+        cost_estimate=pl.CostEstimate(flops=flops, bytes_accessed=0, transcendentals=0),
         compiler_params=pltpu.CompilerParams(vmem_limit_bytes=vmem * 2**20),
     )
 
@@ -38,6 +39,10 @@
 
 def multiply(left, right):
     return jnp.dot(left, right, preferred_element_type=jnp.float32)
+
+
+def contract_turned(left, right):
+    return contract(right, left).T
 
 
 def part_of(index, size):
@@ -102,30 +107,27 @@
 def pair_kernel(width, half, piece, grads, before, sent, kept):
     del before
     t = lax.axis_index("tgt")
-    sent[: 2 * width, :] = contract(piece[...], grads[part_of(1 - t, half), :])
-    kept[: 2 * width, :] = contract(piece[...], grads[part_of(t, half), :])
+    product = contract_turned if 2 * width <= 128 else contract
+    sent[: 2 * width, :] = product(piece[...], grads[part_of(1 - t, half), :])
+    kept[: 2 * width, :] = product(piece[...], grads[part_of(t, half), :])
     share(sent, kept, width)
 
 
-def last_pair_kernel(width, half, scale, piece, grads, third, got, before, sent, kept, near, cross, tile):
-    del before
-    t = lax.axis_index("tgt")
-    sent[...] = contract(piece[...], grads[part_of(1 - t, half), :])
-    kept[...] = contract(piece[...], grads[part_of(t, half), :])
+def last_pair_kernel(
+    width, half, scale, piece, grads, before, third, got, sent, kept, near, cross, tile, back
+):
+    t = lax.axis_index("tgt")
+    sent[...] = contract_turned(piece[...], grads[part_of(1 - t, half), :])
+    kept[...] = contract_turned(piece[...], grads[part_of(t, half), :])
     for to, index in ((near, t), (cross, 1 - t)):
-        to[:width, part_of(t, half)] = kept[part_of(index, width), :]
-        to[:width, part_of(1 - t, half)] = sent[part_of(index, width), :]
-    above = tile.shape[0] // 2
-    value = (third[...] + got[...]) * scale
-    tile[...] = value[: 2 * above].astype(jnp.bfloat16)
-    near[width:, part_of(1 - t, half)] = value[2 * above :]
-    rows = part_of(t, above)
-    near[width:, part_of(t, half)] = (third[rows, :] + got[rows, :]) * scale
-
-
-def finish_kernel(widths, half, scale, flat, before, *refs):
-    del before
-    *ins, tile, back, copy = refs
+        to[:, part_of(t, half)] = kept[part_of(index, width), :]
+        to[:, part_of(1 - t, half)] = sent[part_of(index, width), :]
+    finish_kernel([back.shape[0]], half, scale, before, third, got, tile, back)
+
+
+def finish_kernel(widths, half, scale, before, *refs):
+    del before
+    *ins, tile, back = refs
     t = lax.axis_index("tgt")
     at, total = 0, sum(widths)
     for i, width in enumerate(widths):
@@ -136,12 +138,22 @@
         back[at : at + width, part_of(1 - t, half)] = value[2 * width :]
         at += width
     back[:, part_of(t, half)] = tile[part_of(t, total), :]
-    copy[...] = flat[...]
+
+
+def early_finish_kernel(widths, half, scale, flat, before, *refs):
+    *ins, tile, back = refs
+    total = sum(widths)
+    finish_kernel(widths, half, scale, before, *ins, tile, back.at[pl.ds(0, total)])
+    back[total:, :] = flat[...]
+
+
+def meets_far():
+    place = lax.rem(lax.axis_index("blk"), 4)
+    return (place == 0) | (place == 3)
 
 
 def own_slot():
-    place = lax.rem(lax.axis_index("blk"), 4)
-    return jnp.where((place == 1) | (place == 2), 1, 2)
+    return jnp.where(meets_far(), 2, 1)
 
 
 def most_kernel(half, edge, self_tile, tile, flat, tiles, partial, turned, sems):
@@ -165,12 +177,12 @@
 
 
 def last_kernel(
-    half, edge, scale, before, partial, early, third, back_early, flat_before, flat_after,
-    kept, got, near, cross, tiles, influence, turned, far, late, total, sems,
+    half, edge, scale, before, got, cross, near, kept, partial, early, third, back_early,
+    back_third, flat_before, near_new, near_back, tiles, influence, turned, far, late, total, sems,
 ):
     del before
     slot = own_slot()
-    width = cross.shape[0]
+    width = near.shape[0]
     first, second = early.shape[0] // 2, third.shape[0] // 2
     done = first + second
     copies = []
@@ -179,25 +191,28 @@
         copies.append(pltpu.make_async_copy(source, target, sems.at[len(copies)]))
         copies[-1].start()
 
-    copy(back_early, tiles.at[3 - slot, pl.ds(0, first)])
-    far[first:done, :] = near[width:, :].astype(jnp.bfloat16)
-    far[done:, :] = ((near[:width, :] + cross[...]) * scale).astype(jnp.bfloat16)
+    copy(back_early.at[pl.ds(0, first)], tiles.at[3 - slot, pl.ds(0, first)])
+    far[first:done, :] = back_third[...]
+    summed = ((near[...] + cross[...]) * scale).astype(jnp.bfloat16)
+    far[done:, :] = jnp.where(meets_far(), near_back[...], summed)
     copy(
         far.at[pl.ds(first, second + width)], tiles.at[3 - slot, pl.ds(first, second + width)]
     )
     new = ((kept[...] + got[...]) * scale).astype(jnp.bfloat16)
+    new = jnp.where(meets_far(), new, near_new[...])
     value = partial[...]
     for h in range(2):
+        start = h * half
         late[h, : first - edge, :] = early[h * first + edge : (h + 1) * first, :]
         late[h, first - edge : done - edge, :] = third[h * second : (h + 1) * second, :]
         late[h, done - edge :, :] = new[h * width : (h + 1) * width]
         turned[h] = late[h].T
-        copy(turned.at[h], tiles.at[slot, :, pl.ds(h * half + edge, half - edge)])
+        copy(turned.at[h], tiles.at[slot, :, pl.ds(start + edge, half - edge)])
         value += multiply(
-            flat_before[:, h * half : h * half + edge], early[h * first : h * first + edge, :]
-        ) + multiply(flat_before[:, h * half + edge : (h + 1) * half], late[h])
-    far[:first, :] = back_early[...]
-    total[...] = value + contract(flat_after[...], far[...])
+            flat_before[:, start : start + edge], early[h * first : h * first + edge, :]
+        ) + multiply(flat_before[:, start + edge : start + half], late[h])
+    far[:first, :] = back_early[:first, :]
+    total[...] = value + contract(back_early[first:, :], far[...])
     copy(total, influence)
     for each in copies:
         each.wait()
@@ -212,7 +227,12 @@
     forward = [(b, b - b % 4 + AFTER[b % 4]) for b in range(blocks)]
     back = [(b, b - b % 4 + BEFORE[b % 4]) for b in range(blocks)]
     across = [(t, 1 - t) for t in range(groups)]
-    back_across = [(b * groups + t, c * groups + 1 - t) for b, c in back for t in range(groups)]
+    beside = [(b, b ^ 1) for b in range(blocks)]
+    back_across = [
+        (b * groups + t, c * groups + (1 - t if b % 4 in (0, 3) else t))
+        for b, c in back
+        for t in range(groups)
+    ]
 
     def f32(*shape):
         return jax.ShapeDtypeStruct(shape, jnp.float32)
@@ -222,7 +242,7 @@
 
     widths = [half * n // 16 for n in SIXTEENTHS]
     spans = [(sum(widths[:i]), w) for i, w in enumerate(widths)]
-    first = spans[2][0]
+    first = spans[-2][0]
     edge = half // 2
     flat = targets.T
 
@@ -267,27 +287,41 @@
         return [kept, lax.ppermute(sent, "tgt", across)]
 
     flat_before = lax.ppermute(flat, "blk", forward)
-    sums = pair(widths[0], got[0], mark) + pair(widths[1], got[1], mark)
-    third_sums = pair(widths[2], got[2], self_tile)
-    early, back_early, flat_after = call(
-        functools.partial(finish_kernel, widths[:2], half, scale),
-        [b16(2 * first, half), b16(first, rows), b16(columns, rows)],
-        [VMEM, ANY] + [VMEM] * 4,
-        [VMEM] * 3,
-    )(flat, third_sums[0], *sums)
+    near_sums = pair(widths[-1], lax.ppermute(pieces[-1], "blk", beside), mark)
+    near_new, near_back = call(
+        functools.partial(finish_kernel, widths[-1:], half, scale),
+        [b16(2 * widths[-1], half), b16(widths[-1], rows)],
+        [ANY] + [VMEM] * 2,
+        [VMEM] * 2,
+    )(mark, *near_sums)
+    near_back = lax.ppermute(near_back, "blk", beside)
+    sums = pair(widths[0], got[0], near_back)
+    for w, piece in zip(widths[1:-2], got[1:-2]):
+        sums += pair(w, piece, mark)
+    sums += pair(widths[-2], got[-2], self_tile)
+
+    some = widths[:EARLY]
+    early, back_early = call(
+        functools.partial(early_finish_kernel, some, half, scale),
+        [b16(2 * sum(some), half), b16(sum(some) + columns, rows)],
+        [VMEM, ANY] + [VMEM] * (2 * EARLY),
+        [VMEM] * 2,
+    )(flat, sums[-2], *sums[: 2 * EARLY])
     back_early = lax.ppermute(back_early, "blk", back)
-    flat_after = lax.ppermute(flat_after, "blk", back)
     *_, second, width = widths
-    sent, kept, near, cross, third = call(
+    sent, kept, near, cross, third, back_third = call(
         functools.partial(last_pair_kernel, width, half, scale),
         [f32(2 * width, half)] * 2
-        + [f32(width + second, rows), f32(width, rows), b16(2 * second, half)],
-        [VMEM] * 4 + [ANY],
-        [VMEM] * 5,
-    )(got[3], gradients, *third_sums, early)
+        + [f32(width, rows)] * 2
+        + [b16(2 * second, half), b16(second, rows)],
+        [VMEM] * 2 + [ANY] + [VMEM] * 2,
+        [VMEM] * 6,
+        flops=FLOPS,
+    )(got[-1], gradients, early, *sums[2 * EARLY :])
+    sent = lax.ppermute(sent, "tgt", across)
+    near = lax.ppermute(near, "blk", back)
     cross = lax.ppermute(cross, ("blk", "tgt"), back_across)
-    near = lax.ppermute(near, "blk", back)
-    sent = lax.ppermute(sent, "tgt", across)
+    back_third = lax.ppermute(back_third, "blk", back)
 
     tiles, partial = call(
         functools.partial(most_kernel, half, edge),
@@ -299,7 +333,7 @@
     tiles, influence = call(
         functools.partial(last_kernel, half, edge, scale),
         [b16(3, half, rows), f32(columns, half)],
-        [ANY] + [VMEM] * 10,
+        [ANY] + [VMEM] * 12,
         [ANY] * 2,
         [
             pltpu.VMEM((2, half, half - edge), jnp.bfloat16),
@@ -309,8 +343,10 @@
             pltpu.SemaphoreType.DMA((5,)),
         ],
         {0: 0},
-    )(tiles, partial, early, third, back_early, flat_before, flat_after,
-      kept, sent, near, cross)
+    )(
+        tiles, sent, cross, near, kept, partial, early, third, back_early, back_third,
+        flat_before, near_new, near_back,
+    )
     return tiles, influence.T
 
 

time: 61 us -> 59.9 us (0.982)
  waiting for transfers between devices: 29.2 us -> 23.7 us
  Pallas kernels: 14.3 us -> 16.6 us
  starting transfers between devices: 16.6 us -> 18.6 us
    ppermute x4 -> x5, waiting for transfers between devices: 26.2 us -> 15.1 us  [per_device(): got = [lax.ppermute(piece, 'blk', forward) for piece in (piece, *pieces)]]
    ppermute x1 -> x3, waiting for transfers between devices: 0.01 us -> 5.54 us  [the longest x1 2.62 us: per_device(): near_sums = pair(widths[-1], lax.ppermute(pieces[-1], 'blk', beside), mark)]
    ppermute x1, starting transfers between devices: 0.08 us -> 3.46 us  [per_device(): flat_before = lax.ppermute(flat, 'blk', forward)]
    ppermute x3 -> x5, waiting for transfers between devices: 0.01 us -> 3.08 us  [pair(): return [kept, lax.ppermute(sent, 'tgt', across)]]
    ppermute x1, starting transfers between devices: 2.81 us -> 0.02 us  [per_device(): back_early = lax.ppermute(back_early, 'blk', back)]
    pallas_call x3 -> x5, Pallas kernels: 4.42 us -> 6.88 us  [pair(): call(functools.partial(pair_kernel, width, half), [f32(3 * width, half)]...]
    ppermute x1, starting transfers between devices: 0.26 us -> 2.6 us  [per_device(): cross = lax.ppermute(cross, ('blk', 'tgt'), back_across)]
    ppermute x1, starting transfers between devices: 2.38 us -> 0.23 us  [per_device(): near = lax.ppermute(near, 'blk', back)]
  transfers between devices with their start and end apart: 14 -> 19, of which waited for: 5 -> 8; matrix products, arithmetic and copies ran while one was open for 0% -> 0% of each run, Pallas kernels for 20% -> 24%
where the time goes in v4:
time: 59.9 us; the launch traced here: 59.7 us
  waiting for transfers between devices  23.7 us (40%)
  starting transfers between devices  18.6 us (31%)
  Pallas kernels  16.6 us (28%)
  between operations  0.79 us (1%)
    ppermute x5, waiting for transfers between devices, per_device(): got = [lax.ppermute(piece, 'blk', forward) for piece in (piece, *pieces)]  15.1 us
    pallas_call x5, Pallas kernels, pair(): call(functools.partial(pair_kernel, width, half), [f32(3 * width, half)]...  6.88 us
    ppermute x5, starting transfers between devices, pair(): return [kept, lax.ppermute(sent, 'tgt', across)]  5.38 us
    ppermute x5, starting transfers between devices, per_device(): got = [lax.ppermute(piece, 'blk', forward) for piece in (piece, *pieces)]  3.75 us
    ppermute x1, starting transfers between devices, per_device(): flat_before = lax.ppermute(flat, 'blk', forward)  3.46 us
    ppermute x5, waiting for transfers between devices, pair(): return [kept, lax.ppermute(sent, 'tgt', across)]  3.08 us
    ppermute x1, waiting for transfers between devices, per_device(): near_sums = pair(widths[-1], lax.ppermute(pieces[-1], 'blk', beside), mark)  2.62 us
    ppermute x1, starting transfers between devices, per_device(): cross = lax.ppermute(cross, ('blk', 'tgt'), back_across)  2.6 us
  transfers between devices with their start and end apart: 19, of which 8 were waited for; matrix products, arithmetic and copies ran while one was open for 0% of the time, Pallas kernels for 24%

profile of v4, /device:TPU:1, one launch (start us, length us, event | category | flops | bytes accessed | tf_op | source)
XLA Modules:
  0.0 59.7 jit_solution(7576671763265129323)
XLA Ops:
  0.6 1.3 %shard_map.41 = (bf16[160,4096]{1,0:T(8,128)(2,1)S(1)}, f32[8,128]{1,0:T(8,128)S(1)}) custom-call(bf16[512,4096]{1,0:T(8,128)(2,1)} %grads.3), custom_call_target="tpu_custom_call" | custom-call | tf_op jit(solution)/shard_map/pallas_call | solution.py:249
  1.9 2.1 %collective-permute-start.2 = (bf16[160,4096]{1,0:T(8,128)(2,1)S(1)}, bf16[160,4096]{1,0:T(8,128)(2,1)S(1)}, u32[]{:S(2)}, u32[]{:S(2)}) collective-permute-start(bf16[160,4096]{1,0:T(8,128)(2,1)S(1)} %get-tuple-element.39), channel_id=1, source_target_pairs={{0,2},{2,6},{4,0},{6,4},{8,10},{10,14},{12,8},{14,12},{16,18},{18,... | collective-permute-start | bytes 3932168 | tf_op jit(solution)/shard_map/ppermute | solution.py:275
  4.0 2.2 %shard_map.42.grads = bf16[512,4096]{1,0:T(8,128)(2,1)S(1)} custom-call(bf16[512,4096]{1,0:T(8,128)(2,1)} %grads.3, f32[8,128]{1,0:T(8,128)S(1)} %get-tuple-element.34.before), custom_call_target="tpu_custom_call" | custom-call | tf_op jit(solution)/shard_map/pallas_call | solution.py:257
  6.2 2.4 %shard_map.43 = (f32[256,512]{1,0:T(8,128)S(1)}, f32[256,512]{1,0:T(8,128)S(1)}) custom-call(bf16[512,4096]{1,0:T(8,128)(2,1)S(1)} %shard_map.42.grads, f32[8,128]{1,0:T(8,128)S(1)} %get-tuple-element.34.before), custom_call_target="tpu_custom_call" | custom-call | tf_op jit(solution)/shard_map/pallas_call | solution.py:265
  10.0 2.6 %collective-permute-done.3.piece = bf16[64,4096]{1,0:T(8,128)(2,1)S(1)} collective-permute-done((bf16[64,4096]{1,0:T(8,128)(2,1)S(1)}, bf16[64,4096]{1,0:T(8,128)(2,1)S(1)}, u32[]{:S(2)}, u32[]{:S(2)}) %collective-permute-start.3) | collective-permute-done | bytes 524320 | tf_op jit(solution)/shard_map/ppermute | solution.py:290
  12.6 1.3 %shard_map.47 = (f32[96,256]{1,0:T(8,128)S(1)}, f32[96,256]{1,0:T(8,128)S(1)}) custom-call(bf16[64,4096]{1,0:T(8,128)(2,1)S(1)} %collective-permute-done.3.piece, bf16[512,4096]{1,0:T(8,128)(2,1)S(1)} %shard_map.42.grads, f32[8,128]{1,0:T(8,128)S(1)} %get-tuple-element.34.before), custom_call_target="tpu_custom_call" | custom-call | tf_op jit(solution)/shard_map/pallas_call | solution.py:281
  13.9 1.3 %collective-permute-start.4 = (f32[96,256]{1,0:T(8,128)S(1)}, f32[96,256]{1,0:T(8,128)S(1)}, u32[]{:S(2)}, u32[]{:S(2)}) collective-permute-start(f32[96,256]{1,0:T(8,128)S(1)} %get-tuple-element.42), channel_id=1, source_target_pairs={{0,1},{1,0},{2,3},{3,2},{4,5},{5,4},{6,7},{7,6},{8,9},{9,8},{10,11... | collective-permute-start | bytes 294920 | tf_op jit(solution)/shard_map/ppermute | solution.py:287
  15.5 2.8 %collective-permute-done.4.refs_1_ = f32[96,256]{1,0:T(8,128)S(1)} collective-permute-done((f32[96,256]{1,0:T(8,128)S(1)}, f32[96,256]{1,0:T(8,128)S(1)}, u32[]{:S(2)}, u32[]{:S(2)}) %collective-permute-start.4) | collective-permute-done | bytes 98336 | tf_op jit(solution)/shard_map/ppermute | solution.py:287
  18.3 1.6 %collective-permute-start.5 = (bf16[32,512]{1,0:T(8,128)(2,1)S(1)}, bf16[32,512]{1,0:T(8,128)(2,1)S(1)}, u32[]{:S(2)}, u32[]{:S(2)}) collective-permute-start(bf16[32,512]{1,0:T(8,128)(2,1)S(1)} %get-tuple-element.43), channel_id=1, source_target_pairs={{0,2},{2,0},{4,6},{6,4},{8,10},{10,8},{12,14},{14,12},{16,18},{18,... | collective-permute-start | bytes 98312 | tf_op jit(solution)/shard_map/ppermute | solution.py:297
  21.6 1.6 %shard_map.49 = (f32[240,256]{1,0:T(8,128)S(1)}, f32[240,256]{1,0:T(8,128)S(1)}) custom-call(bf16[160,4096]{1,0:T(8,128)(2,1)S(1)} %collective-permute-done.2.piece, bf16[512,4096]{1,0:T(8,128)(2,1)S(1)} %shard_map.42.grads, bf16[32,512]{1,0:T(8,128)(2,1)S(1)} %collective-permute-done.5.before.near_back), custom_call_target="tpu_custom_call" | custom-call | tf_op jit(solution)/shard_map/pallas_call | solution.py:281
  23.2 6.6 %collective-permute-done.7.piece = bf16[128,4096]{1,0:T(8,128)(2,1)S(1)} collective-permute-done((bf16[128,4096]{1,0:T(8,128)(2,1)S(1)}, bf16[128,4096]{1,0:T(8,128)(2,1)S(1)}, u32[]{:S(2)}, u32[]{:S(2)}) %collective-permute-start.7) | collective-permute-done | bytes 1048608 | tf_op jit(solution)/shard_map/ppermute | solution.py:275
  29.8 1.2 %collective-permute-start.6 = (f32[240,256]{1,0:T(8,128)S(1)}, f32[240,256]{1,0:T(8,128)S(1)}, u32[]{:S(2)}, u32[]{:S(2)}) collective-permute-start(f32[240,256]{1,0:T(8,128)S(1)} %get-tuple-element.45), channel_id=1, source_target_pairs={{0,1},{1,0},{2,3},{3,2},{4,5},{5,4},{6,7},{7,6},{8,9},{9,8},{10,11... | collective-permute-start | bytes 737288 | tf_op jit(solution)/shard_map/ppermute | solution.py:287
  31.0 1.4 %shard_map.50 = (f32[192,256]{1,0:T(8,128)S(1)}, f32[192,256]{1,0:T(8,128)S(1)}) custom-call(bf16[128,4096]{1,0:T(8,128)(2,1)S(1)} %collective-permute-done.7.piece, bf16[512,4096]{1,0:T(8,128)(2,1)S(1)} %shard_map.42.grads, f32[8,128]{1,0:T(8,128)S(1)} %get-tuple-element.34.before), custom_call_target="tpu_custom_call" | custom-call | tf_op jit(solution)/shard_map/pallas_call | solution.py:281
  32.4 5.8 %collective-permute-done.9.piece = bf16[96,4096]{1,0:T(8,128)(2,1)S(1)} collective-permute-done((bf16[96,4096]{1,0:T(8,128)(2,1)S(1)}, bf16[96,4096]{1,0:T(8,128)(2,1)S(1)}, u32[]{:S(2)}, u32[]{:S(2)}) %collective-permute-start.9) | collective-permute-done | bytes 786464 | tf_op jit(solution)/shard_map/ppermute | solution.py:275
  38.2 1.2 %collective-permute-start.8 = (f32[192,256]{1,0:T(8,128)S(1)}, f32[192,256]{1,0:T(8,128)S(1)}, u32[]{:S(2)}, u32[]{:S(2)}) collective-permute-start(f32[192,256]{1,0:T(8,128)S(1)} %get-tuple-element.48), channel_id=1, source_target_pairs={{0,1},{1,0},{2,3},{3,2},{4,5},{5,4},{6,7},{7,6},{8,9},{9,8},{10,11... | collective-permute-start | bytes 589832 | tf_op jit(solution)/shard_map/ppermute | solution.py:287
  39.5 1.3 %shard_map.51 = (f32[144,256]{1,0:T(8,128)S(1)}, f32[144,256]{1,0:T(8,128)S(1)}) custom-call(bf16[96,4096]{1,0:T(8,128)(2,1)S(1)} %collective-permute-done.9.piece, bf16[512,4096]{1,0:T(8,128)(2,1)S(1)} %shard_map.42.grads, f32[8,128]{1,0:T(8,128)S(1)} %get-tuple-element.34.before), custom_call_target="tpu_custom_call" | custom-call | tf_op jit(solution)/shard_map/pallas_call | solution.py:281
  41.2 2.7 %collective-permute-done.1.piece = bf16[64,4096]{1,0:T(8,128)(2,1)S(1)} collective-permute-done((bf16[64,4096]{1,0:T(8,128)(2,1)S(1)}, bf16[64,4096]{1,0:T(8,128)(2,1)S(1)}, u32[]{:S(2)}, u32[]{:S(2)}) %collective-permute-start.1) | collective-permute-done | bytes 524320 | tf_op jit(solution)/shard_map/ppermute | solution.py:275
  43.8 1.3 %shard_map.46 = (f32[96,256]{1,0:T(8,128)S(1)}, f32[96,256]{1,0:T(8,128)S(1)}) custom-call(bf16[64,4096]{1,0:T(8,128)(2,1)S(1)} %collective-permute-done.1.piece, bf16[512,4096]{1,0:T(8,128)(2,1)S(1)} %shard_map.42.grads, bf16[256,512]{1,0:T(8,128)(2,1)S(1)} %shard_map.44.before.self_tile), custom_call_target="tpu_custom_call" | custom-call | tf_op jit(solution)/shard_map/pallas_call | solution.py:281
  45.1 1.3 %collective-permute-start.12 = (f32[96,256]{1,0:T(8,128)S(1)}, f32[96,256]{1,0:T(8,128)S(1)}, u32[]{:S(2)}, u32[]{:S(2)}) collective-permute-start(f32[96,256]{1,0:T(8,128)S(1)} %get-tuple-element.54), channel_id=1, source_target_pairs={{0,1},{1,0},{2,3},{3,2},{4,5},{5,4},{6,7},{7,6},{8,9},{9,8},{10,11... | collective-permute-start | bytes 294920 | tf_op jit(solution)/shard_map/ppermute | solution.py:287
  46.7 3.5 %collective-permute-start.18 = (bf16[64,512]{1,0:T(8,128)(2,1)S(1)}, bf16[64,512]{1,0:T(8,128)(2,1)S(1)}, u32[]{:S(2)}, u32[]{:S(2)}) collective-permute-start(bf16[64,512]{1,0:T(8,128)(2,1)S(1)} %bitcast.2), channel_id=1, source_target_pairs={{0,2},{2,6},{4,0},{6,4},{8,10},{10,14},{12,8},{14,12},{16,18},{18,... | collective-permute-start | bytes 196616 | tf_op jit(solution)/shard_map/ppermute | solution.py:289
  50.4 1.3 %shard_map.54 = (f32[64,256]{1,0:T(8,128)S(1)}, f32[64,256]{1,0:T(8,128)S(1)}, f32[32,512]{1,0:T(8,128)S(1)}, f32[32,512]{1,0:T(8,128)S(1)}, bf16[64,256]{1,0:T(8,128)(2,1)S(1)}, /*index=5*/bf16[32,512]{1,0:T(8,128)(2,1)S(1)}) custom-call(bf16[64,4096]{1,0:T(8,128)(2,1)S(1)} %collective-permute-done.11.piece, bf16[512,4096]{1,0:T(8,128)(2,1)S(1)} %shard_map.42.grads, ...), custom_call_target="tpu_custom_call" | custom-call | flops 3000000000 | tf_op jit(solution)/shard_map/pallas_call | solution.py:312
  51.7 1.0 %collective-permute-start.13 = (f32[64,256]{1,0:T(8,128)S(1)}, f32[64,256]{1,0:T(8,128)S(1)}, u32[]{:S(2)}, u32[]{:S(2)}) collective-permute-start(f32[64,256]{1,0:T(8,128)S(1)} %get-tuple-element.55), channel_id=1, source_target_pairs={{0,1},{1,0},{2,3},{3,2},{4,5},{5,4},{6,7},{7,6},{8,9},{9,8},{10,11... | collective-permute-start | bytes 196616 | tf_op jit(solution)/shard_map/ppermute | solution.py:321
  52.7 2.6 %collective-permute-start.14 = (f32[32,512]{1,0:T(8,128)S(1)}, f32[32,512]{1,0:T(8,128)S(1)}, u32[]{:S(2)}, u32[]{:S(2)}) collective-permute-start(f32[32,512]{1,0:T(8,128)S(1)} %get-tuple-element.56), channel_id=1, source_target_pairs={{0,5},{1,4},{2,0},{3,1},{4,6},{5,7},{6,3},{7,2},{8,13},{9,12},{10,... | collective-permute-start | bytes 196616 | tf_op jit(solution)/shard_map/ppermute | solution.py:323
  56.7 2.1 %collective-permute-done.17.back_third = bf16[32,512]{1,0:T(8,128)(2,1)S(1)} collective-permute-done((bf16[32,512]{1,0:T(8,128)(2,1)S(1)}, bf16[32,512]{1,0:T(8,128)(2,1)S(1)}, u32[]{:S(2)}, u32[]{:S(2)}) %collective-permute-start.17) | collective-permute-done | bytes 32800 | tf_op jit(solution)/shard_map/ppermute | solution.py:324
  (31 shorter events, 6.5 us)
Async XLA Ops:
  1.9 19.3 %collective-permute-start.2 = (bf16[160,4096]{1,0:T(8,128)(2,1)S(1)}, bf16[160,4096]{1,0:T(8,128)(2,1)S(1)}, u32[]{:S(2)}, u32[]{:S(2)}) collective-permute-start(bf16[160,4096]{1,0:T(8,128)(2,1)S(1)} %get-tuple-element.39), channel_id=1, source_target_pairs={{0,2},{2,6},{4,0},{6,4},{8,10},{10,14},{12,8},{14,12},{16,18},{18,... | collective-permute-start | bytes 3932168 | tf_op jit(solution)/shard_map/ppermute | solution.py:275
  9.2 20.6 %collective-permute-start.7 = (bf16[128,4096]{1,0:T(8,128)(2,1)S(1)}, bf16[128,4096]{1,0:T(8,128)(2,1)S(1)}, u32[]{:S(2)}, u32[]{:S(2)}) collective-permute-start(bf16[128,4096]{1,0:T(8,128)(2,1)S(1)} %get-tuple-element.46), channel_id=1, source_target_pairs={{0,2},{2,6},{4,0},{6,4},{8,10},{10,14},{12,8},{14,12},{16,18},{18,... | collective-permute-start | bytes 3145736 | tf_op jit(solution)/shard_map/ppermute | solution.py:275
  9.9 2.7 %collective-permute-start.3 = (bf16[64,4096]{1,0:T(8,128)(2,1)S(1)}, bf16[64,4096]{1,0:T(8,128)(2,1)S(1)}, u32[]{:S(2)}, u32[]{:S(2)}) collective-permute-start(bf16[64,4096]{1,0:T(8,128)(2,1)S(1)} %get-tuple-element.40), channel_id=1, source_target_pairs={{0,2},{2,0},{4,6},{6,4},{8,10},{10,8},{12,14},{14,12},{16,18},{18,... | collective-permute-start | bytes 1572872 | tf_op jit(solution)/shard_map/ppermute | solution.py:290
  9.9 28.3 %collective-permute-start.9 = (bf16[96,4096]{1,0:T(8,128)(2,1)S(1)}, bf16[96,4096]{1,0:T(8,128)(2,1)S(1)}, u32[]{:S(2)}, u32[]{:S(2)}) collective-permute-start(bf16[96,4096]{1,0:T(8,128)(2,1)S(1)} %get-tuple-element.49), channel_id=1, source_target_pairs={{0,2},{2,6},{4,0},{6,4},{8,10},{10,14},{12,8},{14,12},{16,18},{18,... | collective-permute-start | bytes 2359304 | tf_op jit(solution)/shard_map/ppermute | solution.py:275
  13.9 4.3 %collective-permute-start.4 = (f32[96,256]{1,0:T(8,128)S(1)}, f32[96,256]{1,0:T(8,128)S(1)}, u32[]{:S(2)}, u32[]{:S(2)}) collective-permute-start(f32[96,256]{1,0:T(8,128)S(1)} %get-tuple-element.42), channel_id=1, source_target_pairs={{0,1},{1,0},{2,3},{3,2},{4,5},{5,4},{6,7},{7,6},{8,9},{9,8},{10,11... | collective-permute-start | bytes 294920 | tf_op jit(solution)/shard_map/ppermute | solution.py:287
  15.2 25.6 %collective-permute-start = (f32[256,512]{1,0:T(8,128)S(1)}, f32[256,512]{1,0:T(8,128)S(1)}, u32[]{:S(2)}, u32[]{:S(2)}) collective-permute-start(f32[256,512]{1,0:T(8,128)S(1)} %get-tuple-element.36), channel_id=1, source_target_pairs={{0,1},{1,0},{2,3},{3,2},{4,5},{5,4},{6,7},{7,6},{8,9},{9,8},{10,11... | collective-permute-start | bytes 1572872 | tf_op jit(solution)/shard_map/ppermute | solution.py:278
  18.3 2.4 %collective-permute-start.5 = (bf16[32,512]{1,0:T(8,128)(2,1)S(1)}, bf16[32,512]{1,0:T(8,128)(2,1)S(1)}, u32[]{:S(2)}, u32[]{:S(2)}) collective-permute-start(bf16[32,512]{1,0:T(8,128)(2,1)S(1)} %get-tuple-element.43), channel_id=1, source_target_pairs={{0,2},{2,0},{4,6},{6,4},{8,10},{10,8},{12,14},{14,12},{16,18},{18,... | collective-permute-start | bytes 98312 | tf_op jit(solution)/shard_map/ppermute | solution.py:297
  20.7 23.1 %collective-permute-start.1 = (bf16[64,4096]{1,0:T(8,128)(2,1)S(1)}, bf16[64,4096]{1,0:T(8,128)(2,1)S(1)}, u32[]{:S(2)}, u32[]{:S(2)}) collective-permute-start(bf16[64,4096]{1,0:T(8,128)(2,1)S(1)} %get-tuple-element.37), channel_id=1, source_target_pairs={{0,2},{2,6},{4,0},{6,4},{8,10},{10,14},{12,8},{14,12},{16,18},{18,... | collective-permute-start | bytes 1572872 | tf_op jit(solution)/shard_map/ppermute | solution.py:275
  21.3 29.1 %collective-permute-start.11 = (bf16[64,4096]{1,0:T(8,128)(2,1)S(1)}, bf16[64,4096]{1,0:T(8,128)(2,1)S(1)}, u32[]{:S(2)}, u32[]{:S(2)}) collective-permute-start(bf16[64,4096]{1,0:T(8,128)(2,1)S(1)} %get-tuple-element.40), channel_id=1, source_target_pairs={{0,2},{2,6},{4,0},{6,4},{8,10},{10,14},{12,8},{14,12},{16,18},{18,... | collective-permute-start | bytes 1572872 | tf_op jit(solution)/shard_map/ppermute | solution.py:275
  29.8 20.4 %collective-permute-start.6 = (f32[240,256]{1,0:T(8,128)S(1)}, f32[240,256]{1,0:T(8,128)S(1)}, u32[]{:S(2)}, u32[]{:S(2)}) collective-permute-start(f32[240,256]{1,0:T(8,128)S(1)} %get-tuple-element.45), channel_id=1, source_target_pairs={{0,1},{1,0},{2,3},{3,2},{4,5},{5,4},{6,7},{7,6},{8,9},{9,8},{10,11... | collective-permute-start | bytes 737288 | tf_op jit(solution)/shard_map/ppermute | solution.py:287
  38.2 12.0 %collective-permute-start.8 = (f32[192,256]{1,0:T(8,128)S(1)}, f32[192,256]{1,0:T(8,128)S(1)}, u32[]{:S(2)}, u32[]{:S(2)}) collective-permute-start(f32[192,256]{1,0:T(8,128)S(1)} %get-tuple-element.48), channel_id=1, source_target_pairs={{0,1},{1,0},{2,3},{3,2},{4,5},{5,4},{6,7},{7,6},{8,9},{9,8},{10,11... | collective-permute-start | bytes 589832 | tf_op jit(solution)/shard_map/ppermute | solution.py:287
  40.8 6.0 %copy-start = (bf16[512,64]{0,1:T(8,128)(2,1)S(1)}, bf16[512,64]{0,1:T(8,128)(2,1)}, u32[]{:S(2)}) copy-start(bf16[512,64]{0,1:T(8,128)(2,1)} %param.3) | copy-start | bytes 196612
  40.8 5.9 %collective-permute-start.10 = (f32[144,256]{1,0:T(8,128)S(1)}, f32[144,256]{1,0:T(8,128)S(1)}, u32[]{:S(2)}, u32[]{:S(2)}) collective-permute-start(f32[144,256]{1,0:T(8,128)S(1)} %get-tuple-element.51), channel_id=1, source_target_pairs={{0,1},{1,0},{2,3},{3,2},{4,5},{5,4},{6,7},{7,6},{8,9},{9,8},{10,11... | collective-permute-start | bytes 442376 | tf_op jit(solution)/shard_map/ppermute | solution.py:287
  45.1 5.2 %collective-permute-start.12 = (f32[96,256]{1,0:T(8,128)S(1)}, f32[96,256]{1,0:T(8,128)S(1)}, u32[]{:S(2)}, u32[]{:S(2)}) collective-permute-start(f32[96,256]{1,0:T(8,128)S(1)} %get-tuple-element.54), channel_id=1, source_target_pairs={{0,1},{1,0},{2,3},{3,2},{4,5},{5,4},{6,7},{7,6},{8,9},{9,8},{10,11... | collective-permute-start | bytes 294920 | tf_op jit(solution)/shard_map/ppermute | solution.py:287
  46.7 8.8 %collective-permute-start.18 = (bf16[64,512]{1,0:T(8,128)(2,1)S(1)}, bf16[64,512]{1,0:T(8,128)(2,1)S(1)}, u32[]{:S(2)}, u32[]{:S(2)}) collective-permute-start(bf16[64,512]{1,0:T(8,128)(2,1)S(1)} %bitcast.2), channel_id=1, source_target_pairs={{0,2},{2,6},{4,0},{6,4},{8,10},{10,14},{12,8},{14,12},{16,18},{18,... | collective-permute-start | bytes 196616 | tf_op jit(solution)/shard_map/ppermute | solution.py:289
  50.3 8.4 %collective-permute-start.16 = (bf16[256,512]{1,0:T(8,128)(2,1)S(1)}, bf16[256,512]{1,0:T(8,128)(2,1)S(1)}, u32[]{:S(2)}, u32[]{:S(2)}) collective-permute-start(bf16[256,512]{1,0:T(8,128)(2,1)S(1)} %get-tuple-element.61), channel_id=1, source_target_pairs={{0,4},{2,0},{4,6},{6,2},{8,12},{10,8},{12,14},{14,10},{16,20},{18,... | collective-permute-start | bytes 786440 | tf_op jit(solution)/shard_map/ppermute | solution.py:310
  51.7 7.0 %collective-permute-start.13 = (f32[64,256]{1,0:T(8,128)S(1)}, f32[64,256]{1,0:T(8,128)S(1)}, u32[]{:S(2)}, u32[]{:S(2)}) collective-permute-start(f32[64,256]{1,0:T(8,128)S(1)} %get-tuple-element.55), channel_id=1, source_target_pairs={{0,1},{1,0},{2,3},{3,2},{4,5},{5,4},{6,7},{7,6},{8,9},{9,8},{10,11... | collective-permute-start | bytes 196616 | tf_op jit(solution)/shard_map/ppermute | solution.py:321
  52.7 6.1 %collective-permute-start.14 = (f32[32,512]{1,0:T(8,128)S(1)}, f32[32,512]{1,0:T(8,128)S(1)}, u32[]{:S(2)}, u32[]{:S(2)}) collective-permute-start(f32[32,512]{1,0:T(8,128)S(1)} %get-tuple-element.56), channel_id=1, source_target_pairs={{0,5},{1,4},{2,0},{3,1},{4,6},{5,7},{6,3},{7,2},{8,13},{9,12},{10,... | collective-permute-start | bytes 196616 | tf_op jit(solution)/shard_map/ppermute | solution.py:323
  55.3 3.5 %collective-permute-start.15 = (f32[32,512]{1,0:T(8,128)S(1)}, f32[32,512]{1,0:T(8,128)S(1)}, u32[]{:S(2)}, u32[]{:S(2)}) collective-permute-start(f32[32,512]{1,0:T(8,128)S(1)} %get-tuple-element.57), channel_id=1, source_target_pairs={{0,4},{2,0},{4,6},{6,2},{8,12},{10,8},{12,14},{14,10},{16,20},{18,... | collective-permute-start | bytes 196616 | tf_op jit(solution)/shard_map/ppermute | solution.py:322
  55.5 3.2 %collective-permute-start.17 = (bf16[32,512]{1,0:T(8,128)(2,1)S(1)}, bf16[32,512]{1,0:T(8,128)(2,1)S(1)}, u32[]{:S(2)}, u32[]{:S(2)}) collective-permute-start(bf16[32,512]{1,0:T(8,128)(2,1)S(1)} %get-tuple-element.62), channel_id=1, source_target_pairs={{0,4},{2,0},{4,6},{6,2},{8,12},{10,8},{12,14},{14,10},{16,20},{18,... | collective-permute-start | bytes 98312 | tf_op jit(solution)/shard_map/ppermute | solution.py:324

commit v5 on v4

--- a/solution.py
+++ b/solution.py
@@ -13,7 +13,7 @@
 
 FIRST_VMEM = 50
 EARLY = 3
-FLOPS = 3000000000
+FLOPS = 1500000000
 VMEM = pl.BlockSpec(memory_space=pltpu.VMEM)
 ANY = pl.BlockSpec(memory_space=pl.ANY)
 
@@ -116,12 +116,15 @@
 def last_pair_kernel(
     width, half, scale, piece, grads, before, third, got, sent, kept, near, cross, tile, back
 ):
-    t = lax.axis_index("tgt")
-    sent[...] = contract_turned(piece[...], grads[part_of(1 - t, half), :])
-    kept[...] = contract_turned(piece[...], grads[part_of(t, half), :])
-    for to, index in ((near, t), (cross, 1 - t)):
-        to[:, part_of(t, half)] = kept[part_of(index, width), :]
-        to[:, part_of(1 - t, half)] = sent[part_of(index, width), :]
+    @pl.when(meets_far())
+    def _():
+        t = lax.axis_index("tgt")
+        sent[...] = contract_turned(piece[...], grads[part_of(1 - t, half), :])
+        kept[...] = contract_turned(piece[...], grads[part_of(t, half), :])
+        for to, index in ((near, t), (cross, 1 - t)):
+            to[:, part_of(t, half)] = kept[part_of(index, width), :]
+            to[:, part_of(1 - t, half)] = sent[part_of(index, width), :]
+
     finish_kernel([back.shape[0]], half, scale, before, third, got, tile, back)
 
 
@@ -177,7 +180,7 @@
 
 
 def last_kernel(
-    half, edge, scale, before, got, cross, near, kept, partial, early, third, back_early,
+    half, edge, scale, before, cross, got, near, kept, partial, early, third, back_early,
     back_third, flat_before, near_new, near_back, tiles, influence, turned, far, late, total, sems,
 ):
     del before
@@ -344,7 +347,7 @@
         ],
         {0: 0},
     )(
-        tiles, sent, cross, near, kept, partial, early, third, back_early, back_third,
+        tiles, cross, sent, near, kept, partial, early, third, back_early, back_third,
         flat_before, near_new, near_back,
     )
     return tiles, influence.T

time: 59.9 us -> 59.6 us (level)
  starting transfers between devices: 18.6 us -> 20.1 us
  Pallas kernels: 16.6 us -> 15.3 us
    ppermute x1, starting transfers between devices: 0.02 us -> 3 us  [per_device(): back_early = lax.ppermute(back_early, 'blk', back)]
    ppermute x1, starting transfers between devices: 3.46 us -> 0.5 us  [per_device(): flat_before = lax.ppermute(flat, 'blk', forward)]
    pallas_call x1, Pallas kernels: 1.32 us -> 0.02 us  [per_device(): call(functools.partial(last_pair_kernel, width, half, scale), [f32(2 * wi...]
    ppermute x1, starting transfers between devices: 0.97 us -> 1.76 us  [per_device(): sent = lax.ppermute(sent, 'tgt', across)]
  transfers between devices with their start and end apart: 19 -> 19, of which waited for: 8 -> 8; matrix products, arithmetic and copies ran while one was open for 0% -> 0% of each run, Pallas kernels for 24% -> 22%
where the time goes in v5:
time: 59.6 us; the launch traced here: 59.5 us
  waiting for transfers between devices  23.4 us (39%)
  starting transfers between devices  20.1 us (34%)
  Pallas kernels  15.3 us (26%)
  between operations  0.77 us (1%)
    ppermute x5, waiting for transfers between devices, per_device(): got = [lax.ppermute(piece, 'blk', forward) for piece in (piece, *pieces)]  15.1 us
    pallas_call x5, Pallas kernels, pair(): call(functools.partial(pair_kernel, width, half), [f32(3 * width, half)]...  6.88 us
    ppermute x5, starting transfers between devices, pair(): return [kept, lax.ppermute(sent, 'tgt', across)]  5.38 us
    ppermute x5, starting transfers between devices, per_device(): got = [lax.ppermute(piece, 'blk', forward) for piece in (piece, *pieces)]  3.75 us
    ppermute x5, waiting for transfers between devices, pair(): return [kept, lax.ppermute(sent, 'tgt', across)]  3.08 us
    ppermute x1, starting transfers between devices, per_device(): back_early = lax.ppermute(back_early, 'blk', back)  3 us
    ppermute x1, starting transfers between devices, per_device(): cross = lax.ppermute(cross, ('blk', 'tgt'), back_across)  2.86 us
    ppermute x1, waiting for transfers between devices, per_device(): near_sums = pair(widths[-1], lax.ppermute(pieces[-1], 'blk', beside), mark)  2.62 us
  transfers between devices with their start and end apart: 19, of which 8 were waited for; matrix products, arithmetic and copies ran while one was open for 0% of the time, Pallas kernels for 22%

profile of v5, /device:TPU:1, one launch (start us, length us, event | category | flops | bytes accessed | tf_op | source)
XLA Modules:
  0.0 59.5 jit_solution(10712429457863936902)
XLA Ops:
  0.6 1.3 %shard_map.41 = (bf16[160,4096]{1,0:T(8,128)(2,1)S(1)}, f32[8,128]{1,0:T(8,128)S(1)}) custom-call(bf16[512,4096]{1,0:T(8,128)(2,1)} %grads.3), custom_call_target="tpu_custom_call" | custom-call | tf_op jit(solution)/shard_map/pallas_call | solution.py:252
  1.9 2.1 %collective-permute-start.2 = (bf16[160,4096]{1,0:T(8,128)(2,1)S(1)}, bf16[160,4096]{1,0:T(8,128)(2,1)S(1)}, u32[]{:S(2)}, u32[]{:S(2)}) collective-permute-start(bf16[160,4096]{1,0:T(8,128)(2,1)S(1)} %get-tuple-element.39), channel_id=1, source_target_pairs={{0,2},{2,6},{4,0},{6,4},{8,10},{10,14},{12,8},{14,12},{16,18},{18,... | collective-permute-start | bytes 3932168 | tf_op jit(solution)/shard_map/ppermute | solution.py:278
  4.0 2.2 %shard_map.42.grads = bf16[512,4096]{1,0:T(8,128)(2,1)S(1)} custom-call(bf16[512,4096]{1,0:T(8,128)(2,1)} %grads.3, f32[8,128]{1,0:T(8,128)S(1)} %get-tuple-element.34.before), custom_call_target="tpu_custom_call" | custom-call | tf_op jit(solution)/shard_map/pallas_call | solution.py:260
  6.2 2.4 %shard_map.43 = (f32[256,512]{1,0:T(8,128)S(1)}, f32[256,512]{1,0:T(8,128)S(1)}) custom-call(bf16[512,4096]{1,0:T(8,128)(2,1)S(1)} %shard_map.42.grads, f32[8,128]{1,0:T(8,128)S(1)} %get-tuple-element.34.before), custom_call_target="tpu_custom_call" | custom-call | tf_op jit(solution)/shard_map/pallas_call | solution.py:268
  10.0 2.6 %collective-permute-done.3.piece = bf16[64,4096]{1,0:T(8,128)(2,1)S(1)} collective-permute-done((bf16[64,4096]{1,0:T(8,128)(2,1)S(1)}, bf16[64,4096]{1,0:T(8,128)(2,1)S(1)}, u32[]{:S(2)}, u32[]{:S(2)}) %collective-permute-start.3) | collective-permute-done | bytes 524320 | tf_op jit(solution)/shard_map/ppermute | solution.py:293
  12.6 1.3 %shard_map.47 = (f32[96,256]{1,0:T(8,128)S(1)}, f32[96,256]{1,0:T(8,128)S(1)}) custom-call(bf16[64,4096]{1,0:T(8,128)(2,1)S(1)} %collective-permute-done.3.piece, bf16[512,4096]{1,0:T(8,128)(2,1)S(1)} %shard_map.42.grads, f32[8,128]{1,0:T(8,128)S(1)} %get-tuple-element.34.before), custom_call_target="tpu_custom_call" | custom-call | tf_op jit(solution)/shard_map/pallas_call | solution.py:284
  13.9 1.3 %collective-permute-start.4 = (f32[96,256]{1,0:T(8,128)S(1)}, f32[96,256]{1,0:T(8,128)S(1)}, u32[]{:S(2)}, u32[]{:S(2)}) collective-permute-start(f32[96,256]{1,0:T(8,128)S(1)} %get-tuple-element.42), channel_id=1, source_target_pairs={{0,1},{1,0},{2,3},{3,2},{4,5},{5,4},{6,7},{7,6},{8,9},{9,8},{10,11... | collective-permute-start | bytes 294920 | tf_op jit(solution)/shard_map/ppermute | solution.py:290
  15.5 2.8 %collective-permute-done.4.refs_1_ = f32[96,256]{1,0:T(8,128)S(1)} collective-permute-done((f32[96,256]{1,0:T(8,128)S(1)}, f32[96,256]{1,0:T(8,128)S(1)}, u32[]{:S(2)}, u32[]{:S(2)}) %collective-permute-start.4) | collective-permute-done | bytes 98336 | tf_op jit(solution)/shard_map/ppermute | solution.py:290
  18.3 1.6 %collective-permute-start.5 = (bf16[32,512]{1,0:T(8,128)(2,1)S(1)}, bf16[32,512]{1,0:T(8,128)(2,1)S(1)}, u32[]{:S(2)}, u32[]{:S(2)}) collective-permute-start(bf16[32,512]{1,0:T(8,128)(2,1)S(1)} %get-tuple-element.43), channel_id=1, source_target_pairs={{0,2},{2,0},{4,6},{6,4},{8,10},{10,8},{12,14},{14,12},{16,18},{18,... | collective-permute-start | bytes 98312 | tf_op jit(solution)/shard_map/ppermute | solution.py:300
  21.6 1.6 %shard_map.49 = (f32[240,256]{1,0:T(8,128)S(1)}, f32[240,256]{1,0:T(8,128)S(1)}) custom-call(bf16[160,4096]{1,0:T(8,128)(2,1)S(1)} %collective-permute-done.2.piece, bf16[512,4096]{1,0:T(8,128)(2,1)S(1)} %shard_map.42.grads, bf16[32,512]{1,0:T(8,128)(2,1)S(1)} %collective-permute-done.5.before.near_back), custom_call_target="tpu_custom_call" | custom-call | tf_op jit(solution)/shard_map/pallas_call | solution.py:284
  23.2 6.6 %collective-permute-done.7.piece = bf16[128,4096]{1,0:T(8,128)(2,1)S(1)} collective-permute-done((bf16[128,4096]{1,0:T(8,128)(2,1)S(1)}, bf16[128,4096]{1,0:T(8,128)(2,1)S(1)}, u32[]{:S(2)}, u32[]{:S(2)}) %collective-permute-start.7) | collective-permute-done | bytes 1048608 | tf_op jit(solution)/shard_map/ppermute | solution.py:278
  29.8 1.2 %collective-permute-start.6 = (f32[240,256]{1,0:T(8,128)S(1)}, f32[240,256]{1,0:T(8,128)S(1)}, u32[]{:S(2)}, u32[]{:S(2)}) collective-permute-start(f32[240,256]{1,0:T(8,128)S(1)} %get-tuple-element.45), channel_id=1, source_target_pairs={{0,1},{1,0},{2,3},{3,2},{4,5},{5,4},{6,7},{7,6},{8,9},{9,8},{10,11... | collective-permute-start | bytes 737288 | tf_op jit(solution)/shard_map/ppermute | solution.py:290
  31.0 1.4 %shard_map.50 = (f32[192,256]{1,0:T(8,128)S(1)}, f32[192,256]{1,0:T(8,128)S(1)}) custom-call(bf16[128,4096]{1,0:T(8,128)(2,1)S(1)} %collective-permute-done.7.piece, bf16[512,4096]{1,0:T(8,128)(2,1)S(1)} %shard_map.42.grads, f32[8,128]{1,0:T(8,128)S(1)} %get-tuple-element.34.before), custom_call_target="tpu_custom_call" | custom-call | tf_op jit(solution)/shard_map/pallas_call | solution.py:284
  32.4 5.8 %collective-permute-done.9.piece = bf16[96,4096]{1,0:T(8,128)(2,1)S(1)} collective-permute-done((bf16[96,4096]{1,0:T(8,128)(2,1)S(1)}, bf16[96,4096]{1,0:T(8,128)(2,1)S(1)}, u32[]{:S(2)}, u32[]{:S(2)}) %collective-permute-start.9) | collective-permute-done | bytes 786464 | tf_op jit(solution)/shard_map/ppermute | solution.py:278
  38.2 1.2 %collective-permute-start.8 = (f32[192,256]{1,0:T(8,128)S(1)}, f32[192,256]{1,0:T(8,128)S(1)}, u32[]{:S(2)}, u32[]{:S(2)}) collective-permute-start(f32[192,256]{1,0:T(8,128)S(1)} %get-tuple-element.48), channel_id=1, source_target_pairs={{0,1},{1,0},{2,3},{3,2},{4,5},{5,4},{6,7},{7,6},{8,9},{9,8},{10,11... | collective-permute-start | bytes 589832 | tf_op jit(solution)/shard_map/ppermute | solution.py:290
  39.5 1.3 %shard_map.51 = (f32[144,256]{1,0:T(8,128)S(1)}, f32[144,256]{1,0:T(8,128)S(1)}) custom-call(bf16[96,4096]{1,0:T(8,128)(2,1)S(1)} %collective-permute-done.9.piece, bf16[512,4096]{1,0:T(8,128)(2,1)S(1)} %shard_map.42.grads, f32[8,128]{1,0:T(8,128)S(1)} %get-tuple-element.34.before), custom_call_target="tpu_custom_call" | custom-call | tf_op jit(solution)/shard_map/pallas_call | solution.py:284
  41.2 2.7 %collective-permute-done.1.piece = bf16[64,4096]{1,0:T(8,128)(2,1)S(1)} collective-permute-done((bf16[64,4096]{1,0:T(8,128)(2,1)S(1)}, bf16[64,4096]{1,0:T(8,128)(2,1)S(1)}, u32[]{:S(2)}, u32[]{:S(2)}) %collective-permute-start.1) | collective-permute-done | bytes 524320 | tf_op jit(solution)/shard_map/ppermute | solution.py:278
  43.8 1.3 %shard_map.46 = (f32[96,256]{1,0:T(8,128)S(1)}, f32[96,256]{1,0:T(8,128)S(1)}) custom-call(bf16[64,4096]{1,0:T(8,128)(2,1)S(1)} %collective-permute-done.1.piece, bf16[512,4096]{1,0:T(8,128)(2,1)S(1)} %shard_map.42.grads, bf16[256,512]{1,0:T(8,128)(2,1)S(1)} %shard_map.44.before.self_tile), custom_call_target="tpu_custom_call" | custom-call | tf_op jit(solution)/shard_map/pallas_call | solution.py:284
  45.1 1.3 %collective-permute-start.12 = (f32[96,256]{1,0:T(8,128)S(1)}, f32[96,256]{1,0:T(8,128)S(1)}, u32[]{:S(2)}, u32[]{:S(2)}) collective-permute-start(f32[96,256]{1,0:T(8,128)S(1)} %get-tuple-element.54), channel_id=1, source_target_pairs={{0,1},{1,0},{2,3},{3,2},{4,5},{5,4},{6,7},{7,6},{8,9},{9,8},{10,11... | collective-permute-start | bytes 294920 | tf_op jit(solution)/shard_map/ppermute | solution.py:290
  46.9 3.0 %collective-permute-start.16 = (bf16[256,512]{1,0:T(8,128)(2,1)S(1)}, bf16[256,512]{1,0:T(8,128)(2,1)S(1)}, u32[]{:S(2)}, u32[]{:S(2)}) collective-permute-start(bf16[256,512]{1,0:T(8,128)(2,1)S(1)} %get-tuple-element.61), channel_id=1, source_target_pairs={{0,4},{2,0},{4,6},{6,2},{8,12},{10,8},{12,14},{14,10},{16,20},{18,... | collective-permute-start | bytes 786440 | tf_op jit(solution)/shard_map/ppermute | solution.py:313
  50.4 2.9 %collective-permute-start.13 = (f32[32,512]{1,0:T(8,128)S(1)}, f32[32,512]{1,0:T(8,128)S(1)}, u32[]{:S(2)}, u32[]{:S(2)}) collective-permute-start(f32[32,512]{1,0:T(8,128)S(1)} %get-tuple-element.55), channel_id=1, source_target_pairs={{0,5},{1,4},{2,0},{3,1},{4,6},{5,7},{6,3},{7,2},{8,13},{9,12},{10,... | collective-permute-start | bytes 196616 | tf_op jit(solution)/shard_map/ppermute | solution.py:326
  53.3 1.8 %collective-permute-start.14 = (f32[64,256]{1,0:T(8,128)S(1)}, f32[64,256]{1,0:T(8,128)S(1)}, u32[]{:S(2)}, u32[]{:S(2)}) collective-permute-start(f32[64,256]{1,0:T(8,128)S(1)} %get-tuple-element.56), channel_id=1, source_target_pairs={{0,1},{1,0},{2,3},{3,2},{4,5},{5,4},{6,7},{7,6},{8,9},{9,8},{10,11... | collective-permute-start | bytes 196616 | tf_op jit(solution)/shard_map/ppermute | solution.py:324
  56.8 1.7 %collective-permute-done.17.back_third = bf16[32,512]{1,0:T(8,128)(2,1)S(1)} collective-permute-done((bf16[32,512]{1,0:T(8,128)(2,1)S(1)}, bf16[32,512]{1,0:T(8,128)(2,1)S(1)}, u32[]{:S(2)}, u32[]{:S(2)}) %collective-permute-start.17) | collective-permute-done | bytes 32800 | tf_op jit(solution)/shard_map/ppermute | solution.py:327
  58.5 0.9 %shard_map.55 = (bf16[3,256,512]{2,1,0:T(8,128)(2,1)}, f32[64,256]{1,0:T(8,128)}) custom-call(bf16[3,256,512]{2,1,0:T(8,128)(2,1)} %get-tuple-element.53.before, f32[32,512]{1,0:T(8,128)S(1)} %collective-permute-done.13.cross, f32[64,256]{1,0:T(8,128)S(1)} %collective-permute-done.14.got, ...), custom_call_target="tpu_custom_call", output_to_operand_aliasing={{0}: (0, {})} | custom-call | tf_op jit(solution)/shard_map/pallas_call | solution.py:336
  (31 shorter events, 6.5 us)
Async XLA Ops:
  1.9 19.3 %collective-permute-start.2 = (bf16[160,4096]{1,0:T(8,128)(2,1)S(1)}, bf16[160,4096]{1,0:T(8,128)(2,1)S(1)}, u32[]{:S(2)}, u32[]{:S(2)}) collective-permute-start(bf16[160,4096]{1,0:T(8,128)(2,1)S(1)} %get-tuple-element.39), channel_id=1, source_target_pairs={{0,2},{2,6},{4,0},{6,4},{8,10},{10,14},{12,8},{14,12},{16,18},{18,... | collective-permute-start | bytes 3932168 | tf_op jit(solution)/shard_map/ppermute | solution.py:278
  9.2 20.6 %collective-permute-start.7 = (bf16[128,4096]{1,0:T(8,128)(2,1)S(1)}, bf16[128,4096]{1,0:T(8,128)(2,1)S(1)}, u32[]{:S(2)}, u32[]{:S(2)}) collective-permute-start(bf16[128,4096]{1,0:T(8,128)(2,1)S(1)} %get-tuple-element.46), channel_id=1, source_target_pairs={{0,2},{2,6},{4,0},{6,4},{8,10},{10,14},{12,8},{14,12},{16,18},{18,... | collective-permute-start | bytes 3145736 | tf_op jit(solution)/shard_map/ppermute | solution.py:278
  9.9 2.7 %collective-permute-start.3 = (bf16[64,4096]{1,0:T(8,128)(2,1)S(1)}, bf16[64,4096]{1,0:T(8,128)(2,1)S(1)}, u32[]{:S(2)}, u32[]{:S(2)}) collective-permute-start(bf16[64,4096]{1,0:T(8,128)(2,1)S(1)} %get-tuple-element.40), channel_id=1, source_target_pairs={{0,2},{2,0},{4,6},{6,4},{8,10},{10,8},{12,14},{14,12},{16,18},{18,... | collective-permute-start | bytes 1572872 | tf_op jit(solution)/shard_map/ppermute | solution.py:293
  9.9 28.3 %collective-permute-start.9 = (bf16[96,4096]{1,0:T(8,128)(2,1)S(1)}, bf16[96,4096]{1,0:T(8,128)(2,1)S(1)}, u32[]{:S(2)}, u32[]{:S(2)}) collective-permute-start(bf16[96,4096]{1,0:T(8,128)(2,1)S(1)} %get-tuple-element.49), channel_id=1, source_target_pairs={{0,2},{2,6},{4,0},{6,4},{8,10},{10,14},{12,8},{14,12},{16,18},{18,... | collective-permute-start | bytes 2359304 | tf_op jit(solution)/shard_map/ppermute | solution.py:278
  13.9 4.3 %collective-permute-start.4 = (f32[96,256]{1,0:T(8,128)S(1)}, f32[96,256]{1,0:T(8,128)S(1)}, u32[]{:S(2)}, u32[]{:S(2)}) collective-permute-start(f32[96,256]{1,0:T(8,128)S(1)} %get-tuple-element.42), channel_id=1, source_target_pairs={{0,1},{1,0},{2,3},{3,2},{4,5},{5,4},{6,7},{7,6},{8,9},{9,8},{10,11... | collective-permute-start | bytes 294920 | tf_op jit(solution)/shard_map/ppermute | solution.py:290
  15.2 25.6 %collective-permute-start = (f32[256,512]{1,0:T(8,128)S(1)}, f32[256,512]{1,0:T(8,128)S(1)}, u32[]{:S(2)}, u32[]{:S(2)}) collective-permute-start(f32[256,512]{1,0:T(8,128)S(1)} %get-tuple-element.36), channel_id=1, source_target_pairs={{0,1},{1,0},{2,3},{3,2},{4,5},{5,4},{6,7},{7,6},{8,9},{9,8},{10,11... | collective-permute-start | bytes 1572872 | tf_op jit(solution)/shard_map/ppermute | solution.py:281
  18.3 2.4 %collective-permute-start.5 = (bf16[32,512]{1,0:T(8,128)(2,1)S(1)}, bf16[32,512]{1,0:T(8,128)(2,1)S(1)}, u32[]{:S(2)}, u32[]{:S(2)}) collective-permute-start(bf16[32,512]{1,0:T(8,128)(2,1)S(1)} %get-tuple-element.43), channel_id=1, source_target_pairs={{0,2},{2,0},{4,6},{6,4},{8,10},{10,8},{12,14},{14,12},{16,18},{18,... | collective-permute-start | bytes 98312 | tf_op jit(solution)/shard_map/ppermute | solution.py:300
  20.7 23.1 %collective-permute-start.1 = (bf16[64,4096]{1,0:T(8,128)(2,1)S(1)}, bf16[64,4096]{1,0:T(8,128)(2,1)S(1)}, u32[]{:S(2)}, u32[]{:S(2)}) collective-permute-start(bf16[64,4096]{1,0:T(8,128)(2,1)S(1)} %get-tuple-element.37), channel_id=1, source_target_pairs={{0,2},{2,6},{4,0},{6,4},{8,10},{10,14},{12,8},{14,12},{16,18},{18,... | collective-permute-start | bytes 1572872 | tf_op jit(solution)/shard_map/ppermute | solution.py:278
  21.3 29.1 %collective-permute-start.11 = (bf16[64,4096]{1,0:T(8,128)(2,1)S(1)}, bf16[64,4096]{1,0:T(8,128)(2,1)S(1)}, u32[]{:S(2)}, u32[]{:S(2)}) collective-permute-start(bf16[64,4096]{1,0:T(8,128)(2,1)S(1)} %get-tuple-element.40), channel_id=1, source_target_pairs={{0,2},{2,6},{4,0},{6,4},{8,10},{10,14},{12,8},{14,12},{16,18},{18,... | collective-permute-start | bytes 1572872 | tf_op jit(solution)/shard_map/ppermute | solution.py:278
  29.8 17.0 %collective-permute-start.6 = (f32[240,256]{1,0:T(8,128)S(1)}, f32[240,256]{1,0:T(8,128)S(1)}, u32[]{:S(2)}, u32[]{:S(2)}) collective-permute-start(f32[240,256]{1,0:T(8,128)S(1)} %get-tuple-element.45), channel_id=1, source_target_pairs={{0,1},{1,0},{2,3},{3,2},{4,5},{5,4},{6,7},{7,6},{8,9},{9,8},{10,11... | collective-permute-start | bytes 737288 | tf_op jit(solution)/shard_map/ppermute | solution.py:290
  38.2 8.5 %collective-permute-start.8 = (f32[192,256]{1,0:T(8,128)S(1)}, f32[192,256]{1,0:T(8,128)S(1)}, u32[]{:S(2)}, u32[]{:S(2)}) collective-permute-start(f32[192,256]{1,0:T(8,128)S(1)} %get-tuple-element.48), channel_id=1, source_target_pairs={{0,1},{1,0},{2,3},{3,2},{4,5},{5,4},{6,7},{7,6},{8,9},{9,8},{10,11... | collective-permute-start | bytes 589832 | tf_op jit(solution)/shard_map/ppermute | solution.py:290
  40.8 6.0 %copy-start = (bf16[512,64]{0,1:T(8,128)(2,1)S(1)}, bf16[512,64]{0,1:T(8,128)(2,1)}, u32[]{:S(2)}) copy-start(bf16[512,64]{0,1:T(8,128)(2,1)} %param.3) | copy-start | bytes 196612
  40.8 5.9 %collective-permute-start.10 = (f32[144,256]{1,0:T(8,128)S(1)}, f32[144,256]{1,0:T(8,128)S(1)}, u32[]{:S(2)}, u32[]{:S(2)}) collective-permute-start(f32[144,256]{1,0:T(8,128)S(1)} %get-tuple-element.51), channel_id=1, source_target_pairs={{0,1},{1,0},{2,3},{3,2},{4,5},{5,4},{6,7},{7,6},{8,9},{9,8},{10,11... | collective-permute-start | bytes 442376 | tf_op jit(solution)/shard_map/ppermute | solution.py:290
  45.1 5.2 %collective-permute-start.12 = (f32[96,256]{1,0:T(8,128)S(1)}, f32[96,256]{1,0:T(8,128)S(1)}, u32[]{:S(2)}, u32[]{:S(2)}) collective-permute-start(f32[96,256]{1,0:T(8,128)S(1)} %get-tuple-element.54), channel_id=1, source_target_pairs={{0,1},{1,0},{2,3},{3,2},{4,5},{5,4},{6,7},{7,6},{8,9},{9,8},{10,11... | collective-permute-start | bytes 294920 | tf_op jit(solution)/shard_map/ppermute | solution.py:290
  46.9 11.6 %collective-permute-start.16 = (bf16[256,512]{1,0:T(8,128)(2,1)S(1)}, bf16[256,512]{1,0:T(8,128)(2,1)S(1)}, u32[]{:S(2)}, u32[]{:S(2)}) collective-permute-start(bf16[256,512]{1,0:T(8,128)(2,1)S(1)} %get-tuple-element.61), channel_id=1, source_target_pairs={{0,4},{2,0},{4,6},{6,2},{8,12},{10,8},{12,14},{14,10},{16,20},{18,... | collective-permute-start | bytes 786440 | tf_op jit(solution)/shard_map/ppermute | solution.py:313
  49.9 5.5 %collective-permute-start.18 = (bf16[64,512]{1,0:T(8,128)(2,1)S(1)}, bf16[64,512]{1,0:T(8,128)(2,1)S(1)}, u32[]{:S(2)}, u32[]{:S(2)}) collective-permute-start(bf16[64,512]{1,0:T(8,128)(2,1)S(1)} %bitcast.3), channel_id=1, source_target_pairs={{0,2},{2,6},{4,0},{6,4},{8,10},{10,14},{12,8},{14,12},{16,18},{18,... | collective-permute-start | bytes 196616 | tf_op jit(solution)/shard_map/ppermute | solution.py:292
  50.4 8.1 %collective-permute-start.13 = (f32[32,512]{1,0:T(8,128)S(1)}, f32[32,512]{1,0:T(8,128)S(1)}, u32[]{:S(2)}, u32[]{:S(2)}) collective-permute-start(f32[32,512]{1,0:T(8,128)S(1)} %get-tuple-element.55), channel_id=1, source_target_pairs={{0,5},{1,4},{2,0},{3,1},{4,6},{5,7},{6,3},{7,2},{8,13},{9,12},{10,... | collective-permute-start | bytes 196616 | tf_op jit(solution)/shard_map/ppermute | solution.py:326
  53.3 5.2 %collective-permute-start.14 = (f32[64,256]{1,0:T(8,128)S(1)}, f32[64,256]{1,0:T(8,128)S(1)}, u32[]{:S(2)}, u32[]{:S(2)}) collective-permute-start(f32[64,256]{1,0:T(8,128)S(1)} %get-tuple-element.56), channel_id=1, source_target_pairs={{0,1},{1,0},{2,3},{3,2},{4,5},{5,4},{6,7},{7,6},{8,9},{9,8},{10,11... | collective-permute-start | bytes 196616 | tf_op jit(solution)/shard_map/ppermute | solution.py:324
  55.0 3.5 %collective-permute-start.15 = (f32[32,512]{1,0:T(8,128)S(1)}, f32[32,512]{1,0:T(8,128)S(1)}, u32[]{:S(2)}, u32[]{:S(2)}) collective-permute-start(f32[32,512]{1,0:T(8,128)S(1)} %get-tuple-element.57), channel_id=1, source_target_pairs={{0,4},{2,0},{4,6},{6,2},{8,12},{10,8},{12,14},{14,10},{16,20},{18,... | collective-permute-start | bytes 196616 | tf_op jit(solution)/shard_map/ppermute | solution.py:325
  55.4 3.1 %collective-permute-start.17 = (bf16[32,512]{1,0:T(8,128)(2,1)S(1)}, bf16[32,512]{1,0:T(8,128)(2,1)S(1)}, u32[]{:S(2)}, u32[]{:S(2)}) collective-permute-start(bf16[32,512]{1,0:T(8,128)(2,1)S(1)} %get-tuple-element.62), channel_id=1, source_target_pairs={{0,4},{2,0},{4,6},{6,2},{8,12},{10,8},{12,14},{14,10},{16,20},{18,... | collective-permute-start | bytes 98312 | tf_op jit(solution)/shard_map/ppermute | solution.py:327

commit v6 on v5

--- a/solution.py
+++ b/solution.py
@@ -10,10 +10,9 @@
 AFTER = {0: 1, 1: 3, 3: 2, 2: 0}
 BEFORE = {after: before for before, after in AFTER.items()}
 SIXTEENTHS = (5, 4, 3, 2, 2)
-
+EARLY = 3
 FIRST_VMEM = 50
-EARLY = 3
-FLOPS = 1500000000
+FLOPS = 3000000000
 VMEM = pl.BlockSpec(memory_space=pltpu.VMEM)
 ANY = pl.BlockSpec(memory_space=pl.ANY)
 
@@ -71,7 +70,8 @@
 def load_kernel(grads, before, out, sems):
     del before
     size = grads.shape[0] // 4
-    run_copies([(grads.at[pl.ds(i * size, size)], out.at[pl.ds(i * size, size)]) for i in range(4)], sems)
+    parts = [pl.ds(i * size, size) for i in range(4)]
+    run_copies([(grads.at[part], out.at[part]) for part in parts], sems)
 
 
 def rest_kernel(spans, half, grads, before, *refs):
@@ -113,9 +113,9 @@
     share(sent, kept, width)
 
 
-def last_pair_kernel(
-    width, half, scale, piece, grads, before, third, got, sent, kept, near, cross, tile, back
-):
+def last_pair_kernel(width, half, piece, grads, before, sent, kept, near, cross):
+    del before
+
     @pl.when(meets_far())
     def _():
         t = lax.axis_index("tgt")
@@ -125,7 +125,11 @@
             to[:, part_of(t, half)] = kept[part_of(index, width), :]
             to[:, part_of(1 - t, half)] = sent[part_of(index, width), :]
 
-    finish_kernel([back.shape[0]], half, scale, before, third, got, tile, back)
+
+def hand_on_kernel(half, scale, third, got, sent, near, cross, tile, back, *outs):
+    finish_kernel([back.shape[0]], half, scale, None, third, got, tile, back)
+    for value, out in zip((sent, near, cross), outs):
+        out[...] = value[...]
 
 
 def finish_kernel(widths, half, scale, before, *refs):
@@ -180,7 +184,7 @@
 
 
 def last_kernel(
-    half, edge, scale, before, cross, got, near, kept, partial, early, third, back_early,
+    half, edge, scale, before, got, cross, near, kept, partial, early, third, back_early,
     back_third, flat_before, near_new, near_back, tiles, influence, turned, far, late, total, sems,
 ):
     del before
@@ -312,15 +316,20 @@
     )(flat, sums[-2], *sums[: 2 * EARLY])
     back_early = lax.ppermute(back_early, "blk", back)
     *_, second, width = widths
-    sent, kept, near, cross, third, back_third = call(
-        functools.partial(last_pair_kernel, width, half, scale),
-        [f32(2 * width, half)] * 2
-        + [f32(width, rows)] * 2
-        + [b16(2 * second, half), b16(second, rows)],
-        [VMEM] * 2 + [ANY] + [VMEM] * 2,
-        [VMEM] * 6,
+    shapes = [f32(2 * width, half)] + [f32(width, rows)] * 2
+    sent, kept, near, cross = call(
+        functools.partial(last_pair_kernel, width, half),
+        [shapes[0], *shapes],
+        [VMEM] * 2 + [ANY],
+        [VMEM] * 4,
+    )(got[-1], gradients, early)
+    third, back_third, sent, near, cross = call(
+        functools.partial(hand_on_kernel, half, scale),
+        [b16(2 * second, half), b16(second, rows), *shapes],
+        [VMEM] * 5,
+        [VMEM] * 5,
         flops=FLOPS,
-    )(got[-1], gradients, early, *sums[2 * EARLY :])
+    )(*sums[2 * EARLY :], sent, near, cross)
     sent = lax.ppermute(sent, "tgt", across)
     near = lax.ppermute(near, "blk", back)
     cross = lax.ppermute(cross, ("blk", "tgt"), back_across)
@@ -347,7 +356,7 @@
         ],
         {0: 0},
     )(
-        tiles, cross, sent, near, kept, partial, early, third, back_early, back_third,
+        tiles, sent, cross, near, kept, partial, early, third, back_early, back_third,
         flat_before, near_new, near_back,
     )
     return tiles, influence.T

time: 59.6 us -> 59.5 us (level)
  starting transfers between devices: 20.1 us -> 19.1 us
  waiting for transfers between devices: 23.4 us -> 24.2 us
    ppermute x1, starting transfers between devices: 3 us -> 0.02 us  [per_device(): back_early = lax.ppermute(back_early, 'blk', back)]
    ppermute x1, starting transfers between devices: 0.5 us -> 3.46 us  [per_device(): flat_before = lax.ppermute(flat, 'blk', forward)]
    ppermute x1, waiting for transfers between devices: 1.69 us -> 2.49 us  [per_device(): back_third = lax.ppermute(back_third, 'blk', back)]
    ppermute x1, starting transfers between devices: 1.76 us -> 0.97 us  [per_device(): sent = lax.ppermute(sent, 'tgt', across)]
    ppermute x1, starting transfers between devices: 2.86 us -> 3.51 us  [per_device(): cross = lax.ppermute(cross, ('blk', 'tgt'), back_across)]
where the time goes in v6:
time: 59.5 us; the launch traced here: 59.4 us
  waiting for transfers between devices  24.2 us (41%)
  starting transfers between devices  19.1 us (32%)
  Pallas kernels  15.3 us (26%)
  between operations  0.8 us (1%)
    ppermute x5, waiting for transfers between devices, per_device(): got = [lax.ppermute(piece, 'blk', forward) for piece in (piece, *pieces)]  15.1 us
    pallas_call x5, Pallas kernels, pair(): call(functools.partial(pair_kernel, width, half), [f32(3 * width, half)]...  6.89 us
    ppermute x5, starting transfers between devices, pair(): return [kept, lax.ppermute(sent, 'tgt', across)]  5.38 us
    ppermute x5, starting transfers between devices, per_device(): got = [lax.ppermute(piece, 'blk', forward) for piece in (piece, *pieces)]  3.75 us
    ppermute x1, starting transfers between devices, per_device(): cross = lax.ppermute(cross, ('blk', 'tgt'), back_across)  3.51 us
    ppermute x1, starting transfers between devices, per_device(): flat_before = lax.ppermute(flat, 'blk', forward)  3.46 us
    ppermute x5, waiting for transfers between devices, pair(): return [kept, lax.ppermute(sent, 'tgt', across)]  3.08 us
    ppermute x1, waiting for transfers between devices, per_device(): near_sums = pair(widths[-1], lax.ppermute(pieces[-1], 'blk', beside), mark)  2.62 us
  transfers between devices with their start and end apart: 19, of which 8 were waited for; matrix products, arithmetic and copies ran while one was open for 0% of the time, Pallas kernels for 22%

profile of v6, /device:TPU:1, one launch (start us, length us, event | category | flops | bytes accessed | tf_op | source)
XLA Modules:
  0.0 59.4 jit_solution(3318796619274273587)
XLA Ops:
  0.6 1.3 %shard_map.41 = (bf16[160,4096]{1,0:T(8,128)(2,1)S(1)}, f32[8,128]{1,0:T(8,128)S(1)}) custom-call(bf16[512,4096]{1,0:T(8,128)(2,1)} %grads.3), custom_call_target="tpu_custom_call" | custom-call | tf_op jit(solution)/shard_map/pallas_call | solution.py:256
  1.9 2.1 %collective-permute-start.2 = (bf16[160,4096]{1,0:T(8,128)(2,1)S(1)}, bf16[160,4096]{1,0:T(8,128)(2,1)S(1)}, u32[]{:S(2)}, u32[]{:S(2)}) collective-permute-start(bf16[160,4096]{1,0:T(8,128)(2,1)S(1)} %get-tuple-element.42), channel_id=1, source_target_pairs={{0,2},{2,6},{4,0},{6,4},{8,10},{10,14},{12,8},{14,12},{16,18},{18,... | collective-permute-start | bytes 3932168 | tf_op jit(solution)/shard_map/ppermute | solution.py:282
  4.0 2.2 %shard_map.42.grads = bf16[512,4096]{1,0:T(8,128)(2,1)S(1)} custom-call(bf16[512,4096]{1,0:T(8,128)(2,1)} %grads.3, f32[8,128]{1,0:T(8,128)S(1)} %get-tuple-element.37.before), custom_call_target="tpu_custom_call" | custom-call | tf_op jit(solution)/shard_map/pallas_call | solution.py:264
  6.2 2.4 %shard_map.43 = (f32[256,512]{1,0:T(8,128)S(1)}, f32[256,512]{1,0:T(8,128)S(1)}) custom-call(bf16[512,4096]{1,0:T(8,128)(2,1)S(1)} %shard_map.42.grads, f32[8,128]{1,0:T(8,128)S(1)} %get-tuple-element.37.before), custom_call_target="tpu_custom_call" | custom-call | tf_op jit(solution)/shard_map/pallas_call | solution.py:272
  10.0 2.6 %collective-permute-done.3.piece = bf16[64,4096]{1,0:T(8,128)(2,1)S(1)} collective-permute-done((bf16[64,4096]{1,0:T(8,128)(2,1)S(1)}, bf16[64,4096]{1,0:T(8,128)(2,1)S(1)}, u32[]{:S(2)}, u32[]{:S(2)}) %collective-permute-start.3) | collective-permute-done | bytes 524320 | tf_op jit(solution)/shard_map/ppermute | solution.py:297
  12.6 1.3 %shard_map.47 = (f32[96,256]{1,0:T(8,128)S(1)}, f32[96,256]{1,0:T(8,128)S(1)}) custom-call(bf16[64,4096]{1,0:T(8,128)(2,1)S(1)} %collective-permute-done.3.piece, bf16[512,4096]{1,0:T(8,128)(2,1)S(1)} %shard_map.42.grads, f32[8,128]{1,0:T(8,128)S(1)} %get-tuple-element.37.before), custom_call_target="tpu_custom_call" | custom-call | tf_op jit(solution)/shard_map/pallas_call | solution.py:288
  13.9 1.3 %collective-permute-start.4 = (f32[96,256]{1,0:T(8,128)S(1)}, f32[96,256]{1,0:T(8,128)S(1)}, u32[]{:S(2)}, u32[]{:S(2)}) collective-permute-start(f32[96,256]{1,0:T(8,128)S(1)} %get-tuple-element.45), channel_id=1, source_target_pairs={{0,1},{1,0},{2,3},{3,2},{4,5},{5,4},{6,7},{7,6},{8,9},{9,8},{10,11... | collective-permute-start | bytes 294920 | tf_op jit(solution)/shard_map/ppermute | solution.py:294
  15.5 2.8 %collective-permute-done.4.refs_1_ = f32[96,256]{1,0:T(8,128)S(1)} collective-permute-done((f32[96,256]{1,0:T(8,128)S(1)}, f32[96,256]{1,0:T(8,128)S(1)}, u32[]{:S(2)}, u32[]{:S(2)}) %collective-permute-start.4) | collective-permute-done | bytes 98336 | tf_op jit(solution)/shard_map/ppermute | solution.py:294
  18.3 1.6 %collective-permute-start.5 = (bf16[32,512]{1,0:T(8,128)(2,1)S(1)}, bf16[32,512]{1,0:T(8,128)(2,1)S(1)}, u32[]{:S(2)}, u32[]{:S(2)}) collective-permute-start(bf16[32,512]{1,0:T(8,128)(2,1)S(1)} %get-tuple-element.46), channel_id=1, source_target_pairs={{0,2},{2,0},{4,6},{6,4},{8,10},{10,8},{12,14},{14,12},{16,18},{18,... | collective-permute-start | bytes 98312 | tf_op jit(solution)/shard_map/ppermute | solution.py:304
  21.6 1.6 %shard_map.49 = (f32[240,256]{1,0:T(8,128)S(1)}, f32[240,256]{1,0:T(8,128)S(1)}) custom-call(bf16[160,4096]{1,0:T(8,128)(2,1)S(1)} %collective-permute-done.2.piece, bf16[512,4096]{1,0:T(8,128)(2,1)S(1)} %shard_map.42.grads, bf16[32,512]{1,0:T(8,128)(2,1)S(1)} %collective-permute-done.5.before.near_back), custom_call_target="tpu_custom_call" | custom-call | tf_op jit(solution)/shard_map/pallas_call | solution.py:288
  23.2 6.6 %collective-permute-done.7.piece = bf16[128,4096]{1,0:T(8,128)(2,1)S(1)} collective-permute-done((bf16[128,4096]{1,0:T(8,128)(2,1)S(1)}, bf16[128,4096]{1,0:T(8,128)(2,1)S(1)}, u32[]{:S(2)}, u32[]{:S(2)}) %collective-permute-start.7) | collective-permute-done | bytes 1048608 | tf_op jit(solution)/shard_map/ppermute | solution.py:282
  29.8 1.2 %collective-permute-start.6 = (f32[240,256]{1,0:T(8,128)S(1)}, f32[240,256]{1,0:T(8,128)S(1)}, u32[]{:S(2)}, u32[]{:S(2)}) collective-permute-start(f32[240,256]{1,0:T(8,128)S(1)} %get-tuple-element.48), channel_id=1, source_target_pairs={{0,1},{1,0},{2,3},{3,2},{4,5},{5,4},{6,7},{7,6},{8,9},{9,8},{10,11... | collective-permute-start | bytes 737288 | tf_op jit(solution)/shard_map/ppermute | solution.py:294
  31.0 1.4 %shard_map.50 = (f32[192,256]{1,0:T(8,128)S(1)}, f32[192,256]{1,0:T(8,128)S(1)}) custom-call(bf16[128,4096]{1,0:T(8,128)(2,1)S(1)} %collective-permute-done.7.piece, bf16[512,4096]{1,0:T(8,128)(2,1)S(1)} %shard_map.42.grads, f32[8,128]{1,0:T(8,128)S(1)} %get-tuple-element.37.before), custom_call_target="tpu_custom_call" | custom-call | tf_op jit(solution)/shard_map/pallas_call | solution.py:288
  32.4 5.8 %collective-permute-done.9.piece = bf16[96,4096]{1,0:T(8,128)(2,1)S(1)} collective-permute-done((bf16[96,4096]{1,0:T(8,128)(2,1)S(1)}, bf16[96,4096]{1,0:T(8,128)(2,1)S(1)}, u32[]{:S(2)}, u32[]{:S(2)}) %collective-permute-start.9) | collective-permute-done | bytes 786464 | tf_op jit(solution)/shard_map/ppermute | solution.py:282
  38.2 1.2 %collective-permute-start.8 = (f32[192,256]{1,0:T(8,128)S(1)}, f32[192,256]{1,0:T(8,128)S(1)}, u32[]{:S(2)}, u32[]{:S(2)}) collective-permute-start(f32[192,256]{1,0:T(8,128)S(1)} %get-tuple-element.51), channel_id=1, source_target_pairs={{0,1},{1,0},{2,3},{3,2},{4,5},{5,4},{6,7},{7,6},{8,9},{9,8},{10,11... | collective-permute-start | bytes 589832 | tf_op jit(solution)/shard_map/ppermute | solution.py:294
  39.5 1.3 %shard_map.51 = (f32[144,256]{1,0:T(8,128)S(1)}, f32[144,256]{1,0:T(8,128)S(1)}) custom-call(bf16[96,4096]{1,0:T(8,128)(2,1)S(1)} %collective-permute-done.9.piece, bf16[512,4096]{1,0:T(8,128)(2,1)S(1)} %shard_map.42.grads, f32[8,128]{1,0:T(8,128)S(1)} %get-tuple-element.37.before), custom_call_target="tpu_custom_call" | custom-call | tf_op jit(solution)/shard_map/pallas_call | solution.py:288
  41.2 2.7 %collective-permute-done.1.piece = bf16[64,4096]{1,0:T(8,128)(2,1)S(1)} collective-permute-done((bf16[64,4096]{1,0:T(8,128)(2,1)S(1)}, bf16[64,4096]{1,0:T(8,128)(2,1)S(1)}, u32[]{:S(2)}, u32[]{:S(2)}) %collective-permute-start.1) | collective-permute-done | bytes 524320 | tf_op jit(solution)/shard_map/ppermute | solution.py:282
  43.8 1.3 %shard_map.46 = (f32[96,256]{1,0:T(8,128)S(1)}, f32[96,256]{1,0:T(8,128)S(1)}) custom-call(bf16[64,4096]{1,0:T(8,128)(2,1)S(1)} %collective-permute-done.1.piece, bf16[512,4096]{1,0:T(8,128)(2,1)S(1)} %shard_map.42.grads, bf16[256,512]{1,0:T(8,128)(2,1)S(1)} %shard_map.44.before.self_tile), custom_call_target="tpu_custom_call" | custom-call | tf_op jit(solution)/shard_map/pallas_call | solution.py:288
  45.1 1.3 %collective-permute-start.11 = (f32[96,256]{1,0:T(8,128)S(1)}, f32[96,256]{1,0:T(8,128)S(1)}, u32[]{:S(2)}, u32[]{:S(2)}) collective-permute-start(f32[96,256]{1,0:T(8,128)S(1)} %get-tuple-element.57), channel_id=1, source_target_pairs={{0,1},{1,0},{2,3},{3,2},{4,5},{5,4},{6,7},{7,6},{8,9},{9,8},{10,11... | collective-permute-start | bytes 294920 | tf_op jit(solution)/shard_map/ppermute | solution.py:294
  46.7 3.5 %collective-permute-start.18 = (bf16[64,512]{1,0:T(8,128)(2,1)S(1)}, bf16[64,512]{1,0:T(8,128)(2,1)S(1)}, u32[]{:S(2)}, u32[]{:S(2)}) collective-permute-start(bf16[64,512]{1,0:T(8,128)(2,1)S(1)} %bitcast.2), channel_id=1, source_target_pairs={{0,2},{2,6},{4,0},{6,4},{8,10},{10,14},{12,8},{14,12},{16,18},{18,... | collective-permute-start | bytes 196616 | tf_op jit(solution)/shard_map/ppermute | solution.py:296
  50.5 1.0 %collective-permute-start.13 = (f32[64,256]{1,0:T(8,128)S(1)}, f32[64,256]{1,0:T(8,128)S(1)}, u32[]{:S(2)}, u32[]{:S(2)}) collective-permute-start(f32[64,256]{1,0:T(8,128)S(1)} %get-tuple-element.61), channel_id=1, source_target_pairs={{0,1},{1,0},{2,3},{3,2},{4,5},{5,4},{6,7},{7,6},{8,9},{9,8},{10,11... | collective-permute-start | bytes 196616 | tf_op jit(solution)/shard_map/ppermute | solution.py:333
  51.4 3.5 %collective-permute-start.14 = (f32[32,512]{1,0:T(8,128)S(1)}, f32[32,512]{1,0:T(8,128)S(1)}, u32[]{:S(2)}, u32[]{:S(2)}) collective-permute-start(f32[32,512]{1,0:T(8,128)S(1)} %get-tuple-element.62), channel_id=1, source_target_pairs={{0,5},{1,4},{2,0},{3,1},{4,6},{5,7},{6,3},{7,2},{8,13},{9,12},{10,... | collective-permute-start | bytes 196616 | tf_op jit(solution)/shard_map/ppermute | solution.py:335
  55.9 2.5 %collective-permute-done.17.back_third = bf16[32,512]{1,0:T(8,128)(2,1)S(1)} collective-permute-done((bf16[32,512]{1,0:T(8,128)(2,1)S(1)}, bf16[32,512]{1,0:T(8,128)(2,1)S(1)}, u32[]{:S(2)}, u32[]{:S(2)}) %collective-permute-start.17) | collective-permute-done | bytes 32800 | tf_op jit(solution)/shard_map/ppermute | solution.py:336
  58.4 0.9 %shard_map.56 = (bf16[3,256,512]{2,1,0:T(8,128)(2,1)}, f32[64,256]{1,0:T(8,128)}) custom-call(bf16[3,256,512]{2,1,0:T(8,128)(2,1)} %get-tuple-element.56.before, f32[64,256]{1,0:T(8,128)S(1)} %collective-permute-done.13.got, f32[32,512]{1,0:T(8,128)S(1)} %collective-permute-done.14.cross, ...), custom_call_target="tpu_custom_call", output_to_operand_aliasing={{0}: (0, {})} | custom-call | tf_op jit(solution)/shard_map/pallas_call | solution.py:345
  (32 shorter events, 5.2 us)
Async XLA Ops:
  1.9 19.3 %collective-permute-start.2 = (bf16[160,4096]{1,0:T(8,128)(2,1)S(1)}, bf16[160,4096]{1,0:T(8,128)(2,1)S(1)}, u32[]{:S(2)}, u32[]{:S(2)}) collective-permute-start(bf16[160,4096]{1,0:T(8,128)(2,1)S(1)} %get-tuple-element.42), channel_id=1, source_target_pairs={{0,2},{2,6},{4,0},{6,4},{8,10},{10,14},{12,8},{14,12},{16,18},{18,... | collective-permute-start | bytes 3932168 | tf_op jit(solution)/shard_map/ppermute | solution.py:282
  9.2 20.6 %collective-permute-start.7 = (bf16[128,4096]{1,0:T(8,128)(2,1)S(1)}, bf16[128,4096]{1,0:T(8,128)(2,1)S(1)}, u32[]{:S(2)}, u32[]{:S(2)}) collective-permute-start(bf16[128,4096]{1,0:T(8,128)(2,1)S(1)} %get-tuple-element.49), channel_id=1, source_target_pairs={{0,2},{2,6},{4,0},{6,4},{8,10},{10,14},{12,8},{14,12},{16,18},{18,... | collective-permute-start | bytes 3145736 | tf_op jit(solution)/shard_map/ppermute | solution.py:282
  9.9 2.7 %collective-permute-start.3 = (bf16[64,4096]{1,0:T(8,128)(2,1)S(1)}, bf16[64,4096]{1,0:T(8,128)(2,1)S(1)}, u32[]{:S(2)}, u32[]{:S(2)}) collective-permute-start(bf16[64,4096]{1,0:T(8,128)(2,1)S(1)} %get-tuple-element.43), channel_id=1, source_target_pairs={{0,2},{2,0},{4,6},{6,4},{8,10},{10,8},{12,14},{14,12},{16,18},{18,... | collective-permute-start | bytes 1572872 | tf_op jit(solution)/shard_map/ppermute | solution.py:297
  9.9 28.3 %collective-permute-start.9 = (bf16[96,4096]{1,0:T(8,128)(2,1)S(1)}, bf16[96,4096]{1,0:T(8,128)(2,1)S(1)}, u32[]{:S(2)}, u32[]{:S(2)}) collective-permute-start(bf16[96,4096]{1,0:T(8,128)(2,1)S(1)} %get-tuple-element.52), channel_id=1, source_target_pairs={{0,2},{2,6},{4,0},{6,4},{8,10},{10,14},{12,8},{14,12},{16,18},{18,... | collective-permute-start | bytes 2359304 | tf_op jit(solution)/shard_map/ppermute | solution.py:282
  13.9 4.3 %collective-permute-start.4 = (f32[96,256]{1,0:T(8,128)S(1)}, f32[96,256]{1,0:T(8,128)S(1)}, u32[]{:S(2)}, u32[]{:S(2)}) collective-permute-start(f32[96,256]{1,0:T(8,128)S(1)} %get-tuple-element.45), channel_id=1, source_target_pairs={{0,1},{1,0},{2,3},{3,2},{4,5},{5,4},{6,7},{7,6},{8,9},{9,8},{10,11... | collective-permute-start | bytes 294920 | tf_op jit(solution)/shard_map/ppermute | solution.py:294
  15.2 25.6 %collective-permute-start = (f32[256,512]{1,0:T(8,128)S(1)}, f32[256,512]{1,0:T(8,128)S(1)}, u32[]{:S(2)}, u32[]{:S(2)}) collective-permute-start(f32[256,512]{1,0:T(8,128)S(1)} %get-tuple-element.39), channel_id=1, source_target_pairs={{0,1},{1,0},{2,3},{3,2},{4,5},{5,4},{6,7},{7,6},{8,9},{9,8},{10,11... | collective-permute-start | bytes 1572872 | tf_op jit(solution)/shard_map/ppermute | solution.py:285
  18.3 2.4 %collective-permute-start.5 = (bf16[32,512]{1,0:T(8,128)(2,1)S(1)}, bf16[32,512]{1,0:T(8,128)(2,1)S(1)}, u32[]{:S(2)}, u32[]{:S(2)}) collective-permute-start(bf16[32,512]{1,0:T(8,128)(2,1)S(1)} %get-tuple-element.46), channel_id=1, source_target_pairs={{0,2},{2,0},{4,6},{6,4},{8,10},{10,8},{12,14},{14,12},{16,18},{18,... | collective-permute-start | bytes 98312 | tf_op jit(solution)/shard_map/ppermute | solution.py:304
  20.7 23.1 %collective-permute-start.1 = (bf16[64,4096]{1,0:T(8,128)(2,1)S(1)}, bf16[64,4096]{1,0:T(8,128)(2,1)S(1)}, u32[]{:S(2)}, u32[]{:S(2)}) collective-permute-start(bf16[64,4096]{1,0:T(8,128)(2,1)S(1)} %get-tuple-element.40), channel_id=1, source_target_pairs={{0,2},{2,6},{4,0},{6,4},{8,10},{10,14},{12,8},{14,12},{16,18},{18,... | collective-permute-start | bytes 1572872 | tf_op jit(solution)/shard_map/ppermute | solution.py:282
  21.3 29.1 %collective-permute-start.12 = (bf16[64,4096]{1,0:T(8,128)(2,1)S(1)}, bf16[64,4096]{1,0:T(8,128)(2,1)S(1)}, u32[]{:S(2)}, u32[]{:S(2)}) collective-permute-start(bf16[64,4096]{1,0:T(8,128)(2,1)S(1)} %get-tuple-element.43), channel_id=1, source_target_pairs={{0,2},{2,6},{4,0},{6,4},{8,10},{10,14},{12,8},{14,12},{16,18},{18,... | collective-permute-start | bytes 1572872 | tf_op jit(solution)/shard_map/ppermute | solution.py:282
  29.8 20.4 %collective-permute-start.6 = (f32[240,256]{1,0:T(8,128)S(1)}, f32[240,256]{1,0:T(8,128)S(1)}, u32[]{:S(2)}, u32[]{:S(2)}) collective-permute-start(f32[240,256]{1,0:T(8,128)S(1)} %get-tuple-element.48), channel_id=1, source_target_pairs={{0,1},{1,0},{2,3},{3,2},{4,5},{5,4},{6,7},{7,6},{8,9},{9,8},{10,11... | collective-permute-start | bytes 737288 | tf_op jit(solution)/shard_map/ppermute | solution.py:294
  38.2 12.0 %collective-permute-start.8 = (f32[192,256]{1,0:T(8,128)S(1)}, f32[192,256]{1,0:T(8,128)S(1)}, u32[]{:S(2)}, u32[]{:S(2)}) collective-permute-start(f32[192,256]{1,0:T(8,128)S(1)} %get-tuple-element.51), channel_id=1, source_target_pairs={{0,1},{1,0},{2,3},{3,2},{4,5},{5,4},{6,7},{7,6},{8,9},{9,8},{10,11... | collective-permute-start | bytes 589832 | tf_op jit(solution)/shard_map/ppermute | solution.py:294
  40.8 6.0 %copy-start = (bf16[512,64]{0,1:T(8,128)(2,1)S(1)}, bf16[512,64]{0,1:T(8,128)(2,1)}, u32[]{:S(2)}) copy-start(bf16[512,64]{0,1:T(8,128)(2,1)} %param.3) | copy-start | bytes 196612
  40.8 5.9 %collective-permute-start.10 = (f32[144,256]{1,0:T(8,128)S(1)}, f32[144,256]{1,0:T(8,128)S(1)}, u32[]{:S(2)}, u32[]{:S(2)}) collective-permute-start(f32[144,256]{1,0:T(8,128)S(1)} %get-tuple-element.54), channel_id=1, source_target_pairs={{0,1},{1,0},{2,3},{3,2},{4,5},{5,4},{6,7},{7,6},{8,9},{9,8},{10,11... | collective-permute-start | bytes 442376 | tf_op jit(solution)/shard_map/ppermute | solution.py:294
  45.1 5.3 %collective-permute-start.11 = (f32[96,256]{1,0:T(8,128)S(1)}, f32[96,256]{1,0:T(8,128)S(1)}, u32[]{:S(2)}, u32[]{:S(2)}) collective-permute-start(f32[96,256]{1,0:T(8,128)S(1)} %get-tuple-element.57), channel_id=1, source_target_pairs={{0,1},{1,0},{2,3},{3,2},{4,5},{5,4},{6,7},{7,6},{8,9},{9,8},{10,11... | collective-permute-start | bytes 294920 | tf_op jit(solution)/shard_map/ppermute | solution.py:294
  46.7 8.2 %collective-permute-start.18 = (bf16[64,512]{1,0:T(8,128)(2,1)S(1)}, bf16[64,512]{1,0:T(8,128)(2,1)S(1)}, u32[]{:S(2)}, u32[]{:S(2)}) collective-permute-start(bf16[64,512]{1,0:T(8,128)(2,1)S(1)} %bitcast.2), channel_id=1, source_target_pairs={{0,2},{2,6},{4,0},{6,4},{8,10},{10,14},{12,8},{14,12},{16,18},{18,... | collective-permute-start | bytes 196616 | tf_op jit(solution)/shard_map/ppermute | solution.py:296
  50.3 8.1 %collective-permute-start.16 = (bf16[256,512]{1,0:T(8,128)(2,1)S(1)}, bf16[256,512]{1,0:T(8,128)(2,1)S(1)}, u32[]{:S(2)}, u32[]{:S(2)}) collective-permute-start(bf16[256,512]{1,0:T(8,128)(2,1)S(1)} %get-tuple-element.67), channel_id=1, source_target_pairs={{0,4},{2,0},{4,6},{6,2},{8,12},{10,8},{12,14},{14,10},{16,20},{18,... | collective-permute-start | bytes 786440 | tf_op jit(solution)/shard_map/ppermute | solution.py:317
  50.5 7.9 %collective-permute-start.13 = (f32[64,256]{1,0:T(8,128)S(1)}, f32[64,256]{1,0:T(8,128)S(1)}, u32[]{:S(2)}, u32[]{:S(2)}) collective-permute-start(f32[64,256]{1,0:T(8,128)S(1)} %get-tuple-element.61), channel_id=1, source_target_pairs={{0,1},{1,0},{2,3},{3,2},{4,5},{5,4},{6,7},{7,6},{8,9},{9,8},{10,11... | collective-permute-start | bytes 196616 | tf_op jit(solution)/shard_map/ppermute | solution.py:333
  51.4 7.0 %collective-permute-start.14 = (f32[32,512]{1,0:T(8,128)S(1)}, f32[32,512]{1,0:T(8,128)S(1)}, u32[]{:S(2)}, u32[]{:S(2)}) collective-permute-start(f32[32,512]{1,0:T(8,128)S(1)} %get-tuple-element.62), channel_id=1, source_target_pairs={{0,5},{1,4},{2,0},{3,1},{4,6},{5,7},{6,3},{7,2},{8,13},{9,12},{10,... | collective-permute-start | bytes 196616 | tf_op jit(solution)/shard_map/ppermute | solution.py:335
  54.9 3.5 %collective-permute-start.15 = (f32[32,512]{1,0:T(8,128)S(1)}, f32[32,512]{1,0:T(8,128)S(1)}, u32[]{:S(2)}, u32[]{:S(2)}) collective-permute-start(f32[32,512]{1,0:T(8,128)S(1)} %get-tuple-element.63), channel_id=1, source_target_pairs={{0,4},{2,0},{4,6},{6,2},{8,12},{10,8},{12,14},{14,10},{16,20},{18,... | collective-permute-start | bytes 196616 | tf_op jit(solution)/shard_map/ppermute | solution.py:334
  54.9 3.5 %collective-permute-start.17 = (bf16[32,512]{1,0:T(8,128)(2,1)S(1)}, bf16[32,512]{1,0:T(8,128)(2,1)S(1)}, u32[]{:S(2)}, u32[]{:S(2)}) collective-permute-start(bf16[32,512]{1,0:T(8,128)(2,1)S(1)} %get-tuple-element.68), channel_id=1, source_target_pairs={{0,4},{2,0},{4,6},{6,2},{8,12},{10,8},{12,14},{14,10},{16,20},{18,... | collective-permute-start | bytes 98312 | tf_op jit(solution)/shard_map/ppermute | solution.py:336

commit v7 on v6

--- a/solution.py
+++ b/solution.py
@@ -163,12 +163,20 @@
     return jnp.where(meets_far(), 2, 1)
 
 
-def most_kernel(half, edge, self_tile, tile, flat, tiles, partial, turned, sems):
+def most_kernel(
+    half, edge, self_tile, tile, flat, flat_before, back, tiles, partial, turned, far, sems
+):
     slot = own_slot()
     whole = pltpu.make_async_copy(self_tile, tiles.at[0], sems.at[0])
     whole.start()
-    partial[...] = contract(flat[...], self_tile[...])
     copies, size = [], tile.shape[0] // 2
+    returned = pltpu.make_async_copy(
+        back.at[pl.ds(0, size)], tiles.at[3 - slot, pl.ds(0, size)], sems.at[3]
+    )
+    returned.start()
+    far[:size, :] = back[:size, :]
+    far[size:, :] = jnp.zeros((half - size, far.shape[1]), far.dtype)
+    value = contract(flat[...], self_tile[...]) + contract(back[size:, :], far[...])
     for h in range(2):
         part = tile[h * size : h * size + edge, :]
         turned[h] = part.T
@@ -178,7 +186,10 @@
             )
         )
         copies[h].start()
+        value += multiply(flat_before[:, h * half : h * half + edge], part)
+    partial[...] = value
     whole.wait()
+    returned.wait()
     for copy in copies:
         copy.wait()
 
@@ -198,12 +209,12 @@
         copies.append(pltpu.make_async_copy(source, target, sems.at[len(copies)]))
         copies[-1].start()
 
-    copy(back_early.at[pl.ds(0, first)], tiles.at[3 - slot, pl.ds(0, first)])
-    far[first:done, :] = back_third[...]
+    far[: first - edge, :] = jnp.zeros((first - edge, far.shape[1]), far.dtype)
+    far[first - edge : done - edge, :] = back_third[...]
     summed = ((near[...] + cross[...]) * scale).astype(jnp.bfloat16)
-    far[done:, :] = jnp.where(meets_far(), near_back[...], summed)
+    far[done - edge :, :] = jnp.where(meets_far(), near_back[...], summed)
     copy(
-        far.at[pl.ds(first, second + width)], tiles.at[3 - slot, pl.ds(first, second + width)]
+        far.at[pl.ds(first - edge, second + width)], tiles.at[3 - slot, pl.ds(first, second + width)]
     )
     new = ((kept[...] + got[...]) * scale).astype(jnp.bfloat16)
     new = jnp.where(meets_far(), new, near_new[...])
@@ -215,11 +226,9 @@
         late[h, done - edge :, :] = new[h * width : (h + 1) * width]
         turned[h] = late[h].T
         copy(turned.at[h], tiles.at[slot, :, pl.ds(start + edge, half - edge)])
-        value += multiply(
-            flat_before[:, start : start + edge], early[h * first : h * first + edge, :]
-        ) + multiply(flat_before[:, start + edge : start + half], late[h])
-    far[:first, :] = back_early[:first, :]
-    total[...] = value + contract(back_early[first:, :], far[...])
+        value += multiply(flat_before[:, start + edge : start + half], late[h])
+    total[:, :edge] = value[:, :edge]
+    total[:, edge:] = value[:, edge:] + contract(back_early[first:, :], far[...])
     copy(total, influence)
     for each in copies:
         each.wait()
@@ -338,10 +347,14 @@
     tiles, partial = call(
         functools.partial(most_kernel, half, edge),
         [b16(3, half, rows), f32(columns, half)],
-        [VMEM] * 3,
+        [VMEM] * 5,
         [ANY, VMEM],
-        [pltpu.VMEM((2, half, edge), jnp.bfloat16), pltpu.SemaphoreType.DMA((3,))],
-    )(self_tile, early, flat)
+        [
+            pltpu.VMEM((2, half, edge), jnp.bfloat16),
+            pltpu.VMEM((half, rows), jnp.bfloat16),
+            pltpu.SemaphoreType.DMA((4,)),
+        ],
+    )(self_tile, early, flat, flat_before, back_early)
     tiles, influence = call(
         functools.partial(last_kernel, half, edge, scale),
         [b16(3, half, rows), f32(columns, half)],
@@ -349,7 +362,7 @@
         [ANY] * 2,
         [
             pltpu.VMEM((2, half, half - edge), jnp.bfloat16),
-            pltpu.VMEM((half, rows), jnp.bfloat16),
+            pltpu.VMEM((half - edge, rows), jnp.bfloat16),
             pltpu.VMEM((2, half - edge, half), jnp.bfloat16),
             pltpu.VMEM((columns, half), jnp.float32),
             pltpu.SemaphoreType.DMA((5,)),

time: 59.5 us -> 59.4 us (level)
    ppermute x1, waiting for transfers between devices: 2.49 us -> 1.33 us  [per_device(): back_third = lax.ppermute(back_third, 'blk', back)]
    ppermute x1, waiting for transfers between devices: 0.01 us -> 1 us  [per_device(): back_early = lax.ppermute(back_early, 'blk', back)]
  transfers between devices with their start and end apart: 19 -> 19, of which waited for: 8 -> 9; matrix products, arithmetic and copies ran while one was open for 0% -> 0% of each run, Pallas kernels for 22% -> 22%
where the time goes in v7:
time: 59.4 us; the launch traced here: 59.3 us
  waiting for transfers between devices  24 us (40%)
  starting transfers between devices  19.1 us (32%)
  Pallas kernels  15.4 us (26%)
  between operations  0.79 us (1%)
    ppermute x5, waiting for transfers between devices, per_device(): got = [lax.ppermute(piece, 'blk', forward) for piece in (piece, *pieces)]  15.1 us
    pallas_call x5, Pallas kernels, pair(): call(functools.partial(pair_kernel, width, half), [f32(3 * width, half)]...  6.89 us
    ppermute x5, starting transfers between devices, pair(): return [kept, lax.ppermute(sent, 'tgt', across)]  5.38 us
    ppermute x5, starting transfers between devices, per_device(): got = [lax.ppermute(piece, 'blk', forward) for piece in (piece, *pieces)]  3.75 us
    ppermute x1, starting transfers between devices, per_device(): cross = lax.ppermute(cross, ('blk', 'tgt'), back_across)  3.51 us
    ppermute x1, starting transfers between devices, per_device(): flat_before = lax.ppermute(flat, 'blk', forward)  3.46 us
    ppermute x5, waiting for transfers between devices, pair(): return [kept, lax.ppermute(sent, 'tgt', across)]  3.08 us
    ppermute x1, waiting for transfers between devices, per_device(): near_sums = pair(widths[-1], lax.ppermute(pieces[-1], 'blk', beside), mark)  2.62 us
  transfers between devices with their start and end apart: 19, of which 9 were waited for; matrix products, arithmetic and copies ran while one was open for 0% of the time, Pallas kernels for 22%

profile of v7, /device:TPU:1, one launch (start us, length us, event | category | flops | bytes accessed | tf_op | source)
XLA Modules:
  0.0 59.3 jit_solution(13696902306988311284)
XLA Ops:
  0.6 1.3 %shard_map.41 = (bf16[160,4096]{1,0:T(8,128)(2,1)S(1)}, f32[8,128]{1,0:T(8,128)S(1)}) custom-call(bf16[512,4096]{1,0:T(8,128)(2,1)} %grads.3), custom_call_target="tpu_custom_call" | custom-call | tf_op jit(solution)/shard_map/pallas_call | solution.py:265
  1.9 2.1 %collective-permute-start.2 = (bf16[160,4096]{1,0:T(8,128)(2,1)S(1)}, bf16[160,4096]{1,0:T(8,128)(2,1)S(1)}, u32[]{:S(2)}, u32[]{:S(2)}) collective-permute-start(bf16[160,4096]{1,0:T(8,128)(2,1)S(1)} %get-tuple-element.42), channel_id=1, source_target_pairs={{0,2},{2,6},{4,0},{6,4},{8,10},{10,14},{12,8},{14,12},{16,18},{18,... | collective-permute-start | bytes 3932168 | tf_op jit(solution)/shard_map/ppermute | solution.py:291
  4.0 2.2 %shard_map.42.grads = bf16[512,4096]{1,0:T(8,128)(2,1)S(1)} custom-call(bf16[512,4096]{1,0:T(8,128)(2,1)} %grads.3, f32[8,128]{1,0:T(8,128)S(1)} %get-tuple-element.37.before), custom_call_target="tpu_custom_call" | custom-call | tf_op jit(solution)/shard_map/pallas_call | solution.py:273
  6.2 2.4 %shard_map.43 = (f32[256,512]{1,0:T(8,128)S(1)}, f32[256,512]{1,0:T(8,128)S(1)}) custom-call(bf16[512,4096]{1,0:T(8,128)(2,1)S(1)} %shard_map.42.grads, f32[8,128]{1,0:T(8,128)S(1)} %get-tuple-element.37.before), custom_call_target="tpu_custom_call" | custom-call | tf_op jit(solution)/shard_map/pallas_call | solution.py:281
  10.0 2.6 %collective-permute-done.3.piece = bf16[64,4096]{1,0:T(8,128)(2,1)S(1)} collective-permute-done((bf16[64,4096]{1,0:T(8,128)(2,1)S(1)}, bf16[64,4096]{1,0:T(8,128)(2,1)S(1)}, u32[]{:S(2)}, u32[]{:S(2)}) %collective-permute-start.3) | collective-permute-done | bytes 524320 | tf_op jit(solution)/shard_map/ppermute | solution.py:306
  12.6 1.3 %shard_map.47 = (f32[96,256]{1,0:T(8,128)S(1)}, f32[96,256]{1,0:T(8,128)S(1)}) custom-call(bf16[64,4096]{1,0:T(8,128)(2,1)S(1)} %collective-permute-done.3.piece, bf16[512,4096]{1,0:T(8,128)(2,1)S(1)} %shard_map.42.grads, f32[8,128]{1,0:T(8,128)S(1)} %get-tuple-element.37.before), custom_call_target="tpu_custom_call" | custom-call | tf_op jit(solution)/shard_map/pallas_call | solution.py:297
  13.9 1.3 %collective-permute-start.4 = (f32[96,256]{1,0:T(8,128)S(1)}, f32[96,256]{1,0:T(8,128)S(1)}, u32[]{:S(2)}, u32[]{:S(2)}) collective-permute-start(f32[96,256]{1,0:T(8,128)S(1)} %get-tuple-element.45), channel_id=1, source_target_pairs={{0,1},{1,0},{2,3},{3,2},{4,5},{5,4},{6,7},{7,6},{8,9},{9,8},{10,11... | collective-permute-start | bytes 294920 | tf_op jit(solution)/shard_map/ppermute | solution.py:303
  15.5 2.8 %collective-permute-done.4.refs_1_ = f32[96,256]{1,0:T(8,128)S(1)} collective-permute-done((f32[96,256]{1,0:T(8,128)S(1)}, f32[96,256]{1,0:T(8,128)S(1)}, u32[]{:S(2)}, u32[]{:S(2)}) %collective-permute-start.4) | collective-permute-done | bytes 98336 | tf_op jit(solution)/shard_map/ppermute | solution.py:303
  18.3 1.6 %collective-permute-start.5 = (bf16[32,512]{1,0:T(8,128)(2,1)S(1)}, bf16[32,512]{1,0:T(8,128)(2,1)S(1)}, u32[]{:S(2)}, u32[]{:S(2)}) collective-permute-start(bf16[32,512]{1,0:T(8,128)(2,1)S(1)} %get-tuple-element.46), channel_id=1, source_target_pairs={{0,2},{2,0},{4,6},{6,4},{8,10},{10,8},{12,14},{14,12},{16,18},{18,... | collective-permute-start | bytes 98312 | tf_op jit(solution)/shard_map/ppermute | solution.py:313
  21.6 1.6 %shard_map.49 = (f32[240,256]{1,0:T(8,128)S(1)}, f32[240,256]{1,0:T(8,128)S(1)}) custom-call(bf16[160,4096]{1,0:T(8,128)(2,1)S(1)} %collective-permute-done.2.piece, bf16[512,4096]{1,0:T(8,128)(2,1)S(1)} %shard_map.42.grads, bf16[32,512]{1,0:T(8,128)(2,1)S(1)} %collective-permute-done.5.before.near_back), custom_call_target="tpu_custom_call" | custom-call | tf_op jit(solution)/shard_map/pallas_call | solution.py:297
  23.2 6.6 %collective-permute-done.7.piece = bf16[128,4096]{1,0:T(8,128)(2,1)S(1)} collective-permute-done((bf16[128,4096]{1,0:T(8,128)(2,1)S(1)}, bf16[128,4096]{1,0:T(8,128)(2,1)S(1)}, u32[]{:S(2)}, u32[]{:S(2)}) %collective-permute-start.7) | collective-permute-done | bytes 1048608 | tf_op jit(solution)/shard_map/ppermute | solution.py:291
  29.8 1.2 %collective-permute-start.6 = (f32[240,256]{1,0:T(8,128)S(1)}, f32[240,256]{1,0:T(8,128)S(1)}, u32[]{:S(2)}, u32[]{:S(2)}) collective-permute-start(f32[240,256]{1,0:T(8,128)S(1)} %get-tuple-element.48), channel_id=1, source_target_pairs={{0,1},{1,0},{2,3},{3,2},{4,5},{5,4},{6,7},{7,6},{8,9},{9,8},{10,11... | collective-permute-start | bytes 737288 | tf_op jit(solution)/shard_map/ppermute | solution.py:303
  31.0 1.4 %shard_map.50 = (f32[192,256]{1,0:T(8,128)S(1)}, f32[192,256]{1,0:T(8,128)S(1)}) custom-call(bf16[128,4096]{1,0:T(8,128)(2,1)S(1)} %collective-permute-done.7.piece, bf16[512,4096]{1,0:T(8,128)(2,1)S(1)} %shard_map.42.grads, f32[8,128]{1,0:T(8,128)S(1)} %get-tuple-element.37.before), custom_call_target="tpu_custom_call" | custom-call | tf_op jit(solution)/shard_map/pallas_call | solution.py:297
  32.4 5.8 %collective-permute-done.9.piece = bf16[96,4096]{1,0:T(8,128)(2,1)S(1)} collective-permute-done((bf16[96,4096]{1,0:T(8,128)(2,1)S(1)}, bf16[96,4096]{1,0:T(8,128)(2,1)S(1)}, u32[]{:S(2)}, u32[]{:S(2)}) %collective-permute-start.9) | collective-permute-done | bytes 786464 | tf_op jit(solution)/shard_map/ppermute | solution.py:291
  38.2 1.2 %collective-permute-start.8 = (f32[192,256]{1,0:T(8,128)S(1)}, f32[192,256]{1,0:T(8,128)S(1)}, u32[]{:S(2)}, u32[]{:S(2)}) collective-permute-start(f32[192,256]{1,0:T(8,128)S(1)} %get-tuple-element.51), channel_id=1, source_target_pairs={{0,1},{1,0},{2,3},{3,2},{4,5},{5,4},{6,7},{7,6},{8,9},{9,8},{10,11... | collective-permute-start | bytes 589832 | tf_op jit(solution)/shard_map/ppermute | solution.py:303
  39.5 1.3 %shard_map.51 = (f32[144,256]{1,0:T(8,128)S(1)}, f32[144,256]{1,0:T(8,128)S(1)}) custom-call(bf16[96,4096]{1,0:T(8,128)(2,1)S(1)} %collective-permute-done.9.piece, bf16[512,4096]{1,0:T(8,128)(2,1)S(1)} %shard_map.42.grads, f32[8,128]{1,0:T(8,128)S(1)} %get-tuple-element.37.before), custom_call_target="tpu_custom_call" | custom-call | tf_op jit(solution)/shard_map/pallas_call | solution.py:297
  41.2 2.7 %collective-permute-done.1.piece = bf16[64,4096]{1,0:T(8,128)(2,1)S(1)} collective-permute-done((bf16[64,4096]{1,0:T(8,128)(2,1)S(1)}, bf16[64,4096]{1,0:T(8,128)(2,1)S(1)}, u32[]{:S(2)}, u32[]{:S(2)}) %collective-permute-start.1) | collective-permute-done | bytes 524320 | tf_op jit(solution)/shard_map/ppermute | solution.py:291
  43.8 1.3 %shard_map.46 = (f32[96,256]{1,0:T(8,128)S(1)}, f32[96,256]{1,0:T(8,128)S(1)}) custom-call(bf16[64,4096]{1,0:T(8,128)(2,1)S(1)} %collective-permute-done.1.piece, bf16[512,4096]{1,0:T(8,128)(2,1)S(1)} %shard_map.42.grads, bf16[256,512]{1,0:T(8,128)(2,1)S(1)} %shard_map.44.before.self_tile), custom_call_target="tpu_custom_call" | custom-call | tf_op jit(solution)/shard_map/pallas_call | solution.py:297
  45.1 1.3 %collective-permute-start.13 = (f32[96,256]{1,0:T(8,128)S(1)}, f32[96,256]{1,0:T(8,128)S(1)}, u32[]{:S(2)}, u32[]{:S(2)}) collective-permute-start(f32[96,256]{1,0:T(8,128)S(1)} %get-tuple-element.58), channel_id=1, source_target_pairs={{0,1},{1,0},{2,3},{3,2},{4,5},{5,4},{6,7},{7,6},{8,9},{9,8},{10,11... | collective-permute-start | bytes 294920 | tf_op jit(solution)/shard_map/ppermute | solution.py:303
  46.7 3.5 %collective-permute-start.11 = (bf16[64,512]{1,0:T(8,128)(2,1)S(1)}, bf16[64,512]{1,0:T(8,128)(2,1)S(1)}, u32[]{:S(2)}, u32[]{:S(2)}) collective-permute-start(bf16[64,512]{1,0:T(8,128)(2,1)S(1)} %bitcast.2), channel_id=1, source_target_pairs={{0,2},{2,6},{4,0},{6,4},{8,10},{10,14},{12,8},{14,12},{16,18},{18,... | collective-permute-start | bytes 196616 | tf_op jit(solution)/shard_map/ppermute | solution.py:305
  50.5 1.0 %collective-permute-start.15 = (f32[64,256]{1,0:T(8,128)S(1)}, f32[64,256]{1,0:T(8,128)S(1)}, u32[]{:S(2)}, u32[]{:S(2)}) collective-permute-start(f32[64,256]{1,0:T(8,128)S(1)} %get-tuple-element.62), channel_id=1, source_target_pairs={{0,1},{1,0},{2,3},{3,2},{4,5},{5,4},{6,7},{7,6},{8,9},{9,8},{10,11... | collective-permute-start | bytes 196616 | tf_op jit(solution)/shard_map/ppermute | solution.py:342
  51.4 3.5 %collective-permute-start.16 = (f32[32,512]{1,0:T(8,128)S(1)}, f32[32,512]{1,0:T(8,128)S(1)}, u32[]{:S(2)}, u32[]{:S(2)}) collective-permute-start(f32[32,512]{1,0:T(8,128)S(1)} %get-tuple-element.63), channel_id=1, source_target_pairs={{0,5},{1,4},{2,0},{3,1},{4,6},{5,7},{6,3},{7,2},{8,13},{9,12},{10,... | collective-permute-start | bytes 196616 | tf_op jit(solution)/shard_map/ppermute | solution.py:344
  55.1 1.0 %collective-permute-done.12.back.back_early = bf16[256,512]{1,0:T(8,128)(2,1)S(1)} collective-permute-done((bf16[256,512]{1,0:T(8,128)(2,1)S(1)}, bf16[256,512]{1,0:T(8,128)(2,1)S(1)}, u32[]{:S(2)}, u32[]{:S(2)}) %collective-permute-start.12) | collective-permute-done | bytes 262176 | tf_op jit(solution)/shard_map/ppermute | solution.py:326
  57.1 1.3 %collective-permute-done.18.back_third = bf16[32,512]{1,0:T(8,128)(2,1)S(1)} collective-permute-done((bf16[32,512]{1,0:T(8,128)(2,1)S(1)}, bf16[32,512]{1,0:T(8,128)(2,1)S(1)}, u32[]{:S(2)}, u32[]{:S(2)}) %collective-permute-start.18) | collective-permute-done | bytes 32800 | tf_op jit(solution)/shard_map/ppermute | solution.py:345
  (32 shorter events, 6.3 us)
Async XLA Ops:
  1.9 19.3 %collective-permute-start.2 = (bf16[160,4096]{1,0:T(8,128)(2,1)S(1)}, bf16[160,4096]{1,0:T(8,128)(2,1)S(1)}, u32[]{:S(2)}, u32[]{:S(2)}) collective-permute-start(bf16[160,4096]{1,0:T(8,128)(2,1)S(1)} %get-tuple-element.42), channel_id=1, source_target_pairs={{0,2},{2,6},{4,0},{6,4},{8,10},{10,14},{12,8},{14,12},{16,18},{18,... | collective-permute-start | bytes 3932168 | tf_op jit(solution)/shard_map/ppermute | solution.py:291
  9.2 20.6 %collective-permute-start.7 = (bf16[128,4096]{1,0:T(8,128)(2,1)S(1)}, bf16[128,4096]{1,0:T(8,128)(2,1)S(1)}, u32[]{:S(2)}, u32[]{:S(2)}) collective-permute-start(bf16[128,4096]{1,0:T(8,128)(2,1)S(1)} %get-tuple-element.49), channel_id=1, source_target_pairs={{0,2},{2,6},{4,0},{6,4},{8,10},{10,14},{12,8},{14,12},{16,18},{18,... | collective-permute-start | bytes 3145736 | tf_op jit(solution)/shard_map/ppermute | solution.py:291
  9.9 2.7 %collective-permute-start.3 = (bf16[64,4096]{1,0:T(8,128)(2,1)S(1)}, bf16[64,4096]{1,0:T(8,128)(2,1)S(1)}, u32[]{:S(2)}, u32[]{:S(2)}) collective-permute-start(bf16[64,4096]{1,0:T(8,128)(2,1)S(1)} %get-tuple-element.43), channel_id=1, source_target_pairs={{0,2},{2,0},{4,6},{6,4},{8,10},{10,8},{12,14},{14,12},{16,18},{18,... | collective-permute-start | bytes 1572872 | tf_op jit(solution)/shard_map/ppermute | solution.py:306
  9.9 28.3 %collective-permute-start.9 = (bf16[96,4096]{1,0:T(8,128)(2,1)S(1)}, bf16[96,4096]{1,0:T(8,128)(2,1)S(1)}, u32[]{:S(2)}, u32[]{:S(2)}) collective-permute-start(bf16[96,4096]{1,0:T(8,128)(2,1)S(1)} %get-tuple-element.52), channel_id=1, source_target_pairs={{0,2},{2,6},{4,0},{6,4},{8,10},{10,14},{12,8},{14,12},{16,18},{18,... | collective-permute-start | bytes 2359304 | tf_op jit(solution)/shard_map/ppermute | solution.py:291
  13.9 4.3 %collective-permute-start.4 = (f32[96,256]{1,0:T(8,128)S(1)}, f32[96,256]{1,0:T(8,128)S(1)}, u32[]{:S(2)}, u32[]{:S(2)}) collective-permute-start(f32[96,256]{1,0:T(8,128)S(1)} %get-tuple-element.45), channel_id=1, source_target_pairs={{0,1},{1,0},{2,3},{3,2},{4,5},{5,4},{6,7},{7,6},{8,9},{9,8},{10,11... | collective-permute-start | bytes 294920 | tf_op jit(solution)/shard_map/ppermute | solution.py:303
  15.2 25.6 %collective-permute-start = (f32[256,512]{1,0:T(8,128)S(1)}, f32[256,512]{1,0:T(8,128)S(1)}, u32[]{:S(2)}, u32[]{:S(2)}) collective-permute-start(f32[256,512]{1,0:T(8,128)S(1)} %get-tuple-element.39), channel_id=1, source_target_pairs={{0,1},{1,0},{2,3},{3,2},{4,5},{5,4},{6,7},{7,6},{8,9},{9,8},{10,11... | collective-permute-start | bytes 1572872 | tf_op jit(solution)/shard_map/ppermute | solution.py:294
  18.3 2.4 %collective-permute-start.5 = (bf16[32,512]{1,0:T(8,128)(2,1)S(1)}, bf16[32,512]{1,0:T(8,128)(2,1)S(1)}, u32[]{:S(2)}, u32[]{:S(2)}) collective-permute-start(bf16[32,512]{1,0:T(8,128)(2,1)S(1)} %get-tuple-element.46), channel_id=1, source_target_pairs={{0,2},{2,0},{4,6},{6,4},{8,10},{10,8},{12,14},{14,12},{16,18},{18,... | collective-permute-start | bytes 98312 | tf_op jit(solution)/shard_map/ppermute | solution.py:313
  20.7 23.1 %collective-permute-start.1 = (bf16[64,4096]{1,0:T(8,128)(2,1)S(1)}, bf16[64,4096]{1,0:T(8,128)(2,1)S(1)}, u32[]{:S(2)}, u32[]{:S(2)}) collective-permute-start(bf16[64,4096]{1,0:T(8,128)(2,1)S(1)} %get-tuple-element.40), channel_id=1, source_target_pairs={{0,2},{2,6},{4,0},{6,4},{8,10},{10,14},{12,8},{14,12},{16,18},{18,... | collective-permute-start | bytes 1572872 | tf_op jit(solution)/shard_map/ppermute | solution.py:291
  21.3 29.1 %collective-permute-start.14 = (bf16[64,4096]{1,0:T(8,128)(2,1)S(1)}, bf16[64,4096]{1,0:T(8,128)(2,1)S(1)}, u32[]{:S(2)}, u32[]{:S(2)}) collective-permute-start(bf16[64,4096]{1,0:T(8,128)(2,1)S(1)} %get-tuple-element.43), channel_id=1, source_target_pairs={{0,2},{2,6},{4,0},{6,4},{8,10},{10,14},{12,8},{14,12},{16,18},{18,... | collective-permute-start | bytes 1572872 | tf_op jit(solution)/shard_map/ppermute | solution.py:291
  29.8 20.4 %collective-permute-start.6 = (f32[240,256]{1,0:T(8,128)S(1)}, f32[240,256]{1,0:T(8,128)S(1)}, u32[]{:S(2)}, u32[]{:S(2)}) collective-permute-start(f32[240,256]{1,0:T(8,128)S(1)} %get-tuple-element.48), channel_id=1, source_target_pairs={{0,1},{1,0},{2,3},{3,2},{4,5},{5,4},{6,7},{7,6},{8,9},{9,8},{10,11... | collective-permute-start | bytes 737288 | tf_op jit(solution)/shard_map/ppermute | solution.py:303
  38.2 12.0 %collective-permute-start.8 = (f32[192,256]{1,0:T(8,128)S(1)}, f32[192,256]{1,0:T(8,128)S(1)}, u32[]{:S(2)}, u32[]{:S(2)}) collective-permute-start(f32[192,256]{1,0:T(8,128)S(1)} %get-tuple-element.51), channel_id=1, source_target_pairs={{0,1},{1,0},{2,3},{3,2},{4,5},{5,4},{6,7},{7,6},{8,9},{9,8},{10,11... | collective-permute-start | bytes 589832 | tf_op jit(solution)/shard_map/ppermute | solution.py:303
  40.8 6.0 %copy-start = (bf16[512,64]{0,1:T(8,128)(2,1)S(1)}, bf16[512,64]{0,1:T(8,128)(2,1)}, u32[]{:S(2)}) copy-start(bf16[512,64]{0,1:T(8,128)(2,1)} %param.3) | copy-start | bytes 196612
  40.8 5.9 %collective-permute-start.10 = (f32[144,256]{1,0:T(8,128)S(1)}, f32[144,256]{1,0:T(8,128)S(1)}, u32[]{:S(2)}, u32[]{:S(2)}) collective-permute-start(f32[144,256]{1,0:T(8,128)S(1)} %get-tuple-element.54), channel_id=1, source_target_pairs={{0,1},{1,0},{2,3},{3,2},{4,5},{5,4},{6,7},{7,6},{8,9},{9,8},{10,11... | collective-permute-start | bytes 442376 | tf_op jit(solution)/shard_map/ppermute | solution.py:303
  45.1 5.3 %collective-permute-start.13 = (f32[96,256]{1,0:T(8,128)S(1)}, f32[96,256]{1,0:T(8,128)S(1)}, u32[]{:S(2)}, u32[]{:S(2)}) collective-permute-start(f32[96,256]{1,0:T(8,128)S(1)} %get-tuple-element.58), channel_id=1, source_target_pairs={{0,1},{1,0},{2,3},{3,2},{4,5},{5,4},{6,7},{7,6},{8,9},{9,8},{10,11... | collective-permute-start | bytes 294920 | tf_op jit(solution)/shard_map/ppermute | solution.py:303
  46.7 8.2 %collective-permute-start.11 = (bf16[64,512]{1,0:T(8,128)(2,1)S(1)}, bf16[64,512]{1,0:T(8,128)(2,1)S(1)}, u32[]{:S(2)}, u32[]{:S(2)}) collective-permute-start(bf16[64,512]{1,0:T(8,128)(2,1)S(1)} %bitcast.2), channel_id=1, source_target_pairs={{0,2},{2,6},{4,0},{6,4},{8,10},{10,14},{12,8},{14,12},{16,18},{18,... | collective-permute-start | bytes 196616 | tf_op jit(solution)/shard_map/ppermute | solution.py:305
  50.3 5.8 %collective-permute-start.12 = (bf16[256,512]{1,0:T(8,128)(2,1)S(1)}, bf16[256,512]{1,0:T(8,128)(2,1)S(1)}, u32[]{:S(2)}, u32[]{:S(2)}) collective-permute-start(bf16[256,512]{1,0:T(8,128)(2,1)S(1)} %get-tuple-element.56), channel_id=1, source_target_pairs={{0,4},{2,0},{4,6},{6,2},{8,12},{10,8},{12,14},{14,10},{16,20},{18,... | collective-permute-start | bytes 786440 | tf_op jit(solution)/shard_map/ppermute | solution.py:326
  50.5 7.9 %collective-permute-start.15 = (f32[64,256]{1,0:T(8,128)S(1)}, f32[64,256]{1,0:T(8,128)S(1)}, u32[]{:S(2)}, u32[]{:S(2)}) collective-permute-start(f32[64,256]{1,0:T(8,128)S(1)} %get-tuple-element.62), channel_id=1, source_target_pairs={{0,1},{1,0},{2,3},{3,2},{4,5},{5,4},{6,7},{7,6},{8,9},{9,8},{10,11... | collective-permute-start | bytes 196616 | tf_op jit(solution)/shard_map/ppermute | solution.py:342
  51.4 7.0 %collective-permute-start.16 = (f32[32,512]{1,0:T(8,128)S(1)}, f32[32,512]{1,0:T(8,128)S(1)}, u32[]{:S(2)}, u32[]{:S(2)}) collective-permute-start(f32[32,512]{1,0:T(8,128)S(1)} %get-tuple-element.63), channel_id=1, source_target_pairs={{0,5},{1,4},{2,0},{3,1},{4,6},{5,7},{6,3},{7,2},{8,13},{9,12},{10,... | collective-permute-start | bytes 196616 | tf_op jit(solution)/shard_map/ppermute | solution.py:344
  54.9 3.5 %collective-permute-start.17 = (f32[32,512]{1,0:T(8,128)S(1)}, f32[32,512]{1,0:T(8,128)S(1)}, u32[]{:S(2)}, u32[]{:S(2)}) collective-permute-start(f32[32,512]{1,0:T(8,128)S(1)} %get-tuple-element.64), channel_id=1, source_target_pairs={{0,4},{2,0},{4,6},{6,2},{8,12},{10,8},{12,14},{14,10},{16,20},{18,... | collective-permute-start | bytes 196616 | tf_op jit(solution)/shard_map/ppermute | solution.py:343
  54.9 3.5 %collective-permute-start.18 = (bf16[32,512]{1,0:T(8,128)(2,1)S(1)}, bf16[32,512]{1,0:T(8,128)(2,1)S(1)}, u32[]{:S(2)}, u32[]{:S(2)}) collective-permute-start(bf16[32,512]{1,0:T(8,128)(2,1)S(1)} %get-tuple-element.68), channel_id=1, source_target_pairs={{0,4},{2,0},{4,6},{6,2},{8,12},{10,8},{12,14},{14,10},{16,20},{18,... | collective-permute-start | bytes 98312 | tf_op jit(solution)/shard_map/ppermute | solution.py:345

commit v8 on v7

--- a/solution.py
+++ b/solution.py
@@ -9,7 +9,7 @@
 
 AFTER = {0: 1, 1: 3, 3: 2, 2: 0}
 BEFORE = {after: before for before, after in AFTER.items()}
-SIXTEENTHS = (5, 4, 3, 2, 2)
+SIXTEENTHS = (6, 4, 2, 2, 2)
 EARLY = 3
 FIRST_VMEM = 50
 FLOPS = 3000000000

time: 59.4 us -> 59.5 us (level)
  starting transfers between devices: 19.1 us -> 22.7 us
  waiting for transfers between devices: 24 us -> 20.7 us
    ppermute x5, starting transfers between devices: 3.75 us -> 6.62 us  [per_device(): got = [lax.ppermute(piece, 'blk', forward) for piece in (piece, *pieces)]]
    ppermute x5, waiting for transfers between devices: 15.1 us -> 13.5 us  [per_device(): got = [lax.ppermute(piece, 'blk', forward) for piece in (piece, *pieces)]]
    ppermute x1, starting transfers between devices: 0.23 us -> 1.25 us  [per_device(): lax.ppermute(sent, 'tgt', across)]
    ppermute x5, waiting for transfers between devices: 3.08 us -> 2.19 us  [pair(): return [kept, lax.ppermute(sent, 'tgt', across)]]
    ppermute x1, waiting for transfers between devices: 0.86 us -> 0.01 us  [per_device(): near_back = lax.ppermute(near_back, 'blk', beside)]
  transfers between devices with their start and end apart: 19 -> 19, of which waited for: 9 -> 8; matrix products, arithmetic and copies ran while one was open for 0% -> 0% of each run, Pallas kernels for 22% -> 22%
where the time goes in v8:
time: 59.5 us; the launch traced here: 59.4 us
  starting transfers between devices  22.7 us (38%)
  waiting for transfers between devices  20.7 us (35%)
  Pallas kernels  15.1 us (25%)
  between operations  0.79 us (1%)
    ppermute x5, waiting for transfers between devices, per_device(): got = [lax.ppermute(piece, 'blk', forward) for piece in (piece, *pieces)]  13.5 us
    pallas_call x5, Pallas kernels, pair(): call(functools.partial(pair_kernel, width, half), [f32(3 * width, half)]...  6.87 us
    ppermute x5, starting transfers between devices, per_device(): got = [lax.ppermute(piece, 'blk', forward) for piece in (piece, *pieces)]  6.62 us
    ppermute x5, starting transfers between devices, pair(): return [kept, lax.ppermute(sent, 'tgt', across)]  5.38 us
    ppermute x1, starting transfers between devices, per_device(): cross = lax.ppermute(cross, ('blk', 'tgt'), back_across)  3.86 us
    ppermute x1, starting transfers between devices, per_device(): flat_before = lax.ppermute(flat, 'blk', forward)  3.06 us
    ppermute x1, waiting for transfers between devices, per_device(): near_sums = pair(widths[-1], lax.ppermute(pieces[-1], 'blk', beside), mark)  2.73 us
    pallas_call x1, Pallas kernels, per_device(): call(functools.partial(self_kernel, half), [f32(half, rows)] * 2, [VMEM,...  2.35 us
  transfers between devices with their start and end apart: 19, of which 8 were waited for; matrix products, arithmetic and copies ran while one was open for 0% of the time, Pallas kernels for 22%

profile of v8, /device:TPU:1, one launch (start us, length us, event | category | flops | bytes accessed | tf_op | source)
XLA Modules:
  0.0 59.4 jit_solution(6076067151366682328)
XLA Ops:
  0.6 1.4 %shard_map.41 = (bf16[192,4096]{1,0:T(8,128)(2,1)S(1)}, f32[8,128]{1,0:T(8,128)S(1)}) custom-call(bf16[512,4096]{1,0:T(8,128)(2,1)} %grads.3), custom_call_target="tpu_custom_call" | custom-call | tf_op jit(solution)/shard_map/pallas_call | solution.py:265
  2.0 2.1 %collective-permute-start.2 = (bf16[192,4096]{1,0:T(8,128)(2,1)S(1)}, bf16[192,4096]{1,0:T(8,128)(2,1)S(1)}, u32[]{:S(2)}, u32[]{:S(2)}) collective-permute-start(bf16[192,4096]{1,0:T(8,128)(2,1)S(1)} %get-tuple-element.42), channel_id=1, source_target_pairs={{0,2},{2,6},{4,0},{6,4},{8,10},{10,14},{12,8},{14,12},{16,18},{18,... | collective-permute-start | bytes 4718600 | tf_op jit(solution)/shard_map/ppermute | solution.py:291
  4.1 2.2 %shard_map.42.grads = bf16[512,4096]{1,0:T(8,128)(2,1)S(1)} custom-call(bf16[512,4096]{1,0:T(8,128)(2,1)} %grads.3, f32[8,128]{1,0:T(8,128)S(1)} %get-tuple-element.37.before), custom_call_target="tpu_custom_call" | custom-call | tf_op jit(solution)/shard_map/pallas_call | solution.py:273
  6.3 2.4 %shard_map.43 = (f32[256,512]{1,0:T(8,128)S(1)}, f32[256,512]{1,0:T(8,128)S(1)}) custom-call(bf16[512,4096]{1,0:T(8,128)(2,1)S(1)} %shard_map.42.grads, f32[8,128]{1,0:T(8,128)S(1)} %get-tuple-element.37.before), custom_call_target="tpu_custom_call" | custom-call | tf_op jit(solution)/shard_map/pallas_call | solution.py:281
  9.6 2.7 %collective-permute-done.3.piece = bf16[64,4096]{1,0:T(8,128)(2,1)S(1)} collective-permute-done((bf16[64,4096]{1,0:T(8,128)(2,1)S(1)}, bf16[64,4096]{1,0:T(8,128)(2,1)S(1)}, u32[]{:S(2)}, u32[]{:S(2)}) %collective-permute-start.3) | collective-permute-done | bytes 524320 | tf_op jit(solution)/shard_map/ppermute | solution.py:306
  12.4 1.3 %shard_map.47 = (f32[96,256]{1,0:T(8,128)S(1)}, f32[96,256]{1,0:T(8,128)S(1)}) custom-call(bf16[64,4096]{1,0:T(8,128)(2,1)S(1)} %collective-permute-done.3.piece, bf16[512,4096]{1,0:T(8,128)(2,1)S(1)} %shard_map.42.grads, f32[8,128]{1,0:T(8,128)S(1)} %get-tuple-element.37.before), custom_call_target="tpu_custom_call" | custom-call | tf_op jit(solution)/shard_map/pallas_call | solution.py:297
  13.7 1.3 %collective-permute-start.4 = (f32[96,256]{1,0:T(8,128)S(1)}, f32[96,256]{1,0:T(8,128)S(1)}, u32[]{:S(2)}, u32[]{:S(2)}) collective-permute-start(f32[96,256]{1,0:T(8,128)S(1)} %get-tuple-element.45), channel_id=1, source_target_pairs={{0,1},{1,0},{2,3},{3,2},{4,5},{5,4},{6,7},{7,6},{8,9},{9,8},{10,11... | collective-permute-start | bytes 294920 | tf_op jit(solution)/shard_map/ppermute | solution.py:303
  15.8 2.2 %collective-permute-done.4.refs_1_ = f32[96,256]{1,0:T(8,128)S(1)} collective-permute-done((f32[96,256]{1,0:T(8,128)S(1)}, f32[96,256]{1,0:T(8,128)S(1)}, u32[]{:S(2)}, u32[]{:S(2)}) %collective-permute-start.4) | collective-permute-done | bytes 98336 | tf_op jit(solution)/shard_map/ppermute | solution.py:303
  19.0 1.3 %collective-permute-start = (f32[256,512]{1,0:T(8,128)S(1)}, f32[256,512]{1,0:T(8,128)S(1)}, u32[]{:S(2)}, u32[]{:S(2)}) collective-permute-start(f32[256,512]{1,0:T(8,128)S(1)} %get-tuple-element.39), channel_id=1, source_target_pairs={{0,1},{1,0},{2,3},{3,2},{4,5},{5,4},{6,7},{7,6},{8,9},{9,8},{10,11... | collective-permute-start | bytes 1572872 | tf_op jit(solution)/shard_map/ppermute | solution.py:294
  21.4 2.2 %collective-permute-start.14 = (bf16[64,4096]{1,0:T(8,128)(2,1)S(1)}, bf16[64,4096]{1,0:T(8,128)(2,1)S(1)}, u32[]{:S(2)}, u32[]{:S(2)}) collective-permute-start(bf16[64,4096]{1,0:T(8,128)(2,1)S(1)} %get-tuple-element.43), channel_id=1, source_target_pairs={{0,2},{2,6},{4,0},{6,4},{8,10},{10,14},{12,8},{14,12},{16,18},{18,... | collective-permute-start | bytes 1572872 | tf_op jit(solution)/shard_map/ppermute | solution.py:291
  23.6 1.6 %shard_map.49 = (f32[288,256]{1,0:T(8,128)S(1)}, f32[288,256]{1,0:T(8,128)S(1)}) custom-call(bf16[192,4096]{1,0:T(8,128)(2,1)S(1)} %collective-permute-done.2.piece, bf16[512,4096]{1,0:T(8,128)(2,1)S(1)} %shard_map.42.grads, bf16[32,512]{1,0:T(8,128)(2,1)S(1)} %collective-permute-done.5.before.near_back), custom_call_target="tpu_custom_call" | custom-call | tf_op jit(solution)/shard_map/pallas_call | solution.py:297
  25.2 7.5 %collective-permute-done.7.piece = bf16[128,4096]{1,0:T(8,128)(2,1)S(1)} collective-permute-done((bf16[128,4096]{1,0:T(8,128)(2,1)S(1)}, bf16[128,4096]{1,0:T(8,128)(2,1)S(1)}, u32[]{:S(2)}, u32[]{:S(2)}) %collective-permute-start.7) | collective-permute-done | bytes 1048608 | tf_op jit(solution)/shard_map/ppermute | solution.py:291
  32.7 1.2 %collective-permute-start.6 = (f32[288,256]{1,0:T(8,128)S(1)}, f32[288,256]{1,0:T(8,128)S(1)}, u32[]{:S(2)}, u32[]{:S(2)}) collective-permute-start(f32[288,256]{1,0:T(8,128)S(1)} %get-tuple-element.48), channel_id=1, source_target_pairs={{0,1},{1,0},{2,3},{3,2},{4,5},{5,4},{6,7},{7,6},{8,9},{9,8},{10,11... | collective-permute-start | bytes 884744 | tf_op jit(solution)/shard_map/ppermute | solution.py:303
  33.9 1.4 %shard_map.50 = (f32[192,256]{1,0:T(8,128)S(1)}, f32[192,256]{1,0:T(8,128)S(1)}) custom-call(bf16[128,4096]{1,0:T(8,128)(2,1)S(1)} %collective-permute-done.7.piece, bf16[512,4096]{1,0:T(8,128)(2,1)S(1)} %shard_map.42.grads, f32[8,128]{1,0:T(8,128)S(1)} %get-tuple-element.37.before), custom_call_target="tpu_custom_call" | custom-call | tf_op jit(solution)/shard_map/pallas_call | solution.py:297
  35.3 3.0 %collective-permute-done.9.piece = bf16[64,4096]{1,0:T(8,128)(2,1)S(1)} collective-permute-done((bf16[64,4096]{1,0:T(8,128)(2,1)S(1)}, bf16[64,4096]{1,0:T(8,128)(2,1)S(1)}, u32[]{:S(2)}, u32[]{:S(2)}) %collective-permute-start.9) | collective-permute-done | bytes 524320 | tf_op jit(solution)/shard_map/ppermute | solution.py:291
  38.3 1.2 %collective-permute-start.8 = (f32[192,256]{1,0:T(8,128)S(1)}, f32[192,256]{1,0:T(8,128)S(1)}, u32[]{:S(2)}, u32[]{:S(2)}) collective-permute-start(f32[192,256]{1,0:T(8,128)S(1)} %get-tuple-element.51), channel_id=1, source_target_pairs={{0,1},{1,0},{2,3},{3,2},{4,5},{5,4},{6,7},{7,6},{8,9},{9,8},{10,11... | collective-permute-start | bytes 589832 | tf_op jit(solution)/shard_map/ppermute | solution.py:303
  39.5 1.3 %shard_map.51 = (f32[96,256]{1,0:T(8,128)S(1)}, f32[96,256]{1,0:T(8,128)S(1)}) custom-call(bf16[64,4096]{1,0:T(8,128)(2,1)S(1)} %collective-permute-done.9.piece, bf16[512,4096]{1,0:T(8,128)(2,1)S(1)} %shard_map.42.grads, f32[8,128]{1,0:T(8,128)S(1)} %get-tuple-element.37.before), custom_call_target="tpu_custom_call" | custom-call | tf_op jit(solution)/shard_map/pallas_call | solution.py:297
  41.2 2.7 %collective-permute-done.1.piece = bf16[64,4096]{1,0:T(8,128)(2,1)S(1)} collective-permute-done((bf16[64,4096]{1,0:T(8,128)(2,1)S(1)}, bf16[64,4096]{1,0:T(8,128)(2,1)S(1)}, u32[]{:S(2)}, u32[]{:S(2)}) %collective-permute-start.1) | collective-permute-done | bytes 524320 | tf_op jit(solution)/shard_map/ppermute | solution.py:291
  43.9 1.3 %shard_map.46 = (f32[96,256]{1,0:T(8,128)S(1)}, f32[96,256]{1,0:T(8,128)S(1)}) custom-call(bf16[64,4096]{1,0:T(8,128)(2,1)S(1)} %collective-permute-done.1.piece, bf16[512,4096]{1,0:T(8,128)(2,1)S(1)} %shard_map.42.grads, bf16[256,512]{1,0:T(8,128)(2,1)S(1)} %shard_map.44.before.self_tile), custom_call_target="tpu_custom_call" | custom-call | tf_op jit(solution)/shard_map/pallas_call | solution.py:297
  45.2 1.3 %collective-permute-start.13 = (f32[96,256]{1,0:T(8,128)S(1)}, f32[96,256]{1,0:T(8,128)S(1)}, u32[]{:S(2)}, u32[]{:S(2)}) collective-permute-start(f32[96,256]{1,0:T(8,128)S(1)} %get-tuple-element.58), channel_id=1, source_target_pairs={{0,1},{1,0},{2,3},{3,2},{4,5},{5,4},{6,7},{7,6},{8,9},{9,8},{10,11... | collective-permute-start | bytes 294920 | tf_op jit(solution)/shard_map/ppermute | solution.py:303
  46.5 3.1 %collective-permute-start.11 = (bf16[64,512]{1,0:T(8,128)(2,1)S(1)}, bf16[64,512]{1,0:T(8,128)(2,1)S(1)}, u32[]{:S(2)}, u32[]{:S(2)}) collective-permute-start(bf16[64,512]{1,0:T(8,128)(2,1)S(1)} %bitcast.2), channel_id=1, source_target_pairs={{0,2},{2,6},{4,0},{6,4},{8,10},{10,14},{12,8},{14,12},{16,18},{18,... | collective-permute-start | bytes 196616 | tf_op jit(solution)/shard_map/ppermute | solution.py:305
  49.8 1.3 %collective-permute-start.15 = (f32[64,256]{1,0:T(8,128)S(1)}, f32[64,256]{1,0:T(8,128)S(1)}, u32[]{:S(2)}, u32[]{:S(2)}) collective-permute-start(f32[64,256]{1,0:T(8,128)S(1)} %get-tuple-element.62), channel_id=1, source_target_pairs={{0,1},{1,0},{2,3},{3,2},{4,5},{5,4},{6,7},{7,6},{8,9},{9,8},{10,11... | collective-permute-start | bytes 196616 | tf_op jit(solution)/shard_map/ppermute | solution.py:342
  51.1 3.9 %collective-permute-start.16 = (f32[32,512]{1,0:T(8,128)S(1)}, f32[32,512]{1,0:T(8,128)S(1)}, u32[]{:S(2)}, u32[]{:S(2)}) collective-permute-start(f32[32,512]{1,0:T(8,128)S(1)} %get-tuple-element.63), channel_id=1, source_target_pairs={{0,5},{1,4},{2,0},{3,1},{4,6},{5,7},{6,3},{7,2},{8,13},{9,12},{10,... | collective-permute-start | bytes 196616 | tf_op jit(solution)/shard_map/ppermute | solution.py:344
  56.6 1.9 %collective-permute-done.18.back_third = bf16[32,512]{1,0:T(8,128)(2,1)S(1)} collective-permute-done((bf16[32,512]{1,0:T(8,128)(2,1)S(1)}, bf16[32,512]{1,0:T(8,128)(2,1)S(1)}, u32[]{:S(2)}, u32[]{:S(2)}) %collective-permute-start.18) | collective-permute-done | bytes 32800 | tf_op jit(solution)/shard_map/ppermute | solution.py:345
  (32 shorter events, 7.0 us)
Async XLA Ops:
  2.0 19.4 %collective-permute-start.2 = (bf16[192,4096]{1,0:T(8,128)(2,1)S(1)}, bf16[192,4096]{1,0:T(8,128)(2,1)S(1)}, u32[]{:S(2)}, u32[]{:S(2)}) collective-permute-start(bf16[192,4096]{1,0:T(8,128)(2,1)S(1)} %get-tuple-element.42), channel_id=1, source_target_pairs={{0,2},{2,6},{4,0},{6,4},{8,10},{10,14},{12,8},{14,12},{16,18},{18,... | collective-permute-start | bytes 4718600 | tf_op jit(solution)/shard_map/ppermute | solution.py:291
  8.9 23.7 %collective-permute-start.7 = (bf16[128,4096]{1,0:T(8,128)(2,1)S(1)}, bf16[128,4096]{1,0:T(8,128)(2,1)S(1)}, u32[]{:S(2)}, u32[]{:S(2)}) collective-permute-start(bf16[128,4096]{1,0:T(8,128)(2,1)S(1)} %get-tuple-element.49), channel_id=1, source_target_pairs={{0,2},{2,6},{4,0},{6,4},{8,10},{10,14},{12,8},{14,12},{16,18},{18,... | collective-permute-start | bytes 3145736 | tf_op jit(solution)/shard_map/ppermute | solution.py:291
  9.6 2.7 %collective-permute-start.3 = (bf16[64,4096]{1,0:T(8,128)(2,1)S(1)}, bf16[64,4096]{1,0:T(8,128)(2,1)S(1)}, u32[]{:S(2)}, u32[]{:S(2)}) collective-permute-start(bf16[64,4096]{1,0:T(8,128)(2,1)S(1)} %get-tuple-element.43), channel_id=1, source_target_pairs={{0,2},{2,0},{4,6},{6,4},{8,10},{10,8},{12,14},{14,12},{16,18},{18,... | collective-permute-start | bytes 1572872 | tf_op jit(solution)/shard_map/ppermute | solution.py:306
  13.7 4.3 %collective-permute-start.4 = (f32[96,256]{1,0:T(8,128)S(1)}, f32[96,256]{1,0:T(8,128)S(1)}, u32[]{:S(2)}, u32[]{:S(2)}) collective-permute-start(f32[96,256]{1,0:T(8,128)S(1)} %get-tuple-element.45), channel_id=1, source_target_pairs={{0,1},{1,0},{2,3},{3,2},{4,5},{5,4},{6,7},{7,6},{8,9},{9,8},{10,11... | collective-permute-start | bytes 294920 | tf_op jit(solution)/shard_map/ppermute | solution.py:303
  15.0 23.3 %collective-permute-start.9 = (bf16[64,4096]{1,0:T(8,128)(2,1)S(1)}, bf16[64,4096]{1,0:T(8,128)(2,1)S(1)}, u32[]{:S(2)}, u32[]{:S(2)}) collective-permute-start(bf16[64,4096]{1,0:T(8,128)(2,1)S(1)} %get-tuple-element.52), channel_id=1, source_target_pairs={{0,2},{2,6},{4,0},{6,4},{8,10},{10,14},{12,8},{14,12},{16,18},{18,... | collective-permute-start | bytes 1572872 | tf_op jit(solution)/shard_map/ppermute | solution.py:291
  18.0 2.3 %collective-permute-start.5 = (bf16[32,512]{1,0:T(8,128)(2,1)S(1)}, bf16[32,512]{1,0:T(8,128)(2,1)S(1)}, u32[]{:S(2)}, u32[]{:S(2)}) collective-permute-start(bf16[32,512]{1,0:T(8,128)(2,1)S(1)} %get-tuple-element.46), channel_id=1, source_target_pairs={{0,2},{2,0},{4,6},{6,4},{8,10},{10,8},{12,14},{14,12},{16,18},{18,... | collective-permute-start | bytes 98312 | tf_op jit(solution)/shard_map/ppermute | solution.py:313
  19.0 21.8 %collective-permute-start = (f32[256,512]{1,0:T(8,128)S(1)}, f32[256,512]{1,0:T(8,128)S(1)}, u32[]{:S(2)}, u32[]{:S(2)}) collective-permute-start(f32[256,512]{1,0:T(8,128)S(1)} %get-tuple-element.39), channel_id=1, source_target_pairs={{0,1},{1,0},{2,3},{3,2},{4,5},{5,4},{6,7},{7,6},{8,9},{9,8},{10,11... | collective-permute-start | bytes 1572872 | tf_op jit(solution)/shard_map/ppermute | solution.py:294
  20.3 23.6 %collective-permute-start.1 = (bf16[64,4096]{1,0:T(8,128)(2,1)S(1)}, bf16[64,4096]{1,0:T(8,128)(2,1)S(1)}, u32[]{:S(2)}, u32[]{:S(2)}) collective-permute-start(bf16[64,4096]{1,0:T(8,128)(2,1)S(1)} %get-tuple-element.40), channel_id=1, source_target_pairs={{0,2},{2,6},{4,0},{6,4},{8,10},{10,14},{12,8},{14,12},{16,18},{18,... | collective-permute-start | bytes 1572872 | tf_op jit(solution)/shard_map/ppermute | solution.py:291
  21.4 28.3 %collective-permute-start.14 = (bf16[64,4096]{1,0:T(8,128)(2,1)S(1)}, bf16[64,4096]{1,0:T(8,128)(2,1)S(1)}, u32[]{:S(2)}, u32[]{:S(2)}) collective-permute-start(bf16[64,4096]{1,0:T(8,128)(2,1)S(1)} %get-tuple-element.43), channel_id=1, source_target_pairs={{0,2},{2,6},{4,0},{6,4},{8,10},{10,14},{12,8},{14,12},{16,18},{18,... | collective-permute-start | bytes 1572872 | tf_op jit(solution)/shard_map/ppermute | solution.py:291
  32.7 16.9 %collective-permute-start.6 = (f32[288,256]{1,0:T(8,128)S(1)}, f32[288,256]{1,0:T(8,128)S(1)}, u32[]{:S(2)}, u32[]{:S(2)}) collective-permute-start(f32[288,256]{1,0:T(8,128)S(1)} %get-tuple-element.48), channel_id=1, source_target_pairs={{0,1},{1,0},{2,3},{3,2},{4,5},{5,4},{6,7},{7,6},{8,9},{9,8},{10,11... | collective-permute-start | bytes 884744 | tf_op jit(solution)/shard_map/ppermute | solution.py:303
  38.3 11.3 %collective-permute-start.8 = (f32[192,256]{1,0:T(8,128)S(1)}, f32[192,256]{1,0:T(8,128)S(1)}, u32[]{:S(2)}, u32[]{:S(2)}) collective-permute-start(f32[192,256]{1,0:T(8,128)S(1)} %get-tuple-element.51), channel_id=1, source_target_pairs={{0,1},{1,0},{2,3},{3,2},{4,5},{5,4},{6,7},{7,6},{8,9},{9,8},{10,11... | collective-permute-start | bytes 589832 | tf_op jit(solution)/shard_map/ppermute | solution.py:303
  40.9 5.7 %copy-start = (bf16[512,64]{0,1:T(8,128)(2,1)S(1)}, bf16[512,64]{0,1:T(8,128)(2,1)}, u32[]{:S(2)}) copy-start(bf16[512,64]{0,1:T(8,128)(2,1)} %param.3) | copy-start | bytes 196612
  40.9 5.7 %collective-permute-start.10 = (f32[96,256]{1,0:T(8,128)S(1)}, f32[96,256]{1,0:T(8,128)S(1)}, u32[]{:S(2)}, u32[]{:S(2)}) collective-permute-start(f32[96,256]{1,0:T(8,128)S(1)} %get-tuple-element.54), channel_id=1, source_target_pairs={{0,1},{1,0},{2,3},{3,2},{4,5},{5,4},{6,7},{7,6},{8,9},{9,8},{10,11... | collective-permute-start | bytes 294920 | tf_op jit(solution)/shard_map/ppermute | solution.py:303
  45.2 4.6 %collective-permute-start.13 = (f32[96,256]{1,0:T(8,128)S(1)}, f32[96,256]{1,0:T(8,128)S(1)}, u32[]{:S(2)}, u32[]{:S(2)}) collective-permute-start(f32[96,256]{1,0:T(8,128)S(1)} %get-tuple-element.58), channel_id=1, source_target_pairs={{0,1},{1,0},{2,3},{3,2},{4,5},{5,4},{6,7},{7,6},{8,9},{9,8},{10,11... | collective-permute-start | bytes 294920 | tf_op jit(solution)/shard_map/ppermute | solution.py:303
  46.5 8.5 %collective-permute-start.11 = (bf16[64,512]{1,0:T(8,128)(2,1)S(1)}, bf16[64,512]{1,0:T(8,128)(2,1)S(1)}, u32[]{:S(2)}, u32[]{:S(2)}) collective-permute-start(bf16[64,512]{1,0:T(8,128)(2,1)S(1)} %bitcast.2), channel_id=1, source_target_pairs={{0,2},{2,6},{4,0},{6,4},{8,10},{10,14},{12,8},{14,12},{16,18},{18,... | collective-permute-start | bytes 196616 | tf_op jit(solution)/shard_map/ppermute | solution.py:305
  49.7 5.9 %collective-permute-start.12 = (bf16[256,512]{1,0:T(8,128)(2,1)S(1)}, bf16[256,512]{1,0:T(8,128)(2,1)S(1)}, u32[]{:S(2)}, u32[]{:S(2)}) collective-permute-start(bf16[256,512]{1,0:T(8,128)(2,1)S(1)} %get-tuple-element.56), channel_id=1, source_target_pairs={{0,4},{2,0},{4,6},{6,2},{8,12},{10,8},{12,14},{14,10},{16,20},{18,... | collective-permute-start | bytes 786440 | tf_op jit(solution)/shard_map/ppermute | solution.py:326
  49.8 8.6 %collective-permute-start.15 = (f32[64,256]{1,0:T(8,128)S(1)}, f32[64,256]{1,0:T(8,128)S(1)}, u32[]{:S(2)}, u32[]{:S(2)}) collective-permute-start(f32[64,256]{1,0:T(8,128)S(1)} %get-tuple-element.62), channel_id=1, source_target_pairs={{0,1},{1,0},{2,3},{3,2},{4,5},{5,4},{6,7},{7,6},{8,9},{9,8},{10,11... | collective-permute-start | bytes 196616 | tf_op jit(solution)/shard_map/ppermute | solution.py:342
  51.1 7.3 %collective-permute-start.16 = (f32[32,512]{1,0:T(8,128)S(1)}, f32[32,512]{1,0:T(8,128)S(1)}, u32[]{:S(2)}, u32[]{:S(2)}) collective-permute-start(f32[32,512]{1,0:T(8,128)S(1)} %get-tuple-element.63), channel_id=1, source_target_pairs={{0,5},{1,4},{2,0},{3,1},{4,6},{5,7},{6,3},{7,2},{8,13},{9,12},{10,... | collective-permute-start | bytes 196616 | tf_op jit(solution)/shard_map/ppermute | solution.py:344
  55.0 3.5 %collective-permute-start.17 = (f32[32,512]{1,0:T(8,128)S(1)}, f32[32,512]{1,0:T(8,128)S(1)}, u32[]{:S(2)}, u32[]{:S(2)}) collective-permute-start(f32[32,512]{1,0:T(8,128)S(1)} %get-tuple-element.64), channel_id=1, source_target_pairs={{0,4},{2,0},{4,6},{6,2},{8,12},{10,8},{12,14},{14,10},{16,20},{18,... | collective-permute-start | bytes 196616 | tf_op jit(solution)/shard_map/ppermute | solution.py:343
  55.0 3.5 %collective-permute-start.18 = (bf16[32,512]{1,0:T(8,128)(2,1)S(1)}, bf16[32,512]{1,0:T(8,128)(2,1)S(1)}, u32[]{:S(2)}, u32[]{:S(2)}) collective-permute-start(bf16[32,512]{1,0:T(8,128)(2,1)S(1)} %get-tuple-element.68), channel_id=1, source_target_pairs={{0,4},{2,0},{4,6},{6,2},{8,12},{10,8},{12,14},{14,10},{16,20},{18,... | collective-permute-start | bytes 98312 | tf_op jit(solution)/shard_map/ppermute | solution.py:345
